TPU v7x, 32 devices: a whole 2x2x4 slice. The times are simulated.
32 devices in a mesh: groups: 2 (over y), blk: 8 (over z, x), uly: 2 (over core).
Axes of the slice: x: 2, y: 2, z: 4, core: 2. Of those that a mesh axis runs over, the one named last changes fastest.
Arguments:
- query: bfloat16 [4096, 1536], P(('groups', 'blk', 'uly')), parts along dimension 0, may hold values from -12 to 12
- key: bfloat16 [4096, 1536], P(('groups', 'blk', 'uly')), parts along dimension 0, may hold values from -6 to 6
- value: bfloat16 [4096, 1536], P(('groups', 'blk', 'uly')), parts along dimension 0, may hold values from -6 to 6
- keep: int32 [64, 28], P(('groups', 'blk')), parts along dimension 0, may hold values from 0 to 1, as said below
Outputs:
- attended: bfloat16 [4096, 1536], P(('groups', 'blk', 'uly')), parts along dimension 0
There are 2 independent parts, one for each index of `groups`. A program takes and returns all parts, laid end to end along the dimension named above; each array names one. Nothing has to cross between parts.
Inputs may be any that keep to these rules, and one draw needn't show every extreme that they name: Tile i has coordinates (i // 8, (i // 2) % 4, i % 2) in the clip's grid of tiles. keep[i, j] refers to key tile (i // 4 - 3) * 4 + j; it is 0 where that tile lies outside the clip, 1 where it is tile i itself, and otherwise 1 exactly when each coordinate differs from tile i's by no more than a per-tile reach of 0 or 1 in that coordinate.
All inputs are finite; a program needn't handle non-finite values.
Results may differ from a plain program's by a relative error of at most 0.0029.
Values may be sent and summed in bfloat16 or wider, within the bound.
No kernel may reach another device: no remote copies, remote signals or barrier semaphores. Data moves between devices by JAX's collectives and lax.ppermute only.
A program may use at most 64 MiB of HBM per device.

v0:
```python
import math

import jax
import jax.numpy as jnp
from jax import lax
from jax.sharding import PartitionSpec as P

HD = 128
TILE = 64


neg_fill = -1e30


def from_behind(block, axis, distance):
    devices = range(lax.axis_size(axis))
    route = [(i - distance, i) for i in devices if i - distance in devices]
    return lax.ppermute(block, axis, route)


def band_mask(flags, key_tiles, first_tile):
    width = flags.shape[1]
    column = key_tiles - first_tile
    onehot = (column[None, :] == jnp.arange(width, dtype=jnp.int32)[:, None]).astype(jnp.float32)
    return jnp.dot(flags, onehot, precision=lax.Precision.HIGHEST) > 0.5


def attend(carry, keys, values, key_tiles, queries, flags, first_tile):
    count = keys.shape[0]
    local_heads = queries.shape[1]
    tile_mask = band_mask(flags, key_tiles, first_tile)
    mask = jnp.repeat(tile_mask, TILE, axis=0)[:, None, :]
    scale = 1.0 / math.sqrt(HD)
    peak, total, accum = carry
    keys_h = keys.reshape(count, local_heads, HD)
    values_h = values.reshape(count, local_heads, HD)
    scores = jnp.einsum("qhd,khd->qhk", queries, keys_h, preferred_element_type=jnp.float32) * scale
    masked = jnp.where(mask, scores, neg_fill)
    new_peak = jnp.maximum(peak, jnp.max(masked, axis=2))
    weights = jnp.where(mask, jnp.exp(masked - new_peak[:, :, None]), 0.0)
    factor = jnp.exp(peak - new_peak)
    total = total * factor + jnp.sum(weights, axis=2)
    accum = accum * factor[:, :, None] + jnp.einsum(
        "qhk,khd->qhd", weights.astype(jnp.bfloat16), values_h, preferred_element_type=jnp.float32
    )
    return (new_peak, total, accum)


def body(query, key, value, keep):
    q_loc, k_loc, v_loc = (
        lax.all_to_all(query, "uly", split_axis=1, concat_axis=0, tiled=True),
        lax.all_to_all(key, "uly", split_axis=1, concat_axis=0, tiled=True),
        lax.all_to_all(value, "uly", split_axis=1, concat_axis=0, tiled=True),
    )
    rows = q_loc.shape[0]
    local_heads = q_loc.shape[1] // HD
    tiles_here = rows // TILE
    width = keep.shape[1]
    radius = (width // tiles_here - 1) // 2
    position = lax.axis_index("blk")
    first_tile = (position - radius) * tiles_here
    flags = keep.astype(jnp.float32)
    queries = q_loc.reshape(rows, local_heads, HD)
    initial = (
        jnp.full((rows, local_heads), neg_fill, jnp.float32),
        jnp.zeros((rows, local_heads), jnp.float32),
        jnp.zeros((rows, local_heads, HD), jnp.float32),
    )

    def tiles_of(block):
        return (block * rows + jnp.arange(rows, dtype=jnp.int32)) // TILE

    def step(carry, keys, values, key_tiles):
        return attend(carry, keys, values, key_tiles, queries, flags, first_tile)

    own_pair = jnp.stack((k_loc, v_loc))
    carry = step(initial, k_loc, v_loc, tiles_of(position))
    for distance in range(1, radius + 1):
        moved = [from_behind(own_pair, "blk", sign * distance) for sign in (1, -1)]
        step_carry = carry
        lower = moved[0]
        upper = moved[1]
        step_carry = step(step_carry, lower[0], lower[1], tiles_of(position - distance))
        carry = step(step_carry, upper[0], upper[1], tiles_of(position + distance))
    peak, total, accum = carry
    output = (accum / total[:, :, None]).astype(jnp.bfloat16).reshape(rows, local_heads * HD)
    return lax.all_to_all(output, "uly", split_axis=0, concat_axis=1, tiled=True)


def solution(mesh):
    return jax.shard_map(
        body,
        mesh=mesh,
        in_specs=(
            P(("groups", "blk", "uly"), None),
            P(("groups", "blk", "uly"), None),
            P(("groups", "blk", "uly"), None),
            P(("groups", "blk"), None),
        ),
        out_specs=P(("groups", "blk", "uly"), None),
        check_vma=False,
    )
```

profile of v0, /device:TPU:9, one launch (start us, length us, event | category | flops | bytes accessed | tf_op | source)
XLA Modules:
  0.0 110.6 jit_solution(11380944460250216101)
XLA Ops:
  0.0 2.0 %copy.108 = bf16[128,1536]{0,1:T(8,128)(2,1)} copy(bf16[128,1536]{1,0:T(8,128)(2,1)} %param.5) | data formatting | bytes 786432 | tf_op args[1]
  2.0 4.1 %all-to-all-start = ((bf16[128,2,768]{0,2,1:T(8,128)(2,1)}), bf16[128,2,768]{0,2,1:T(8,128)(2,1)S(1)}, u32[]{:S(2)}, u32[]{:S(2)}) async-start(bf16[128,2,768]{0,2,1:T(8,128)(2,1)} %bitcast.2), calls=%async_computation | async-start | bytes 786432 | tf_op jit(solution)/shard_map/all_to_all | solution.py:52
  6.1 0.9 copy.114
  7.0 0.4 all-to-all-done
  7.4 3.8 %all-to-all-start.2 = ((bf16[128,2,768]{0,2,1:T(8,128)(2,1)}), bf16[128,2,768]{0,2,1:T(8,128)(2,1)S(1)}, u32[]{:S(2)}, u32[]{:S(2)}) async-start(bf16[128,2,768]{0,2,1:T(8,128)(2,1)} %bitcast.7), calls=%async_computation.2 | async-start | bytes 786432 | tf_op jit(solution)/shard_map/all_to_all | solution.py:53
  11.2 0.4 copy.109
  11.9 0.8 constant_dynamic-update-slice_fusion.1
  12.7 0.4 copy.115
  13.3 0.8 constant_dynamic-update-slice_fusion
  14.1 1.3 %collective-permute-start.5 = (bf16[2,256,768]{1,2,0:T(8,128)(2,1)}, bf16[2,256,768]{1,2,0:T(8,128)(2,1)S(1)}, u32[]{:S(2)}, u32[]{:S(2)}) collective-permute-start(bf16[2,256,768]{1,2,0:T(8,128)(2,1)} %constant_dynamic-update-slice_fusion), channel_id=1, source_target_pairs={{6,0},{8,2},{10,4},{12,6},{14,8},{7,1},{9,3},{11,5},{13,7},{15,9},... | collective-permute-start | bytes 2359304 | tf_op jit(solution)/shard_map/ppermute | solution.py:18
  15.4 5.8 %collective-permute-start.4 = (bf16[2,256,768]{1,2,0:T(8,128)(2,1)}, bf16[2,256,768]{1,2,0:T(8,128)(2,1)}, u32[]{:S(2)}, u32[]{:S(2)}) collective-permute-start(bf16[2,256,768]{1,2,0:T(8,128)(2,1)} %constant_dynamic-update-slice_fusion), channel_id=1, source_target_pairs={{0,6},{2,8},{4,10},{6,12},{8,14},{1,7},{3,9},{5,11},{7,13},{9,15},... | collective-permute-start | bytes 2359304 | tf_op jit(solution)/shard_map/ppermute | solution.py:18
  21.3 1.9 %collective-permute-start.3 = (bf16[2,256,768]{1,2,0:T(8,128)(2,1)}, bf16[2,256,768]{1,2,0:T(8,128)(2,1)}, u32[]{:S(2)}, u32[]{:S(2)}) collective-permute-start(bf16[2,256,768]{1,2,0:T(8,128)(2,1)} %constant_dynamic-update-slice_fusion), channel_id=1, source_target_pairs={{4,0},{6,2},{8,4},{10,6},{12,8},{14,10},{5,1},{7,3},{9,5},{11,7},{... | collective-permute-start | bytes 2359304 | tf_op jit(solution)/shard_map/ppermute | solution.py:18
  23.2 3.4 %collective-permute-start.2 = (bf16[2,256,768]{1,2,0:T(8,128)(2,1)}, bf16[2,256,768]{1,2,0:T(8,128)(2,1)}, u32[]{:S(2)}, u32[]{:S(2)}) collective-permute-start(bf16[2,256,768]{1,2,0:T(8,128)(2,1)} %constant_dynamic-update-slice_fusion), channel_id=1, source_target_pairs={{0,4},{2,6},{4,8},{6,10},{8,12},{10,14},{1,5},{3,7},{5,9},{7,11},{... | collective-permute-start | bytes 2359304 | tf_op jit(solution)/shard_map/ppermute | solution.py:18
  26.6 3.1 %collective-permute-start = (bf16[2,256,768]{1,2,0:T(8,128)(2,1)}, bf16[2,256,768]{1,2,0:T(8,128)(2,1)}, u32[]{:S(2)}, u32[]{:S(2)}) collective-permute-start(bf16[2,256,768]{1,2,0:T(8,128)(2,1)} %constant_dynamic-update-slice_fusion), channel_id=1, source_target_pairs={{0,2},{2,4},{4,6},{6,8},{8,10},{10,12},{12,14},{1,3},{3,5},{5,7},{... | collective-permute-start | bytes 2359304 | tf_op jit(solution)/shard_map/ppermute | solution.py:18
  29.7 0.9 copy.110
  30.6 5.1 %all-to-all-start.1 = ((bf16[128,2,768]{0,2,1:T(8,128)(2,1)}), bf16[128,2,768]{0,2,1:T(8,128)(2,1)S(1)}, u32[]{:S(2)}, u32[]{:S(2)}) async-start(bf16[128,2,768]{0,2,1:T(8,128)(2,1)} %bitcast.4), calls=%async_computation.1 | async-start | bytes 786432 | tf_op jit(solution)/shard_map/all_to_all | solution.py:51
  38.7 0.4 copy.111
  39.3 0.5 fusion.107
  39.8 12.7 %collective-permute-start.1 = (bf16[2,256,768]{1,2,0:T(8,128)(2,1)}, bf16[2,256,768]{1,2,0:T(8,128)(2,1)S(1)}, u32[]{:S(2)}, u32[]{:S(2)}) collective-permute-start(bf16[2,256,768]{1,2,0:T(8,128)(2,1)} %constant_dynamic-update-slice_fusion), channel_id=1, source_target_pairs={{2,0},{4,2},{6,4},{8,6},{10,8},{12,10},{14,12},{3,1},{5,3},{7,5},{... | collective-permute-start | bytes 2359304 | tf_op jit(solution)/shard_map/ppermute | solution.py:18
  52.5 1.2 %fusion.99 = (bf16[1,256,768]{1,2,0:T(8,128)(2,1)S(1)}, bf16[1,256,768]{1,2,0:T(8,128)(2,1)S(1)}) fusion(bf16[2,256,768]{1,2,0:T(8,128)(2,1)} %collective-permute-done.4), kind=kLoop, calls=%fused_computation.165 | loop fusion | bytes 1572864 | tf_op jit(solution)/shard_map/slice | solution.py:83
  53.7 17.3 %collective-permute-done.2 = bf16[2,256,768]{1,2,0:T(8,128)(2,1)} collective-permute-done((bf16[2,256,768]{1,2,0:T(8,128)(2,1)}, bf16[2,256,768]{1,2,0:T(8,128)(2,1)}, u32[]{:S(2)}, u32[]{:S(2)}) %collective-permute-start.2) | collective-permute-done | bytes 786464 | tf_op jit(solution)/shard_map/ppermute | solution.py:18
  70.9 1.2 %fusion.97 = (bf16[1,256,768]{1,2,0:T(8,128)(2,1)S(1)}, bf16[1,256,768]{1,2,0:T(8,128)(2,1)S(1)}) fusion(bf16[2,256,768]{1,2,0:T(8,128)(2,1)} %collective-permute-done.2), kind=kLoop, calls=%fused_computation.163 | loop fusion | bytes 1572864 | tf_op jit(solution)/shard_map/slice | solution.py:83
  72.1 15.1 %collective-permute-done = bf16[2,256,768]{1,2,0:T(8,128)(2,1)} collective-permute-done((bf16[2,256,768]{1,2,0:T(8,128)(2,1)}, bf16[2,256,768]{1,2,0:T(8,128)(2,1)}, u32[]{:S(2)}, u32[]{:S(2)}) %collective-permute-start) | collective-permute-done | bytes 786464 | tf_op jit(solution)/shard_map/ppermute | solution.py:18
  87.3 1.2 %fusion.95 = (bf16[1,256,768]{1,2,0:T(8,128)(2,1)S(1)}, bf16[1,256,768]{1,2,0:T(8,128)(2,1)S(1)}) fusion(bf16[2,256,768]{1,2,0:T(8,128)(2,1)} %collective-permute-done), kind=kLoop, calls=%fused_computation.161 | loop fusion | bytes 1572864 | tf_op jit(solution)/shard_map/slice | solution.py:83
  88.4 0.5 fusion.106
  88.9 4.2 %collective-permute-done.1 = bf16[2,256,768]{1,2,0:T(8,128)(2,1)S(1)} collective-permute-done((bf16[2,256,768]{1,2,0:T(8,128)(2,1)}, bf16[2,256,768]{1,2,0:T(8,128)(2,1)S(1)}, u32[]{:S(2)}, u32[]{:S(2)}) %collective-permute-start.1) | collective-permute-done | bytes 786464 | tf_op jit(solution)/shard_map/ppermute | solution.py:18
  93.1 0.5 fusion.105
  93.6 0.5 fusion.104
  94.1 1.2 %fusion.98 = (bf16[1,256,768]{1,2,0:T(8,128)(2,1)S(1)}, bf16[1,256,768]{1,2,0:T(8,128)(2,1)S(1)}) fusion(bf16[2,256,768]{1,2,0:T(8,128)(2,1)} %collective-permute-done.3), kind=kLoop, calls=%fused_computation.164 | loop fusion | bytes 1572864 | tf_op jit(solution)/shard_map/slice | solution.py:84
  95.2 0.5 fusion.103
  95.7 0.5 fusion.102
  96.2 0.5 fusion.101
  96.7 0.3 fusion.26
  97.0 0.5 convolution_bitcast_fusion
  97.5 0.3 fusion.24
  97.9 0.5 convolution_bitcast_fusion.1
  98.4 0.3 fusion.22
  98.7 0.5 convolution_bitcast_fusion.2
  99.2 0.3 fusion.20
  99.5 0.5 convolution_bitcast_fusion.3
  100.0 0.3 fusion.18
  100.3 0.5 convolution_bitcast_fusion.4
  100.9 0.3 fusion.14
  101.2 0.3 fusion.16
  101.5 0.9 fusion.1
  102.5 2.0 %fusion.28 = bf16[256,6,128]{2,0,1:T(8,128)(2,1)S(1)} fusion(f32[256,6,128]{2,0,1:T(8,128)S(1)} %convolution_bitcast_fusion, f32[256,6,128]{2,0,1:T(8,128)S(1)} %convolution_bitcast_fusion.1, f32[256,6,128]{2,0,1:T(8,128)S(1)} %convolution_bitcast_fusion.2, f32[256,6,128]{2,0,1:T(8,128)S(1)} %convolution_bitcast_fusion.3, ...), kind=kOutput, calls=%fused_computation.49 | convolution fusion | flops 104398848 | bytes 7186432 | tf_op jit(solution)/shard_map/qhk,khd->qhd/dot_general | solution.py:43
  104.8 4.8 %all_to_all.67 = bf16[2,128,768]{1,2,0:T(8,128)(2,1)S(1)} all-to-all(bf16[2,128,768]{1,2,0:T(8,128)(2,1)S(1)} %copy.151), channel_id=1, replica_groups=mesh['groups'=2,'blk'=8,'uly'=2] {'uly'}, dimensions={0} | all-to-all | bytes 786432 | tf_op jit(solution)/shard_map/all_to_all | solution.py:87
  109.6 0.9 copy.152
  (48 shorter events, 4.1 us)
Async XLA Ops:
  0.0 6.1 %copy-start = (bf16[128,1536]{1,0:T(8,128)(2,1)S(1)}, bf16[128,1536]{1,0:T(8,128)(2,1)}, u32[]{:S(2)}) copy-start(bf16[128,1536]{1,0:T(8,128)(2,1)} %param.6) | copy-start | bytes 1179652
  2.0 5.4 %all-to-all-start = ((bf16[128,2,768]{0,2,1:T(8,128)(2,1)}), bf16[128,2,768]{0,2,1:T(8,128)(2,1)S(1)}, u32[]{:S(2)}, u32[]{:S(2)}) async-start(bf16[128,2,768]{0,2,1:T(8,128)(2,1)} %bitcast.2), calls=%async_computation | async-start | bytes 786432 | tf_op jit(solution)/shard_map/all_to_all | solution.py:52
  7.4 5.3 %all-to-all-start.2 = ((bf16[128,2,768]{0,2,1:T(8,128)(2,1)}), bf16[128,2,768]{0,2,1:T(8,128)(2,1)S(1)}, u32[]{:S(2)}, u32[]{:S(2)}) async-start(bf16[128,2,768]{0,2,1:T(8,128)(2,1)} %bitcast.7), calls=%async_computation.2 | async-start | bytes 786432 | tf_op jit(solution)/shard_map/all_to_all | solution.py:53
  11.9 17.8 %copy-start.1 = (bf16[128,1536]{1,0:T(8,128)(2,1)S(1)}, bf16[128,1536]{1,0:T(8,128)(2,1)}, u32[]{:S(2)}) copy-start(bf16[128,1536]{1,0:T(8,128)(2,1)} %param.4) | copy-start | bytes 1179652
  13.1 22.6 %copy-start.2 = (s32[4,28]{1,0:T(4,128)S(1)}, s32[4,28]{1,0:T(4,128)}, u32[]{:S(2)}) copy-start(s32[4,28]{1,0:T(4,128)} %param.7) | copy-start | bytes 1348
  14.1 82.0 %collective-permute-start.5 = (bf16[2,256,768]{1,2,0:T(8,128)(2,1)}, bf16[2,256,768]{1,2,0:T(8,128)(2,1)S(1)}, u32[]{:S(2)}, u32[]{:S(2)}) collective-permute-start(bf16[2,256,768]{1,2,0:T(8,128)(2,1)} %constant_dynamic-update-slice_fusion), channel_id=1, source_target_pairs={{6,0},{8,2},{10,4},{12,6},{14,8},{7,1},{9,3},{11,5},{13,7},{15,9},... | collective-permute-start | bytes 2359304 | tf_op jit(solution)/shard_map/ppermute | solution.py:18
  15.4 24.4 %collective-permute-start.4 = (bf16[2,256,768]{1,2,0:T(8,128)(2,1)}, bf16[2,256,768]{1,2,0:T(8,128)(2,1)}, u32[]{:S(2)}, u32[]{:S(2)}) collective-permute-start(bf16[2,256,768]{1,2,0:T(8,128)(2,1)} %constant_dynamic-update-slice_fusion), channel_id=1, source_target_pairs={{0,6},{2,8},{4,10},{6,12},{8,14},{1,7},{3,9},{5,11},{7,13},{9,15},... | collective-permute-start | bytes 2359304 | tf_op jit(solution)/shard_map/ppermute | solution.py:18
  21.3 72.8 %collective-permute-start.3 = (bf16[2,256,768]{1,2,0:T(8,128)(2,1)}, bf16[2,256,768]{1,2,0:T(8,128)(2,1)}, u32[]{:S(2)}, u32[]{:S(2)}) collective-permute-start(bf16[2,256,768]{1,2,0:T(8,128)(2,1)} %constant_dynamic-update-slice_fusion), channel_id=1, source_target_pairs={{4,0},{6,2},{8,4},{10,6},{12,8},{14,10},{5,1},{7,3},{9,5},{11,7},{... | collective-permute-start | bytes 2359304 | tf_op jit(solution)/shard_map/ppermute | solution.py:18
  23.2 47.8 %collective-permute-start.2 = (bf16[2,256,768]{1,2,0:T(8,128)(2,1)}, bf16[2,256,768]{1,2,0:T(8,128)(2,1)}, u32[]{:S(2)}, u32[]{:S(2)}) collective-permute-start(bf16[2,256,768]{1,2,0:T(8,128)(2,1)} %constant_dynamic-update-slice_fusion), channel_id=1, source_target_pairs={{0,4},{2,6},{4,8},{6,10},{8,12},{10,14},{1,5},{3,7},{5,9},{7,11},{... | collective-permute-start | bytes 2359304 | tf_op jit(solution)/shard_map/ppermute | solution.py:18
  26.6 60.7 %collective-permute-start = (bf16[2,256,768]{1,2,0:T(8,128)(2,1)}, bf16[2,256,768]{1,2,0:T(8,128)(2,1)}, u32[]{:S(2)}, u32[]{:S(2)}) collective-permute-start(bf16[2,256,768]{1,2,0:T(8,128)(2,1)} %constant_dynamic-update-slice_fusion), channel_id=1, source_target_pairs={{0,2},{2,4},{4,6},{6,8},{8,10},{10,12},{12,14},{1,3},{3,5},{5,7},{... | collective-permute-start | bytes 2359304 | tf_op jit(solution)/shard_map/ppermute | solution.py:18
  30.6 8.0 %all-to-all-start.1 = ((bf16[128,2,768]{0,2,1:T(8,128)(2,1)}), bf16[128,2,768]{0,2,1:T(8,128)(2,1)S(1)}, u32[]{:S(2)}, u32[]{:S(2)}) async-start(bf16[128,2,768]{0,2,1:T(8,128)(2,1)} %bitcast.4), calls=%async_computation.1 | async-start | bytes 786432 | tf_op jit(solution)/shard_map/all_to_all | solution.py:51
  39.8 53.3 %collective-permute-start.1 = (bf16[2,256,768]{1,2,0:T(8,128)(2,1)}, bf16[2,256,768]{1,2,0:T(8,128)(2,1)S(1)}, u32[]{:S(2)}, u32[]{:S(2)}) collective-permute-start(bf16[2,256,768]{1,2,0:T(8,128)(2,1)} %constant_dynamic-update-slice_fusion), channel_id=1, source_target_pairs={{2,0},{4,2},{6,4},{8,6},{10,8},{12,10},{14,12},{3,1},{5,3},{7,5},{... | collective-permute-start | bytes 2359304 | tf_op jit(solution)/shard_map/ppermute | solution.py:18
where the time goes:
time: 111 us
  starting transfers between devices  41.2 us (37%)
  waiting for transfers between devices  37 us (33%)
  local copies, waits for them, and re-layouts  15.2 us (14%)
  matrix products  9.74 us (9%)
  blocking collectives  4.79 us (4%)
  other arithmetic  2.19 us (2%)
    ppermute x6, waiting for transfers between devices, from_behind(): return lax.ppermute(block, axis, route)  36.6 us
    ppermute x6, starting transfers between devices, from_behind(): return lax.ppermute(block, axis, route)  28.2 us
    dot_general x7, matrix products, attend(): jnp.einsum('qhk,khd->qhd', weights.astype(jnp.bfloat16), values_h, prefer...  5.62 us
    all_to_all x1, starting transfers between devices, body(): lax.all_to_all(query, 'uly', split_axis=1, concat_axis=0, tiled=True)  5.06 us
    all_to_all x1, blocking collectives, body(): lax.all_to_all(output, 'uly', split_axis=0, concat_axis=1, tiled=True)  4.79 us
    unnamed x10, local copies, waits for them, and re-layouts  4.57 us
    all_to_all x1, starting transfers between devices, body(): lax.all_to_all(key, 'uly', split_axis=1, concat_axis=0, tiled=True)  4.13 us
    all_to_all x1, starting transfers between devices, body(): lax.all_to_all(value, 'uly', split_axis=1, concat_axis=0, tiled=True)  3.83 us
  transfers between devices with their start and end apart: 9, of which 4 were waited for; matrix products, arithmetic and copies ran while one was open for 13% of the time, Pallas kernels for 0%

commit v1 on v0

v1 whole, which is shorter than its diff:
```python
import functools
import math

import jax
import jax.numpy as jnp
from jax import lax
from jax.experimental import pallas as pl
from jax.experimental.pallas import tpu as pltpu
from jax.sharding import PartitionSpec as P

HD = 128
TILE = 64
TH = 4
TW = 2
HEADS_STEP = 2
FILL = -1e30
LOG2E = 1.4426950408889634


def plane_pairs(n_blk, n_uly, parity):
    rows = TH // n_uly
    planes = n_blk // rows
    route = []
    for blk in range(n_blk):
        t = blk // rows
        other = t + 1 if t % 2 == parity else t - 1
        for u in range(n_uly):
            if 0 <= other < planes:
                there = (other * rows + blk % rows) * n_uly + u
            else:
                there = blk * n_uly + n_uly - 1 - u
            route.append((blk * n_uly + u, there))
    return route


def row_pairs(n_groups, n_blk, n_uly):
    route = []
    size = n_blk * n_uly
    for g in range(n_groups):
        for i in range(size):
            h = i % TH
            if h == 1:
                there = g * size + i + 1
            elif h == 2:
                there = g * size + i - 1
            else:
                there = (g + 1) % n_groups * size + i
            route.append((g * size + i, there))
    return route


def scores_kernel(meta, keep_own, keep_x, q_own, q_d, q_x, k_own, k_e, k_o, p_ref, st_own, st_d, st_x, bias):
    scale = LOG2E / math.sqrt(HD)
    parity, xh, u, inner = meta[0], meta[1], meta[2], meta[3]
    step = 1 - 2 * parity

    @pl.when(pl.program_id(0) == 0)
    def _():
        first = lax.broadcasted_iota(jnp.int32, (1, HD), 1) < TILE
        for src in range(3):
            table = keep_x if src == 2 else keep_own
            row = TW * (u if src == 0 else 1 - u)
            half = (1 - xh) if src == 2 else xh
            for n, dt in enumerate((0, step, -step)):
                column = TH * TW * dt + TW * (2 * xh + u) - 2 * TW * half + 12
                for w in range(TW):
                    col = jnp.clip(column + w, 0, keep_own.shape[1] - 1)
                    low = jnp.where(table[row, col] > 0, 0.0, FILL)
                    high = jnp.where(table[row + 1, col] > 0, 0.0, FILL)
                    bias[pl.ds((src * 3 + n) * TW + w, 1), :] = jnp.where(first, low, high)

    def one(src, i, q_ref, st_ref):
        cols = pl.ds(i * HD, HD)
        q = q_ref[:, cols]
        parts = []
        for n, k_ref in enumerate((k_own, k_e, k_o)):
            s = lax.dot_general(k_ref[:, cols], q, (((1,), (1,)), ((), ())), preferred_element_type=jnp.float32)
            for w in range(TW):
                b = bias[pl.ds((src * 3 + n) * TW + w, 1), :]
                parts.append(s[w * TILE : (w + 1) * TILE] * scale + b)
        t = jnp.concatenate(parts, axis=0)
        m = jnp.max(t, axis=0, keepdims=True)
        e = jnp.exp2(t - m)
        total = jnp.sum(e, axis=0, keepdims=True)
        p_ref[i, :, src * HD : (src + 1) * HD] = e.astype(jnp.bfloat16)
        st_ref[0, pl.ds(i, 1), :] = m
        st_ref[0, pl.ds(HEADS_STEP + i, 1), :] = total

    for i in range(HEADS_STEP):
        one(0, i, q_own, st_own)
        one(1, i, q_d, st_d)

    @pl.when(inner == 1)
    def _():
        for i in range(HEADS_STEP):
            one(2, i, q_x, st_x)


def values_kernel(p_ref, v_own, v_e, v_o, st_own, st_d, st_x, o_own, o_d, o_x):
    for i in range(HEADS_STEP):
        cols = pl.ds(i * HD, HD)
        v = jnp.concatenate([v_own[:, cols], v_e[:, cols], v_o[:, cols]], axis=0)
        acc = lax.dot_general(v, p_ref[i], (((0,), (0,)), ((), ())), preferred_element_type=jnp.float32)
        for src, (o_ref, st) in enumerate(((o_own, st_own), (o_d, st_d), (o_x, st_x))):
            total = st[0, pl.ds(HEADS_STEP + i, 1), :]
            o_ref[cols, :] = (acc[:, src * HD : (src + 1) * HD] / total).astype(o_ref.dtype)


def combine_kernel(meta, o_own, o_d, o_x, st_own, st_d, st_x, out):
    inner = meta[3] == 1
    m0, l0 = st_own[0, :HEADS_STEP], st_own[0, HEADS_STEP:]
    m1, l1 = st_d[0, :HEADS_STEP], st_d[0, HEADS_STEP:]
    m2 = jnp.where(inner, st_x[0, :HEADS_STEP], FILL)
    l2 = jnp.where(inner, st_x[0, HEADS_STEP:], 0.0)
    peak = jnp.maximum(jnp.maximum(m0, m1), m2)
    f0, f1, f2 = l0 * jnp.exp2(m0 - peak), l1 * jnp.exp2(m1 - peak), l2 * jnp.exp2(m2 - peak)
    total = f0 + f1 + f2
    w0, w1, w2 = f0 / total, f1 / total, f2 / total
    for i in range(HEADS_STEP):
        cols = pl.ds(i * HD, HD)
        o = o_own[cols, :] * w0[i : i + 1] + o_d[cols, :].astype(jnp.float32) * w1[i : i + 1]
        x = jnp.where(inner, o_x[cols, :].astype(jnp.float32), 0.0)
        o = o + x * w2[i : i + 1]
        out[:, cols] = o.T.astype(out.dtype)


def body(n_groups, query, key, value, keep):
    n_blk, n_uly = lax.axis_size("blk"), lax.axis_size("uly")
    rows, width = query.shape
    heads = width // HD
    steps = heads // HEADS_STEP
    axes = ("blk", "uly")
    everyone = ("groups", "blk", "uly")
    even, odd = plane_pairs(n_blk, n_uly, 0), plane_pairs(n_blk, n_uly, 1)
    cross = row_pairs(n_groups, n_blk, n_uly)
    cores = [(0, 1), (1, 0)]
    halves = [(b, b ^ 1) for b in range(n_blk)]

    blk, u = lax.axis_index("blk"), lax.axis_index("uly")
    xh = blk % 2
    meta = jnp.stack([blk // 2 % 2, xh, u, (xh != u).astype(jnp.int32)]).astype(jnp.int32)

    k_e = lax.ppermute(key, axes, even)
    k_o = lax.ppermute(key, axes, odd)
    keep_x = lax.ppermute(keep, "blk", halves)
    q_x = lax.ppermute(query, everyone, cross)
    q_d = lax.ppermute(query, "uly", cores)
    v_e = lax.ppermute(value, axes, even)
    v_o = lax.ppermute(value, axes, odd)

    smem = pl.BlockSpec(memory_space=pltpu.SMEM)
    feat = pl.BlockSpec((rows, HEADS_STEP * HD), lambda g: (0, g))
    tall = pl.BlockSpec((HEADS_STEP * HD, rows), lambda g: (g, 0))
    stat = pl.BlockSpec((1, 2 * HEADS_STEP, rows), lambda g: (g, 0, 0))
    prob = pl.BlockSpec((HEADS_STEP, 3 * rows, 3 * rows), lambda g: (g, 0, 0))
    stat_shape = jax.ShapeDtypeStruct((steps, 2 * HEADS_STEP, rows), jnp.float32)

    p, st_own, st_d, st_x = pl.pallas_call(
        scores_kernel,
        grid=(steps,),
        in_specs=[smem, smem, smem] + [feat] * 6,
        out_specs=[prob, stat, stat, stat],
        out_shape=[jax.ShapeDtypeStruct((heads, 3 * rows, 3 * rows), jnp.bfloat16), stat_shape, stat_shape, stat_shape],
        scratch_shapes=[pltpu.VMEM((24, HD), jnp.float32)],
        name="scores",
    )(meta, keep, keep_x, query, q_d, q_x, key, k_e, k_o)

    in_d = lax.ppermute(st_d, "uly", cores)
    in_x = lax.ppermute(st_x, everyone, cross)

    o_own, o_d, o_x = pl.pallas_call(
        values_kernel,
        grid=(steps,),
        in_specs=[prob, feat, feat, feat, stat, stat, stat],
        out_specs=[tall, tall, tall],
        out_shape=[
            jax.ShapeDtypeStruct((width, rows), jnp.float32),
            jax.ShapeDtypeStruct((width, rows), jnp.bfloat16),
            jax.ShapeDtypeStruct((width, rows), jnp.bfloat16),
        ],
        name="values",
    )(p, value, v_e, v_o, st_own, st_d, st_x)

    back_x = lax.ppermute(o_x, everyone, cross)
    back_d = lax.ppermute(o_d, "uly", cores)

    return pl.pallas_call(
        combine_kernel,
        grid=(steps,),
        in_specs=[smem, tall, tall, tall, stat, stat, stat],
        out_specs=feat,
        out_shape=jax.ShapeDtypeStruct((rows, width), query.dtype),
        name="combine",
    )(meta, o_own, back_d, back_x, st_own, in_d, in_x)


def solution(mesh):
    tokens = P(("groups", "blk", "uly"), None)
    return jax.shard_map(
        functools.partial(body, mesh.shape["groups"]),
        mesh=mesh,
        in_specs=(tokens, tokens, tokens, P(("groups", "blk"), None)),
        out_specs=tokens,
        check_vma=False,
    )
```

time: 111 us -> 46.2 us (0.42)
  the two profiles are of different devices: /device:TPU:9 before, /device:TPU:0 now
where the time goes in v1:
time: 46.2 us; the launch traced here: 45.5 us
  Pallas kernels  17.3 us (37%)
  waiting for transfers between devices  12.8 us (28%)
  starting transfers between devices  11.5 us (25%)
  local copies, waits for them, and re-layouts  3.23 us (7%)
  other arithmetic  0.6 us (1%)
    pallas_call x1, Pallas kernels, body(): pl.pallas_call(scores_kernel, grid=(steps,), in_specs=[smem, smem, smem]...  6.63 us
    pallas_call x1, Pallas kernels, body(): pl.pallas_call(values_kernel, grid=(steps,), in_specs=[prob, feat, feat,...  6.01 us
    ppermute x1, waiting for transfers between devices, body(): in_x = lax.ppermute(st_x, everyone, cross)  5.93 us
    ppermute x1, waiting for transfers between devices, body(): k_e = lax.ppermute(key, axes, even)  5.79 us
    pallas_call x1, Pallas kernels, body(): pl.pallas_call(combine_kernel, grid=(steps,), in_specs=[smem, tall, tall,...  4.62 us
    unnamed x26, local copies, waits for them, and re-layouts  3.23 us
    ppermute x1, starting transfers between devices, body(): v_e = lax.ppermute(value, axes, even)  3.15 us
    ppermute x1, starting transfers between devices, body(): keep_x = lax.ppermute(keep, 'blk', halves)  2.49 us
  transfers between devices with their start and end apart: 11, of which 3 were waited for; matrix products, arithmetic and copies ran while one was open for 1% of the time, Pallas kernels for 15%

profile of v1, /device:TPU:0, one launch (start us, length us, event | category | flops | bytes accessed | tf_op | source)
XLA Modules:
  0.0 45.5 jit_solution(9041695106112716246)
XLA Ops:
  0.0 0.5 collective-permute-start.1
  0.5 2.5 %collective-permute-start = (s32[4,28]{1,0:T(4,128)}, s32[4,28]{1,0:T(4,128)S(1)}, u32[]{:S(2)}, u32[]{:S(2)}) collective-permute-start(s32[4,28]{1,0:T(4,128)} %keep_own.1), channel_id=1, source_target_pairs={{0,2},{2,0},{4,6},{6,4},{8,10},{10,8},{12,14},{14,12},{1,3},{3,1},... | collective-permute-start | bytes 1352 | tf_op jit(solution)/shard_map/ppermute | solution.py:145
  2.9 1.5 %collective-permute-start.2 = (bf16[128,1536]{1,0:T(8,128)(2,1)}, bf16[128,1536]{1,0:T(8,128)(2,1)S(1)}, u32[]{:S(2)}, u32[]{:S(2)}) collective-permute-start(bf16[128,1536]{1,0:T(8,128)(2,1)} %q_own.1), channel_id=1, source_target_pairs={{0,16},{1,2},{2,1},{3,19},{4,20},{5,6},{6,5},{7,23},{8,24},{9,10},... | collective-permute-start | bytes 1179656 | tf_op jit(solution)/shard_map/ppermute | solution.py:146
  4.5 1.6 %collective-permute-start.3 = (bf16[128,1536]{1,0:T(8,128)(2,1)}, bf16[128,1536]{1,0:T(8,128)(2,1)S(1)}, u32[]{:S(2)}, u32[]{:S(2)}) collective-permute-start(bf16[128,1536]{1,0:T(8,128)(2,1)} %k_own.1), channel_id=1, source_target_pairs={{0,4},{1,5},{2,6},{3,7},{4,0},{5,1},{6,2},{7,3},{8,12},{9,13},{10,... | collective-permute-start | bytes 1179656 | tf_op jit(solution)/shard_map/ppermute | solution.py:143
  6.0 0.0 collective-permute-start.4
  6.0 0.0 collective-permute-done.keep_x
  6.0 0.0 copy-start.12
  6.1 3.1 %collective-permute-start.5 = (bf16[128,1536]{1,0:T(8,128)(2,1)}, bf16[128,1536]{1,0:T(8,128)(2,1)S(1)}, u32[]{:S(2)}, u32[]{:S(2)}) collective-permute-start(bf16[128,1536]{1,0:T(8,128)(2,1)} %v_own.1), channel_id=1, source_target_pairs={{0,4},{1,5},{2,6},{3,7},{4,0},{5,1},{6,2},{7,3},{8,12},{9,13},{10,... | collective-permute-start | bytes 1179656 | tf_op jit(solution)/shard_map/ppermute | solution.py:148
  9.2 0.0 collective-permute-done.1.q_d
  9.2 0.0 copy-start.2
  9.2 0.0 collective-permute-start.6
  9.2 0.6 %pad_add_fusion.meta = s32[4]{0:T(128)} fusion(s32[1]{0:T(128)} %bitcast.3, s32[1]{0:T(128)} %bitcast.2, s32[1]{0:T(128)} %bitcast.1, s32[1]{0:T(128)} %bitcast), kind=kLoop, calls=%fused_computation | loop fusion | flops 12 | bytes 32 | tf_op jit(solution)/shard_map/stack | solution.py:141
  9.8 1.1 %collective-permute-done.2.q_x = bf16[128,1536]{1,0:T(8,128)(2,1)S(1)} collective-permute-done((bf16[128,1536]{1,0:T(8,128)(2,1)}, bf16[128,1536]{1,0:T(8,128)(2,1)S(1)}, u32[]{:S(2)}, u32[]{:S(2)}) %collective-permute-start.2) | collective-permute-done | bytes 393248 | tf_op jit(solution)/shard_map/ppermute | solution.py:146
  10.9 0.0 copy-start.3
  10.9 5.8 %collective-permute-done.3.k_e = bf16[128,1536]{1,0:T(8,128)(2,1)S(1)} collective-permute-done((bf16[128,1536]{1,0:T(8,128)(2,1)}, bf16[128,1536]{1,0:T(8,128)(2,1)S(1)}, u32[]{:S(2)}, u32[]{:S(2)}) %collective-permute-start.3) | collective-permute-done | bytes 393248 | tf_op jit(solution)/shard_map/ppermute | solution.py:143
  16.7 0.0 copy-start.4
  16.7 0.0 collective-permute-done.4.k_o
  16.7 0.0 copy-done.12
  16.7 0.0 copy-done.2
  16.7 0.0 copy-done.3
  16.8 0.7 %copy-done.4 = bf16[128,1536]{1,0:T(8,128)(2,1)} copy-done((bf16[128,1536]{1,0:T(8,128)(2,1)}, bf16[128,1536]{1,0:T(8,128)(2,1)S(1)}, u32[]{:S(2)}) %copy-start.4) | copy-done | bytes 393240
  17.5 0.8 %copy-done.5 = bf16[128,1536]{1,0:T(8,128)(2,1)} copy-done((bf16[128,1536]{1,0:T(8,128)(2,1)}, bf16[128,1536]{1,0:T(8,128)(2,1)S(1)}, u32[]{:S(2)}) %copy-start.5) | copy-done | bytes 393240
  18.2 6.6 %scores.1 = (bf16[12,384,384]{2,1,0:T(8,128)(2,1)}, f32[6,4,128]{2,1,0:T(4,128)}, f32[6,4,128]{2,1,0:T(4,128)}, f32[6,4,128]{2,1,0:T(4,128)}) custom-call(s32[4]{0:T(128)} %pad_add_fusion.meta, s32[4,28]{1,0:T(4,128)} %keep_own.1, s32[4,28]{1,0:T(4,128)} %copy-done.12, bf16[128,1536]{1,0:T(8,128)(2,1)} %q_own.1, bf16[128,1536]{1,0:T(8,128)(2,1)} %copy-done.2, ...), custom_call_target="tpu_custom_call" | custom-call | tf_op jit(solution)/shard_map/scores/pallas_call | solution.py:158
  24.9 0.0 copy-start.10
  24.9 0.0 collective-permute-done.5.v_e
  24.9 0.0 copy-start.6
  24.9 0.0 collective-permute-done.6.v_o
  24.9 0.0 copy-start.7
  24.9 0.7 %copy-done.6 = bf16[128,1536]{1,0:T(8,128)(2,1)} copy-done((bf16[128,1536]{1,0:T(8,128)(2,1)}, bf16[128,1536]{1,0:T(8,128)(2,1)S(1)}, u32[]{:S(2)}) %copy-start.6) | copy-done | bytes 393240
  25.6 0.2 copy-done.7
  25.8 6.0 %values.1 = (f32[1536,128]{1,0:T(8,128)}, bf16[1536,128]{1,0:T(8,128)(2,1)}, bf16[1536,128]{1,0:T(8,128)(2,1)}) custom-call(bf16[12,384,384]{2,1,0:T(8,128)(2,1)} %get-tuple-element.12.p_ref, bf16[128,1536]{1,0:T(8,128)(2,1)} %v_own.1, bf16[128,1536]{1,0:T(8,128)(2,1)} %copy-done.6, bf16[128,1536]{1,0:T(8,128)(2,1)} %copy-done.7, ...), custom_call_target="tpu_custom_call" | custom-call | tf_op jit(solution)/shard_map/values/pallas_call | solution.py:171
  31.8 0.0 collective-permute-start.7
  31.9 0.5 %collective-permute-start.8 = (bf16[1536,128]{1,0:T(8,128)(2,1)}, bf16[1536,128]{1,0:T(8,128)(2,1)S(1)}, u32[]{:S(2)}, u32[]{:S(2)}) collective-permute-start(bf16[1536,128]{1,0:T(8,128)(2,1)} %get-tuple-element.18), channel_id=1, source_target_pairs={{0,16},{1,2},{2,1},{3,19},{4,20},{5,6},{6,5},{7,23},{8,24},{9,10},... | collective-permute-start | bytes 1179656 | tf_op jit(solution)/shard_map/ppermute | solution.py:184
  32.3 0.0 copy-done.11
  32.3 1.6 %collective-permute-start.10 = (f32[6,4,128]{2,1,0:T(4,128)S(1)}, f32[6,4,128]{2,1,0:T(4,128)S(1)}, u32[]{:S(2)}, u32[]{:S(2)}) collective-permute-start(f32[6,4,128]{2,1,0:T(4,128)S(1)} %copy-done.11), channel_id=1, source_target_pairs={{0,16},{1,2},{2,1},{3,19},{4,20},{5,6},{6,5},{7,23},{8,24},{9,10},... | collective-permute-start | bytes 36872 | tf_op jit(solution)/shard_map/ppermute | solution.py:169
  33.9 0.0 copy-done.10
  33.9 0.2 collective-permute-start.9
  34.1 5.9 %collective-permute-done.10.st_x = f32[6,4,128]{2,1,0:T(4,128)S(1)} collective-permute-done((f32[6,4,128]{2,1,0:T(4,128)S(1)}, f32[6,4,128]{2,1,0:T(4,128)S(1)}, u32[]{:S(2)}, u32[]{:S(2)}) %collective-permute-start.10) | collective-permute-done | bytes 12320 | tf_op jit(solution)/shard_map/ppermute | solution.py:169
  40.0 0.0 collective-permute-done.9.st_d
  40.0 0.0 collective-permute-done.7.o_d
  40.0 0.0 copy-start
  40.1 0.0 collective-permute-done.8.o_x
  40.1 0.0 copy-start.1
  40.1 0.6 %copy-done.8 = f32[6,4,128]{2,1,0:T(4,128)} copy-done((f32[6,4,128]{2,1,0:T(4,128)}, f32[6,4,128]{2,1,0:T(4,128)S(1)}, u32[]{:S(2)}) %copy-start.8) | copy-done | bytes 12312
  40.6 0.0 copy-done.9
  40.6 0.2 copy-done
  40.8 0.1 copy-done.1
  40.9 4.6 %combine.1 = bf16[128,1536]{1,0:T(8,128)(2,1)} custom-call(s32[4]{0:T(128)} %pad_add_fusion.meta, f32[1536,128]{1,0:T(8,128)} %get-tuple-element.16.o_own, bf16[1536,128]{1,0:T(8,128)(2,1)} %copy-done, bf16[1536,128]{1,0:T(8,128)(2,1)} %copy-done.1, f32[6,4,128]{2,1,0:T(4,128)} %get-tuple-element.13.st_own, f32[6,4,128]{2,1,0:T(4,128)} %copy-done.9, ...), custom_call_target="tpu_custom_call" | custom-call | tf_op jit(solution)/shard_map/combine/pallas_call | solution.py:187
  (4 shorter events, 0.0 us)
Async XLA Ops:
  0.0 9.2 %collective-permute-start.1 = (bf16[128,1536]{1,0:T(8,128)(2,1)}, bf16[128,1536]{1,0:T(8,128)(2,1)S(1)}, u32[]{:S(2)}, u32[]{:S(2)}) collective-permute-start(bf16[128,1536]{1,0:T(8,128)(2,1)} %q_own.1), channel_id=1, source_target_pairs={{0,1},{1,0},{2,3},{3,2},{4,5},{5,4},{6,7},{7,6},{8,9},{9,8},{10,11... | collective-permute-start | bytes 1179656 | tf_op jit(solution)/shard_map/ppermute | solution.py:147
  0.5 5.6 %collective-permute-start = (s32[4,28]{1,0:T(4,128)}, s32[4,28]{1,0:T(4,128)S(1)}, u32[]{:S(2)}, u32[]{:S(2)}) collective-permute-start(s32[4,28]{1,0:T(4,128)} %keep_own.1), channel_id=1, source_target_pairs={{0,2},{2,0},{4,6},{6,4},{8,10},{10,8},{12,14},{14,12},{1,3},{3,1},... | collective-permute-start | bytes 1352 | tf_op jit(solution)/shard_map/ppermute | solution.py:145
  2.9 8.0 %collective-permute-start.2 = (bf16[128,1536]{1,0:T(8,128)(2,1)}, bf16[128,1536]{1,0:T(8,128)(2,1)S(1)}, u32[]{:S(2)}, u32[]{:S(2)}) collective-permute-start(bf16[128,1536]{1,0:T(8,128)(2,1)} %q_own.1), channel_id=1, source_target_pairs={{0,16},{1,2},{2,1},{3,19},{4,20},{5,6},{6,5},{7,23},{8,24},{9,10},... | collective-permute-start | bytes 1179656 | tf_op jit(solution)/shard_map/ppermute | solution.py:146
  4.5 12.3 %collective-permute-start.3 = (bf16[128,1536]{1,0:T(8,128)(2,1)}, bf16[128,1536]{1,0:T(8,128)(2,1)S(1)}, u32[]{:S(2)}, u32[]{:S(2)}) collective-permute-start(bf16[128,1536]{1,0:T(8,128)(2,1)} %k_own.1), channel_id=1, source_target_pairs={{0,4},{1,5},{2,6},{3,7},{4,0},{5,1},{6,2},{7,3},{8,12},{9,13},{10,... | collective-permute-start | bytes 1179656 | tf_op jit(solution)/shard_map/ppermute | solution.py:143
  6.0 10.7 %collective-permute-start.4 = (bf16[128,1536]{1,0:T(8,128)(2,1)}, bf16[128,1536]{1,0:T(8,128)(2,1)S(1)}, u32[]{:S(2)}, u32[]{:S(2)}) collective-permute-start(bf16[128,1536]{1,0:T(8,128)(2,1)} %k_own.1), channel_id=1, source_target_pairs={{0,1},{1,0},{2,3},{3,2},{4,8},{5,9},{6,10},{7,11},{8,4},{9,5},{10,... | collective-permute-start | bytes 1179656 | tf_op jit(solution)/shard_map/ppermute | solution.py:144
  6.0 10.7 %copy-start.12 = (s32[4,28]{1,0:T(4,128)}, s32[4,28]{1,0:T(4,128)S(1)}, u32[]{:S(2)}) copy-start(s32[4,28]{1,0:T(4,128)S(1)} %collective-permute-done.keep_x) | copy-start | bytes 1348
  6.1 18.8 %collective-permute-start.5 = (bf16[128,1536]{1,0:T(8,128)(2,1)}, bf16[128,1536]{1,0:T(8,128)(2,1)S(1)}, u32[]{:S(2)}, u32[]{:S(2)}) collective-permute-start(bf16[128,1536]{1,0:T(8,128)(2,1)} %v_own.1), channel_id=1, source_target_pairs={{0,4},{1,5},{2,6},{3,7},{4,0},{5,1},{6,2},{7,3},{8,12},{9,13},{10,... | collective-permute-start | bytes 1179656 | tf_op jit(solution)/shard_map/ppermute | solution.py:148
  9.2 7.5 %copy-start.2 = (bf16[128,1536]{1,0:T(8,128)(2,1)}, bf16[128,1536]{1,0:T(8,128)(2,1)S(1)}, u32[]{:S(2)}) copy-start(bf16[128,1536]{1,0:T(8,128)(2,1)S(1)} %collective-permute-done.1.q_d) | copy-start | bytes 1179652
  9.2 15.7 %collective-permute-start.6 = (bf16[128,1536]{1,0:T(8,128)(2,1)}, bf16[128,1536]{1,0:T(8,128)(2,1)S(1)}, u32[]{:S(2)}, u32[]{:S(2)}) collective-permute-start(bf16[128,1536]{1,0:T(8,128)(2,1)} %v_own.1), channel_id=1, source_target_pairs={{0,1},{1,0},{2,3},{3,2},{4,8},{5,9},{6,10},{7,11},{8,4},{9,5},{10,... | collective-permute-start | bytes 1179656 | tf_op jit(solution)/shard_map/ppermute | solution.py:149
  10.9 5.8 %copy-start.3 = (bf16[128,1536]{1,0:T(8,128)(2,1)}, bf16[128,1536]{1,0:T(8,128)(2,1)S(1)}, u32[]{:S(2)}) copy-start(bf16[128,1536]{1,0:T(8,128)(2,1)S(1)} %collective-permute-done.2.q_x) | copy-start | bytes 1179652
  16.7 0.8 %copy-start.4 = (bf16[128,1536]{1,0:T(8,128)(2,1)}, bf16[128,1536]{1,0:T(8,128)(2,1)S(1)}, u32[]{:S(2)}) copy-start(bf16[128,1536]{1,0:T(8,128)(2,1)S(1)} %collective-permute-done.3.k_e) | copy-start | bytes 1179652
  17.5 0.8 %copy-start.5 = (bf16[128,1536]{1,0:T(8,128)(2,1)}, bf16[128,1536]{1,0:T(8,128)(2,1)S(1)}, u32[]{:S(2)}) copy-start(bf16[128,1536]{1,0:T(8,128)(2,1)S(1)} %collective-permute-done.4.k_o) | copy-start | bytes 1179652
  24.9 7.5 %copy-start.11 = (f32[6,4,128]{2,1,0:T(4,128)S(1)}, f32[6,4,128]{2,1,0:T(4,128)}, u32[]{:S(2)}) copy-start(f32[6,4,128]{2,1,0:T(4,128)} %get-tuple-element.15.st_x) | copy-start | bytes 36868
  24.9 9.1 %copy-start.10 = (f32[6,4,128]{2,1,0:T(4,128)S(1)}, f32[6,4,128]{2,1,0:T(4,128)}, u32[]{:S(2)}) copy-start(f32[6,4,128]{2,1,0:T(4,128)} %get-tuple-element.14.st_d) | copy-start | bytes 36868
  24.9 0.7 %copy-start.6 = (bf16[128,1536]{1,0:T(8,128)(2,1)}, bf16[128,1536]{1,0:T(8,128)(2,1)S(1)}, u32[]{:S(2)}) copy-start(bf16[128,1536]{1,0:T(8,128)(2,1)S(1)} %collective-permute-done.5.v_e) | copy-start | bytes 1179652
  24.9 0.9 %copy-start.7 = (bf16[128,1536]{1,0:T(8,128)(2,1)}, bf16[128,1536]{1,0:T(8,128)(2,1)S(1)}, u32[]{:S(2)}) copy-start(bf16[128,1536]{1,0:T(8,128)(2,1)S(1)} %collective-permute-done.6.v_o) | copy-start | bytes 1179652
  31.8 8.2 %collective-permute-start.7 = (bf16[1536,128]{1,0:T(8,128)(2,1)}, bf16[1536,128]{1,0:T(8,128)(2,1)S(1)}, u32[]{:S(2)}, u32[]{:S(2)}) collective-permute-start(bf16[1536,128]{1,0:T(8,128)(2,1)} %get-tuple-element.17), channel_id=1, source_target_pairs={{0,1},{1,0},{2,3},{3,2},{4,5},{5,4},{6,7},{7,6},{8,9},{9,8},{10,11... | collective-permute-start | bytes 1179656 | tf_op jit(solution)/shard_map/ppermute | solution.py:185
  31.9 8.2 %collective-permute-start.8 = (bf16[1536,128]{1,0:T(8,128)(2,1)}, bf16[1536,128]{1,0:T(8,128)(2,1)S(1)}, u32[]{:S(2)}, u32[]{:S(2)}) collective-permute-start(bf16[1536,128]{1,0:T(8,128)(2,1)} %get-tuple-element.18), channel_id=1, source_target_pairs={{0,16},{1,2},{2,1},{3,19},{4,20},{5,6},{6,5},{7,23},{8,24},{9,10},... | collective-permute-start | bytes 1179656 | tf_op jit(solution)/shard_map/ppermute | solution.py:184
  32.3 7.7 %collective-permute-start.10 = (f32[6,4,128]{2,1,0:T(4,128)S(1)}, f32[6,4,128]{2,1,0:T(4,128)S(1)}, u32[]{:S(2)}, u32[]{:S(2)}) collective-permute-start(f32[6,4,128]{2,1,0:T(4,128)S(1)} %copy-done.11), channel_id=1, source_target_pairs={{0,16},{1,2},{2,1},{3,19},{4,20},{5,6},{6,5},{7,23},{8,24},{9,10},... | collective-permute-start | bytes 36872 | tf_op jit(solution)/shard_map/ppermute | solution.py:169
  33.9 6.1 %collective-permute-start.9 = (f32[6,4,128]{2,1,0:T(4,128)S(1)}, f32[6,4,128]{2,1,0:T(4,128)S(1)}, u32[]{:S(2)}, u32[]{:S(2)}) collective-permute-start(f32[6,4,128]{2,1,0:T(4,128)S(1)} %copy-done.10), channel_id=1, source_target_pairs={{0,1},{1,0},{2,3},{3,2},{4,5},{5,4},{6,7},{7,6},{8,9},{9,8},{10,11... | collective-permute-start | bytes 36872 | tf_op jit(solution)/shard_map/ppermute | solution.py:168
  40.0 0.6 %copy-start.8 = (f32[6,4,128]{2,1,0:T(4,128)}, f32[6,4,128]{2,1,0:T(4,128)S(1)}, u32[]{:S(2)}) copy-start(f32[6,4,128]{2,1,0:T(4,128)S(1)} %collective-permute-done.10.st_x) | copy-start | bytes 36868
  40.0 0.6 %copy-start.9 = (f32[6,4,128]{2,1,0:T(4,128)}, f32[6,4,128]{2,1,0:T(4,128)S(1)}, u32[]{:S(2)}) copy-start(f32[6,4,128]{2,1,0:T(4,128)S(1)} %collective-permute-done.9.st_d) | copy-start | bytes 36868
  40.0 0.7 %copy-start = (bf16[1536,128]{1,0:T(8,128)(2,1)}, bf16[1536,128]{1,0:T(8,128)(2,1)S(1)}, u32[]{:S(2)}) copy-start(bf16[1536,128]{1,0:T(8,128)(2,1)S(1)} %collective-permute-done.7.o_d) | copy-start | bytes 1179652
  40.1 0.9 %copy-start.1 = (bf16[1536,128]{1,0:T(8,128)(2,1)}, bf16[1536,128]{1,0:T(8,128)(2,1)S(1)}, u32[]{:S(2)}) copy-start(bf16[1536,128]{1,0:T(8,128)(2,1)S(1)} %collective-permute-done.8.o_x) | copy-start | bytes 1179652

commit v2 on v0

v2 whole, which is shorter than its diff:
```python
import functools
import math

import jax
import jax.numpy as jnp
from jax import lax
from jax.experimental import pallas as pl
from jax.experimental.pallas import tpu as pltpu
from jax.sharding import PartitionSpec as P

HD = 128
TILE = 64
TH = 4
TW = 2
HEADS_STEP = 2
STAT = 16
FLAG_ROWS = 16
FILL = -1e30
LOG2E = 1.4426950408889634


def plane_pairs(n_blk, n_uly, parity):
    blks = TH // n_uly
    route = []
    for blk in range(n_blk):
        t = blk // blks
        other = t + 1 if t % 2 == parity else t - 1
        for u in range(n_uly):
            there = blk, n_uly - 1 - u
            if 0 <= other < n_blk // blks:
                there = other * blks + blk % blks, u
            route.append((blk * n_uly + u, there[0] * n_uly + there[1]))
    return route


def row_pairs(n_groups, n_blk, n_uly):
    route = []
    size = n_blk * n_uly
    for g in range(n_groups):
        for i in range(size):
            h = i % TH
            if h == 1:
                there = g * size + i + 1
            elif h == 2:
                there = g * size + i - 1
            else:
                there = (g + 1) % n_groups * size + i
            route.append((g * size + i, there))
    return route


def place():
    n_uly = lax.axis_size("uly")
    rows = TH // n_uly
    blk = lax.axis_index("blk")
    row = lax.rem(blk, rows) * n_uly + lax.axis_index("uly")
    return lax.rem(lax.div(blk, rows), 2), row, (row > 0) & (row < TH - 1)


def flag_rows(keep, parity, key_row, query_row):
    first = lax.broadcasted_iota(jnp.int32, (1, HD), 1) < TILE
    tiles = keep.shape[0]
    line = lax.rem(query_row * TW, tiles)
    base = (keep.shape[1] - tiles) // 2
    step = 1 - 2 * parity
    rows = []
    for dt in (0, step, -step):
        column = base + TH * TW * dt + TW * (key_row - query_row) + line
        for w in range(TW):
            col = jnp.clip(column + w, 0, keep.shape[1] - 1)
            low = (keep[line, col] > 0).astype(jnp.float32)
            high = (keep[line + 1, col] > 0).astype(jnp.float32)
            rows.append(jnp.where(first, low, high))
    return rows


def prepare_kernel(keep_hbm, q_hbm, bias, q_out, keep, sems):
    tokens = q_hbm.shape[0]
    flags = pltpu.make_async_copy(keep_hbm, keep, sems.at[0])
    flags.start()
    copy = pltpu.make_async_copy(q_hbm, q_out.at[:tokens], sems.at[1])
    copy.start()
    flags.wait()
    parity, row, _ = place()
    sibling = row + 1 - 2 * lax.rem(row, 2)
    across = jnp.where(row < TH // 2, row + 1, row - 1)
    rows = flag_rows(keep, parity, row, row) + flag_rows(keep, parity, row, sibling)
    rows += [jnp.ones((1, HD), jnp.float32)] * (bias.shape[0] - len(rows))
    bias[...] = (jnp.concatenate(rows, axis=0) - 1.0) * -FILL
    rows = flag_rows(keep, parity, across, row)
    rows += [jnp.zeros((1, HD), jnp.float32)] * (FLAG_ROWS - len(rows))
    q_out[tokens:, :HD] = jnp.concatenate(rows, axis=0).astype(q_out.dtype)
    copy.wait()


def unit(h, q_ref, k_ref, flags, p_ref, st_ref, src):
    scale = LOG2E / math.sqrt(HD)
    cols = pl.ds(pl.multiple_of(h * HD, HD), HD)
    s = lax.dot_general(
        k_ref[:, cols], q_ref[: k_ref.shape[0], cols], (((1,), (1,)), ((), ())), preferred_element_type=jnp.float32
    )
    t = jnp.concatenate([s[w * TILE : (w + 1) * TILE] * scale + flags[w] for w in range(TW)], axis=0)
    m = jnp.max(t, axis=0, keepdims=True)
    e = jnp.exp2(t - m)
    p_ref[h, :, src * HD : (src + 1) * HD] = e.astype(jnp.bfloat16)
    st_ref[src, pl.ds(h, 1), :] = m
    st_ref[src, pl.ds(STAT + h, 1), :] = jnp.sum(e, axis=0, keepdims=True)


def all_heads(p_ref, units):
    def step(j, _):
        for i in range(HEADS_STEP):
            for args in units:
                unit(j * HEADS_STEP + i, *args)
        return 0

    lax.fori_loop(0, p_ref.shape[0] // HEADS_STEP, step, 0)


def bias_rows(bias, src, plane):
    at = (src * 3 + plane) * TW
    return [bias[at + w : at + w + 1, :] for w in range(TW)]


def own_scores_kernel(bias, k_hbm, v_hbm, q_own, q_d, p_d, st_d, k_own, v_a, v_b, sems):
    copies = [
        pltpu.make_async_copy(k_hbm, k_own, sems.at[0]),
        pltpu.make_async_copy(v_hbm.at[:, : v_a.shape[1]], v_a, sems.at[1]),
        pltpu.make_async_copy(v_hbm.at[:, v_a.shape[1] :], v_b, sems.at[2]),
    ]
    for copy in copies:
        copy.start()
    st_d[...] = jnp.ones_like(st_d)
    for copy in copies:
        copy.wait()
    all_heads(
        p_d,
        [
            (q_own, k_own, bias_rows(bias, 0, 0), p_d, st_d, 0),
            (q_d, k_own, bias_rows(bias, 1, 0), p_d, st_d, 1),
        ],
    )


def near_scores_kernel(bias, k_e, k_o, q_own, q_d, p_1, st_1, p_2, st_2):
    units = []
    for plane, k_ref, p_ref, st_ref in ((1, k_e, p_1, st_1), (2, k_o, p_2, st_2)):
        st_ref[...] = jnp.ones_like(st_ref)
        units += [(q, k_ref, bias_rows(bias, src, plane), p_ref, st_ref, src) for src, q in enumerate((q_own, q_d))]
    all_heads(p_1, units)


def far_scores_kernel(k_own, k_e, k_o, q_x, p_0, st_0, p_1, st_1, p_2, st_2):
    _, _, inner = place()

    @pl.when(inner)
    def _():
        tokens = k_own.shape[0]
        flags = [q_x[tokens + r : tokens + r + 1, :HD].astype(jnp.float32) for r in range(3 * TW)]
        units = []
        for plane, k_ref, p_ref, st_ref in ((0, k_own, p_0, st_0), (1, k_e, p_1, st_1), (2, k_o, p_2, st_2)):
            st_ref[...] = jnp.ones_like(st_ref)
            rows = [(f - 1.0) * -FILL for f in flags[plane * TW : (plane + 1) * TW]]
            units.append((q_x, k_ref, rows, p_ref, st_ref, 0))
        all_heads(p_0, units)


def merge(stats, src):
    peaks = [st[src, :STAT] for st in stats]
    sums = [st[src, STAT:] for st in stats]
    peak = functools.reduce(jnp.maximum, peaks)
    factors = [jnp.exp2(m - peak) for m in peaks]
    total = sum(f * v for f, v in zip(factors, sums))
    return peak, total, [f / total for f in factors]


def mix(heads, ps, vs, factors, outs):
    for n, h in enumerate(heads):
        cols = pl.ds(n * HD, HD)
        dots = [
            lax.dot_general(v[:, cols], p[h], (((0,), (0,)), ((), ())), preferred_element_type=jnp.float32)
            for p, v in zip(ps, vs)
        ]
        for src, out in enumerate(outs):
            part = [d[:, src * HD : (src + 1) * HD] * f[h : h + 1] for d, f in zip(dots, factors[src])]
            out[cols, :] = (part[0] + part[1] + part[2]).astype(out.dtype)


def put_split(o_ref, at, values, pieces):
    for _ in range(pieces):
        piece = values.astype(jnp.bfloat16)
        o_ref[at : at + STAT, :] = piece
        values = values - piece.astype(jnp.float32)
        at += STAT


def get_split(o_ref, at, pieces):
    return sum(o_ref[at + n * STAT : at + (n + 1) * STAT, :].astype(jnp.float32) for n in range(pieces))


def far_values_kernel(heads, p0, p1, p2, s0, s1, s2, v_own, v_e, v_o, o_x):
    _, _, inner = place()

    @pl.when(inner)
    def _():
        peak, total, factors = merge((s0, s1, s2), 0)
        mix(heads, (p0, p1, p2), (v_own, v_e, v_o), [factors], [o_x])
        if heads[0] == 0:
            put_split(o_x, len(heads) * HD, peak, 3)
        else:
            put_split(o_x, len(heads) * HD, total, 2)


def near_values_kernel(heads, p0, p1, p2, s0, s1, s2, v_own, v_e, v_o, o_own, o_d, *st_own):
    peak, total, own = merge((s0, s1, s2), 0)
    for ref in st_own:
        ref[:STAT] = peak
        ref[STAT:] = total
    peak, total, sib = merge((s0, s1, s2), 1)
    if heads[0] == 0:
        put_split(o_d, len(heads) * HD, peak, 3)
        put_split(o_d, (len(heads) * HD) + 3 * STAT, total, 2)
    mix(heads, (p0, p1, p2), (v_own, v_e, v_o), [own, sib], [o_own, o_d])


def combine_kernel(own_a, own_b, xa, xb, da, db, st_own, out):
    _, _, inner = place()

    wide_a, wide_b = own_a.shape[0], own_b.shape[0]
    m0, l0 = st_own[:STAT], st_own[STAT:]
    m1, l1 = get_split(da, wide_a, 3), get_split(da, wide_a + 3 * STAT, 2)
    m2, l2 = get_split(xa, wide_a, 3), get_split(xb, wide_b, 2)
    m2, l2 = jnp.where(inner, m2, FILL), jnp.where(inner, l2, 0.0)
    peak = jnp.maximum(jnp.maximum(m0, m1), m2)
    f0, f1, f2 = l0 * jnp.exp2(m0 - peak), l1 * jnp.exp2(m1 - peak), l2 * jnp.exp2(m2 - peak)
    total = f0 + f1 + f2
    w0, w1, w2 = f0 / total, f1 / total, f2 / total
    h = 0
    for o_own, o_x, o_d in ((own_a, xa, da), (own_b, xb, db)):
        for n in range(o_own.shape[0] // HD):
            cols = pl.ds(n * HD, HD)
            x = jnp.where(inner, o_x[cols, :].astype(jnp.float32), 0.0)
            o = o_own[cols, :] * w0[h : h + 1] + o_d[cols, :].astype(jnp.float32) * w1[h : h + 1] + x * w2[h : h + 1]
            out[:, pl.ds(h * HD, HD)] = o.T.astype(out.dtype)
            h += 1


def body(n_groups, query, key, value, keep):
    n_blk, n_uly = lax.axis_size("blk"), lax.axis_size("uly")
    rows, width = query.shape
    heads = width // HD
    first = heads * 2 // 3
    heads_a, heads_b = range(first), range(first, heads)
    wide_a, wide_b = first * HD, width - first * HD
    everyone = ("groups", "blk", "uly")
    cross = row_pairs(n_groups, n_blk, n_uly)
    cores = [(0, 1), (1, 0)]
    vmem = pl.BlockSpec(memory_space=pltpu.VMEM)
    hbm = pl.BlockSpec(memory_space=pltpu.HBM)
    bf16, f32 = jnp.bfloat16, jnp.float32

    def exchange(x, parity):
        return lax.ppermute(x, ("blk", "uly"), plane_pairs(n_blk, n_uly, parity))

    def call(kernel, name, us, in_specs, out_shape, scratch=()):
        return pl.pallas_call(
            kernel,
            in_specs=in_specs,
            out_specs=jax.tree.map(lambda _: vmem, out_shape),
            out_shape=out_shape,
            scratch_shapes=scratch,
            compiler_params=pltpu.CompilerParams(vmem_limit_bytes=16 * 1024 * 1024),
            cost_estimate=pl.CostEstimate(flops=int(us * 1e9), bytes_accessed=0, transcendentals=0),
            name=name,
        )

    def array(dtype, *shape):
        return jax.ShapeDtypeStruct(shape, dtype)

    p_near, s_near = array(bf16, heads, rows, 2 * rows), array(f32, 2, 2 * STAT, rows)
    p_far, s_far = array(bf16, heads, rows, rows), array(f32, 1, 2 * STAT, rows)
    far_a, far_b = array(bf16, wide_a + 3 * STAT, rows), array(bf16, wide_b + 2 * STAT, rows)
    near_a, near_b = array(bf16, wide_a + 5 * STAT, rows), array(bf16, wide_b, rows)

    k_e = exchange(key, 0)
    k_o = exchange(key, 1)
    q_d = lax.ppermute(query, "uly", cores)
    q_late, _ = lax.optimization_barrier((query, q_d))
    near, q_own = call(
        prepare_kernel,
        "prepare",
        0.7,
        [hbm, hbm],
        [array(f32, 16, HD), array(bf16, rows + FLAG_ROWS, width)],
        [pltpu.SMEM(keep.shape, keep.dtype), pltpu.SemaphoreType.DMA((2,))],
    )(keep, q_late)
    q_x = lax.ppermute(q_own, everyone, cross)

    pd0, sd0, k_own, v_a, v_b = call(
        own_scores_kernel,
        "own_scores",
        1.5,
        [vmem, hbm, hbm, vmem, vmem],
        [p_near, s_near, array(bf16, rows, width), array(bf16, rows, wide_a), array(bf16, rows, wide_b)],
        [pltpu.SemaphoreType.DMA((3,))],
    )(near, key, value, q_own, q_d)

    va_e = exchange(v_a, 0)
    va_o = exchange(v_a, 1)
    v_last, k_e, k_o, _ = lax.optimization_barrier((v_b, k_e, k_o, sd0))
    vb_e = exchange(v_last, 0)
    vb_o = exchange(v_last, 1)

    pd1, sd1, pd2, sd2 = call(near_scores_kernel, "near_scores", 2, [vmem] * 5, [p_near, s_near] * 2)(
        near, k_e, k_o, q_own, q_d
    )
    q_x, _ = lax.optimization_barrier((q_x, sd2))
    px0, sx0, px1, sx1, px2, sx2 = call(far_scores_kernel, "far_scores", 0, [vmem] * 4, [p_far, s_far] * 3)(
        k_own, k_e, k_o, q_x
    )
    va_e, va_o, _ = lax.optimization_barrier((va_e, va_o, sx2))
    far = px0, px1, px2, sx0, sx1, sx2
    nigh = pd0, pd1, pd2, sd0, sd1, sd2

    xa = call(functools.partial(far_values_kernel, heads_a), "far_values_a", 2, [vmem] * 9, far_a)(
        *far, v_a, va_e, va_o
    )
    back_xa = lax.ppermute(xa, everyone, cross)
    va_e, va_o, _ = lax.optimization_barrier((va_e, va_o, xa))
    own_a, da, s_own = call(
        functools.partial(near_values_kernel, heads_a),
        "near_values_a",
        2,
        [vmem] * 9,
        [array(f32, wide_a, rows), near_a, array(f32, 2 * STAT, rows)],
    )(*nigh, v_a, va_e, va_o)
    back_da = lax.ppermute(da, "uly", cores)

    vb_e, vb_o, _, _ = lax.optimization_barrier((vb_e, vb_o, s_own, xa))
    xb = call(functools.partial(far_values_kernel, heads_b), "far_values_b", 5, [vmem] * 9, far_b)(
        *far, v_b, vb_e, vb_o
    )
    back_xb = lax.ppermute(xb, everyone, cross)
    own_b, db = call(
        functools.partial(near_values_kernel, heads_b), "near_values_b", 5, [vmem] * 9, [array(f32, wide_b, rows), near_b]
    )(*nigh, v_b, vb_e, vb_o)
    back_db = lax.ppermute(db, "uly", cores)

    return call(combine_kernel, "combine", 0, [vmem] * 7, array(query.dtype, rows, width))(
        own_a, own_b, back_xa, back_xb, back_da, back_db, s_own
    )


def solution(mesh):
    tokens = P(("groups", "blk", "uly"), None)
    return jax.shard_map(
        functools.partial(body, mesh.shape["groups"]),
        mesh=mesh,
        in_specs=(tokens, tokens, tokens, P(("groups", "blk"), None)),
        out_specs=tokens,
        check_vma=False,
    )
```

time: 111 us -> 29.7 us (0.27)
  the two profiles are of different devices: /device:TPU:9 before, /device:TPU:1 now
where the time goes in v2:
time: 29.7 us; the launch traced here: 29.6 us
  starting transfers between devices  14.2 us (48%)
  Pallas kernels  9.58 us (32%)
  waiting for transfers between devices  4.01 us (14%)
  local copies, waits for them, and re-layouts  1.68 us (6%)
    ppermute x6, starting transfers between devices, exchange(): return lax.ppermute(x, ('blk', 'uly'), plane_pairs(n_blk, n_uly, parity))  10.2 us
    ppermute x1, waiting for transfers between devices, body(): back_xb = lax.ppermute(xb, everyone, cross)  2.68 us
    pallas_call x1, Pallas kernels, body(): call(near_scores_kernel, 'near_scores', 2, [vmem] * 5, [p_near, s_near] * 2)  2.25 us
    pallas_call x1, Pallas kernels, body(): call(far_scores_kernel, 'far_scores', 0, [vmem] * 4, [p_far, s_far] * 3)  1.89 us
    pallas_call x1, Pallas kernels, body(): call(own_scores_kernel, 'own_scores', 1.5, [vmem, hbm, hbm, vmem, vmem],...  1.85 us
    unnamed x8, local copies, waits for them, and re-layouts  1.68 us
    ppermute x1, starting transfers between devices, body(): q_x = lax.ppermute(q_own, everyone, cross)  1.51 us
    ppermute x1, starting transfers between devices, body(): back_xa = lax.ppermute(xa, everyone, cross)  1.15 us
  transfers between devices with their start and end apart: 12, of which 3 were waited for; matrix products, arithmetic and copies ran while one was open for 0% of the time, Pallas kernels for 29%

profile of v2, /device:TPU:1, one launch (start us, length us, event | category | flops | bytes accessed | tf_op | source)
XLA Modules:
  0.0 29.6 jit_solution(5210436225524012694)
XLA Ops:
  0.0 0.1 collective-permute-start
  0.1 2.7 %collective-permute-start.1 = (bf16[128,1536]{1,0:T(8,128)(2,1)}, bf16[128,1536]{1,0:T(8,128)(2,1)S(1)}, u32[]{:S(2)}, u32[]{:S(2)}) collective-permute-start(bf16[128,1536]{1,0:T(8,128)(2,1)} %k_hbm.1), channel_id=1, source_target_pairs={{0,4},{1,5},{2,6},{3,7},{4,0},{5,1},{6,2},{7,3},{8,12},{9,13},{10,... | collective-permute-start | bytes 1179656 | tf_op jit(solution)/shard_map/ppermute | solution.py:263
  2.8 0.3 collective-permute-start.2
  3.1 0.0 collective-permute-done.q_d
  3.1 0.0 copy-start
  3.1 1.0 %copy-done = bf16[128,1536]{1,0:T(8,128)(2,1)S(1)} copy-done((bf16[128,1536]{1,0:T(8,128)(2,1)S(1)}, bf16[128,1536]{1,0:T(8,128)(2,1)}, u32[]{:S(2)}) %copy-start) | copy-done | bytes 393240
  4.1 0.0 copy-start.3
  4.1 0.7 %copy-done.3 = s32[4,28]{1,0:T(4,128)S(1)} copy-done((s32[4,28]{1,0:T(4,128)S(1)}, s32[4,28]{1,0:T(4,128)}, u32[]{:S(2)}) %copy-start.3) | copy-done | bytes 472
  4.8 0.0 copy-start.1
  4.8 0.0 copy-start.2
  4.8 0.7 %prepare.1 = (f32[16,128]{1,0:T(8,128)S(1)}, bf16[144,1536]{1,0:T(8,128)(2,1)S(1)}) custom-call(s32[4,28]{1,0:T(4,128)S(1)} %copy-done.3, bf16[128,1536]{1,0:T(8,128)(2,1)S(1)} %copy-done), custom_call_target="tpu_custom_call" | custom-call | flops 700000000 | tf_op jit(solution)/shard_map/prepare/pallas_call | solution.py:289
  5.5 1.5 %collective-permute-start.5 = (bf16[144,1536]{1,0:T(8,128)(2,1)S(1)}, bf16[144,1536]{1,0:T(8,128)(2,1)S(1)}, u32[]{:S(2)}, u32[]{:S(2)}) collective-permute-start(bf16[144,1536]{1,0:T(8,128)(2,1)S(1)} %get-tuple-element.40.q_own), channel_id=1, source_target_pairs={{0,16},{1,2},{2,1},{3,19},{4,20},{5,6},{6,5},{7,23},{8,24},{9,10},... | collective-permute-start | bytes 1327112 | tf_op jit(solution)/shard_map/ppermute | solution.py:297
  7.0 0.0 copy-done.1
  7.0 0.0 copy-done.2
  7.0 1.8 %own_scores.1 = (bf16[12,128,256]{2,1,0:T(8,128)(2,1)S(1)}, f32[2,32,128]{2,1,0:T(8,128)S(1)}, bf16[128,1536]{1,0:T(8,128)(2,1)S(1)}, bf16[128,1024]{1,0:T(8,128)(2,1)S(1)}, bf16[128,512]{1,0:T(8,128)(2,1)S(1)}) custom-call(f32[16,128]{1,0:T(8,128)S(1)} %get-tuple-element.39.bias, bf16[128,1536]{1,0:T(8,128)(2,1)S(1)} %copy-done.2, ...), custom_call_target="tpu_custom_call" | custom-call | flops 1500000000 | tf_op jit(solution)/shard_map/own_scores/pallas_call | solution.py:299
  8.9 2.6 %collective-permute-start.3 = (bf16[128,1024]{1,0:T(8,128)(2,1)S(1)}, bf16[128,1024]{1,0:T(8,128)(2,1)S(1)}, u32[]{:S(2)}, u32[]{:S(2)}) collective-permute-start(bf16[128,1024]{1,0:T(8,128)(2,1)S(1)} %get-tuple-element.50.v_own), channel_id=1, source_target_pairs={{0,4},{1,5},{2,6},{3,7},{4,0},{5,1},{6,2},{7,3},{8,12},{9,13},{10,... | collective-permute-start | bytes 786440 | tf_op jit(solution)/shard_map/ppermute | solution.py:263
  11.5 0.7 %collective-permute-start.4 = (bf16[128,1024]{1,0:T(8,128)(2,1)S(1)}, bf16[128,1024]{1,0:T(8,128)(2,1)S(1)}, u32[]{:S(2)}, u32[]{:S(2)}) collective-permute-start(bf16[128,1024]{1,0:T(8,128)(2,1)S(1)} %get-tuple-element.50.v_own), channel_id=1, source_target_pairs={{0,1},{1,0},{2,3},{3,2},{4,8},{5,9},{6,10},{7,11},{8,4},{9,5},{10,... | collective-permute-start | bytes 786440 | tf_op jit(solution)/shard_map/ppermute | solution.py:263
  12.2 0.3 %collective-permute-done.1.k_e = bf16[128,1536]{1,0:T(8,128)(2,1)S(1)} collective-permute-done((bf16[128,1536]{1,0:T(8,128)(2,1)}, bf16[128,1536]{1,0:T(8,128)(2,1)S(1)}, u32[]{:S(2)}, u32[]{:S(2)}) %collective-permute-start.1) | collective-permute-done | bytes 393248 | tf_op jit(solution)/shard_map/ppermute | solution.py:263
  12.5 0.0 collective-permute-done.2.k_o
  12.5 2.4 %collective-permute-start.6 = (bf16[128,512]{1,0:T(8,128)(2,1)S(1)}, bf16[128,512]{1,0:T(8,128)(2,1)S(1)}, u32[]{:S(2)}, u32[]{:S(2)}) collective-permute-start(bf16[128,512]{1,0:T(8,128)(2,1)S(1)} %get-tuple-element.64.v_own), channel_id=1, source_target_pairs={{0,4},{1,5},{2,6},{3,7},{4,0},{5,1},{6,2},{7,3},{8,12},{9,13},{10,... | collective-permute-start | bytes 393224 | tf_op jit(solution)/shard_map/ppermute | solution.py:263
  14.9 1.4 %collective-permute-start.7 = (bf16[128,512]{1,0:T(8,128)(2,1)S(1)}, bf16[128,512]{1,0:T(8,128)(2,1)S(1)}, u32[]{:S(2)}, u32[]{:S(2)}) collective-permute-start(bf16[128,512]{1,0:T(8,128)(2,1)S(1)} %get-tuple-element.64.v_own), channel_id=1, source_target_pairs={{0,1},{1,0},{2,3},{3,2},{4,8},{5,9},{6,10},{7,11},{8,4},{9,5},{10,... | collective-permute-start | bytes 393224 | tf_op jit(solution)/shard_map/ppermute | solution.py:263
  16.4 2.3 %near_scores.1 = (bf16[12,128,256]{2,1,0:T(8,128)(2,1)S(1)}, f32[2,32,128]{2,1,0:T(8,128)S(1)}, bf16[12,128,256]{2,1,0:T(8,128)(2,1)S(1)}, f32[2,32,128]{2,1,0:T(8,128)S(1)}) custom-call(f32[16,128]{1,0:T(8,128)S(1)} %get-tuple-element.39.bias, bf16[128,1536]{1,0:T(8,128)(2,1)S(1)} %collective-permute-done.1.k_e, ...), custom_call_target="tpu_custom_call" | custom-call | flops 2000000000 | tf_op jit(solution)/shard_map/near_scores/pallas_call | solution.py:314
  18.6 0.0 collective-permute-done.5.q_x
  18.6 1.9 %far_scores.1 = (bf16[12,128,128]{2,1,0:T(8,128)(2,1)S(1)}, f32[1,32,128]{2,1,0:T(8,128)S(1)}, bf16[12,128,128]{2,1,0:T(8,128)(2,1)S(1)}, f32[1,32,128]{2,1,0:T(...) custom-call(bf16[128,1536]{1,0:T(8,128)(2,1)S(1)} %get-tuple-element.51.k_own, ...), custom_call_target="tpu_custom_call" | custom-call | tf_op jit(solution)/shard_map/far_scores/pallas_call | solution.py:318
  20.5 0.0 collective-permute-done.3.v_e
  20.5 0.0 collective-permute-done.4.v_o
  20.6 0.4 %far_values_a.1 = bf16[1072,128]{1,0:T(8,128)(2,1)S(1)} custom-call(bf16[12,128,128]{2,1,0:T(8,128)(2,1)S(1)} %get-tuple-element.56.p0, bf16[12,128,128]{2,1,0:T(8,128)(2,1)S(1)} %get-tuple-element.57.p1, bf16[12,128,128]{2,1,0:T(8,128)(2,1)S(1)} %get-tuple-element.58.p2, f32[1,32,128]{2,1,0:T(8,128)S(1)} %get-tuple-element.59.s0, ...), custom_call_target="tpu_custom_call" | custom-call | flops 2000000000 | tf_op jit(solution)/shard_map/far_values_a/pallas_call | solution.py:325
  21.0 1.2 %collective-permute-start.8 = (bf16[1072,128]{1,0:T(8,128)(2,1)S(1)}, bf16[1072,128]{1,0:T(8,128)(2,1)S(1)}, u32[]{:S(2)}, u32[]{:S(2)}) collective-permute-start(bf16[1072,128]{1,0:T(8,128)(2,1)S(1)} %far_values_a.1), channel_id=1, source_target_pairs={{0,16},{1,2},{2,1},{3,19},{4,20},{5,6},{6,5},{7,23},{8,24},{9,10},... | collective-permute-start | bytes 823304 | tf_op jit(solution)/shard_map/ppermute | solution.py:328
  22.1 0.6 %near_values_a.1 = (f32[1024,128]{1,0:T(8,128)S(1)}, bf16[1104,128]{1,0:T(8,128)(2,1)S(1)}, f32[32,128]{1,0:T(8,128)S(1)}) custom-call(bf16[12,128,256]{2,1,0:T(8,128)(2,1)S(1)} %get-tuple-element.41.p0, bf16[12,128,256]{2,1,0:T(8,128)(2,1)S(1)} %get-tuple-element.46.p1, bf16[12,128,256]{2,1,0:T(8,128)(2,1)S(1)} %get-tuple-element.47.p2, ...), custom_call_target="tpu_custom_call" | custom-call | flops 2000000000 | tf_op jit(solution)/shard_map/near_values_a/pallas_call | solution.py:330
  22.8 0.0 collective-permute-done.6.v_e
  22.8 0.0 collective-permute-done.7.v_o
  22.8 0.3 %far_values_b.1 = bf16[544,128]{1,0:T(8,128)(2,1)S(1)} custom-call(bf16[12,128,128]{2,1,0:T(8,128)(2,1)S(1)} %get-tuple-element.56.p0, bf16[12,128,128]{2,1,0:T(8,128)(2,1)S(1)} %get-tuple-element.57.p1, bf16[12,128,128]{2,1,0:T(8,128)(2,1)S(1)} %get-tuple-element.58.p2, f32[1,32,128]{2,1,0:T(8,128)S(1)} %get-tuple-element.59.s0, ...), custom_call_target="tpu_custom_call" | custom-call | flops 5000000000 | tf_op jit(solution)/shard_map/far_values_b/pallas_call | solution.py:340
  23.1 0.7 %collective-permute-start.9 = (bf16[544,128]{1,0:T(8,128)(2,1)S(1)}, bf16[544,128]{1,0:T(8,128)(2,1)S(1)}, u32[]{:S(2)}, u32[]{:S(2)}) collective-permute-start(bf16[544,128]{1,0:T(8,128)(2,1)S(1)} %far_values_b.1), channel_id=1, source_target_pairs={{0,16},{1,2},{2,1},{3,19},{4,20},{5,6},{6,5},{7,23},{8,24},{9,10},... | collective-permute-start | bytes 417800 | tf_op jit(solution)/shard_map/ppermute | solution.py:343
  23.8 0.0 collective-permute-start.10
  23.8 0.4 %near_values_b.1 = (f32[512,128]{1,0:T(8,128)S(1)}, bf16[512,128]{1,0:T(8,128)(2,1)S(1)}) custom-call(bf16[12,128,256]{2,1,0:T(8,128)(2,1)S(1)} %get-tuple-element.41.p0, bf16[12,128,256]{2,1,0:T(8,128)(2,1)S(1)} %get-tuple-element.46.p1, bf16[12,128,256]{2,1,0:T(8,128)(2,1)S(1)} %get-tuple-element.47.p2, f32[2,32,128]{2,1,0:T(8,128)S(1)} %get-tuple-element.43.s0, ...), custom_call_target="tpu_custom_call" | custom-call | flops 5000000000 | tf_op jit(solution)/shard_map/near_values_b/pallas_call | solution.py:344
  24.2 0.6 %collective-permute-start.11 = (bf16[512,128]{1,0:T(8,128)(2,1)S(1)}, bf16[512,128]{1,0:T(8,128)(2,1)S(1)}, u32[]{:S(2)}, u32[]{:S(2)}) collective-permute-start(bf16[512,128]{1,0:T(8,128)(2,1)S(1)} %get-tuple-element.70), channel_id=1, source_target_pairs={{0,1},{1,0},{2,3},{3,2},{4,5},{5,4},{6,7},{7,6},{8,9},{9,8},{10,11... | collective-permute-start | bytes 393224 | tf_op jit(solution)/shard_map/ppermute | solution.py:347
  24.8 1.0 %collective-permute-done.11.db = bf16[512,128]{1,0:T(8,128)(2,1)S(1)} collective-permute-done((bf16[512,128]{1,0:T(8,128)(2,1)S(1)}, bf16[512,128]{1,0:T(8,128)(2,1)S(1)}, u32[]{:S(2)}, u32[]{:S(2)}) %collective-permute-start.11) | collective-permute-done | bytes 131104 | tf_op jit(solution)/shard_map/ppermute | solution.py:347
  25.8 2.7 %collective-permute-done.9.xb = bf16[544,128]{1,0:T(8,128)(2,1)S(1)} collective-permute-done((bf16[544,128]{1,0:T(8,128)(2,1)S(1)}, bf16[544,128]{1,0:T(8,128)(2,1)S(1)}, u32[]{:S(2)}, u32[]{:S(2)}) %collective-permute-start.9) | collective-permute-done | bytes 139296 | tf_op jit(solution)/shard_map/ppermute | solution.py:343
  28.5 0.0 collective-permute-done.8.xa
  28.5 0.0 collective-permute-done.10.da
  28.5 1.1 %combine.1 = bf16[128,1536]{1,0:T(8,128)(2,1)} custom-call(f32[1024,128]{1,0:T(8,128)S(1)} %get-tuple-element.63.own_a, f32[512,128]{1,0:T(8,128)S(1)} %get-tuple-element.68.own_b, bf16[1072,128]{1,0:T(8,128)(2,1)S(1)} %collective-permute-done.8.xa, bf16[544,128]{1,0:T(8,128)(2,1)S(1)} %collective-permute-done.9.xb, ...), custom_call_target="tpu_custom_call" | custom-call | tf_op jit(solution)/shard_map/combine/pallas_call | solution.py:349
Async XLA Ops:
  0.0 3.1 %collective-permute-start = (bf16[128,1536]{1,0:T(8,128)(2,1)}, bf16[128,1536]{1,0:T(8,128)(2,1)S(1)}, u32[]{:S(2)}, u32[]{:S(2)}) collective-permute-start(bf16[128,1536]{1,0:T(8,128)(2,1)} %q_hbm), channel_id=1, source_target_pairs={{0,1},{1,0},{2,3},{3,2},{4,5},{5,4},{6,7},{7,6},{8,9},{9,8},{10,11... | collective-permute-start | bytes 1179656 | tf_op jit(solution)/shard_map/ppermute | solution.py:287
  0.1 12.4 %collective-permute-start.1 = (bf16[128,1536]{1,0:T(8,128)(2,1)}, bf16[128,1536]{1,0:T(8,128)(2,1)S(1)}, u32[]{:S(2)}, u32[]{:S(2)}) collective-permute-start(bf16[128,1536]{1,0:T(8,128)(2,1)} %k_hbm.1), channel_id=1, source_target_pairs={{0,4},{1,5},{2,6},{3,7},{4,0},{5,1},{6,2},{7,3},{8,12},{9,13},{10,... | collective-permute-start | bytes 1179656 | tf_op jit(solution)/shard_map/ppermute | solution.py:263
  2.8 9.7 %collective-permute-start.2 = (bf16[128,1536]{1,0:T(8,128)(2,1)}, bf16[128,1536]{1,0:T(8,128)(2,1)S(1)}, u32[]{:S(2)}, u32[]{:S(2)}) collective-permute-start(bf16[128,1536]{1,0:T(8,128)(2,1)} %k_hbm.1), channel_id=1, source_target_pairs={{0,1},{1,0},{2,3},{3,2},{4,8},{5,9},{6,10},{7,11},{8,4},{9,5},{10,... | collective-permute-start | bytes 1179656 | tf_op jit(solution)/shard_map/ppermute | solution.py:263
  3.1 1.0 %copy-start = (bf16[128,1536]{1,0:T(8,128)(2,1)S(1)}, bf16[128,1536]{1,0:T(8,128)(2,1)}, u32[]{:S(2)}) copy-start(bf16[128,1536]{1,0:T(8,128)(2,1)} %q_hbm) | copy-start | bytes 1179652
  4.1 0.7 %copy-start.3 = (s32[4,28]{1,0:T(4,128)S(1)}, s32[4,28]{1,0:T(4,128)}, u32[]{:S(2)}) copy-start(s32[4,28]{1,0:T(4,128)} %keep_hbm.1) | copy-start | bytes 1348
  4.8 2.3 %copy-start.1 = (bf16[128,1536]{1,0:T(8,128)(2,1)S(1)}, bf16[128,1536]{1,0:T(8,128)(2,1)}, u32[]{:S(2)}) copy-start(bf16[128,1536]{1,0:T(8,128)(2,1)} %v_hbm.1) | copy-start | bytes 1179652
  4.8 2.3 %copy-start.2 = (bf16[128,1536]{1,0:T(8,128)(2,1)S(1)}, bf16[128,1536]{1,0:T(8,128)(2,1)}, u32[]{:S(2)}) copy-start(bf16[128,1536]{1,0:T(8,128)(2,1)} %k_hbm.1) | copy-start | bytes 1179652
  5.5 13.1 %collective-permute-start.5 = (bf16[144,1536]{1,0:T(8,128)(2,1)S(1)}, bf16[144,1536]{1,0:T(8,128)(2,1)S(1)}, u32[]{:S(2)}, u32[]{:S(2)}) collective-permute-start(bf16[144,1536]{1,0:T(8,128)(2,1)S(1)} %get-tuple-element.40.q_own), channel_id=1, source_target_pairs={{0,16},{1,2},{2,1},{3,19},{4,20},{5,6},{6,5},{7,23},{8,24},{9,10},... | collective-permute-start | bytes 1327112 | tf_op jit(solution)/shard_map/ppermute | solution.py:297
  8.9 11.7 %collective-permute-start.3 = (bf16[128,1024]{1,0:T(8,128)(2,1)S(1)}, bf16[128,1024]{1,0:T(8,128)(2,1)S(1)}, u32[]{:S(2)}, u32[]{:S(2)}) collective-permute-start(bf16[128,1024]{1,0:T(8,128)(2,1)S(1)} %get-tuple-element.50.v_own), channel_id=1, source_target_pairs={{0,4},{1,5},{2,6},{3,7},{4,0},{5,1},{6,2},{7,3},{8,12},{9,13},{10,... | collective-permute-start | bytes 786440 | tf_op jit(solution)/shard_map/ppermute | solution.py:263
  11.5 9.1 %collective-permute-start.4 = (bf16[128,1024]{1,0:T(8,128)(2,1)S(1)}, bf16[128,1024]{1,0:T(8,128)(2,1)S(1)}, u32[]{:S(2)}, u32[]{:S(2)}) collective-permute-start(bf16[128,1024]{1,0:T(8,128)(2,1)S(1)} %get-tuple-element.50.v_own), channel_id=1, source_target_pairs={{0,1},{1,0},{2,3},{3,2},{4,8},{5,9},{6,10},{7,11},{8,4},{9,5},{10,... | collective-permute-start | bytes 786440 | tf_op jit(solution)/shard_map/ppermute | solution.py:263
  12.5 10.3 %collective-permute-start.6 = (bf16[128,512]{1,0:T(8,128)(2,1)S(1)}, bf16[128,512]{1,0:T(8,128)(2,1)S(1)}, u32[]{:S(2)}, u32[]{:S(2)}) collective-permute-start(bf16[128,512]{1,0:T(8,128)(2,1)S(1)} %get-tuple-element.64.v_own), channel_id=1, source_target_pairs={{0,4},{1,5},{2,6},{3,7},{4,0},{5,1},{6,2},{7,3},{8,12},{9,13},{10,... | collective-permute-start | bytes 393224 | tf_op jit(solution)/shard_map/ppermute | solution.py:263
  14.9 7.9 %collective-permute-start.7 = (bf16[128,512]{1,0:T(8,128)(2,1)S(1)}, bf16[128,512]{1,0:T(8,128)(2,1)S(1)}, u32[]{:S(2)}, u32[]{:S(2)}) collective-permute-start(bf16[128,512]{1,0:T(8,128)(2,1)S(1)} %get-tuple-element.64.v_own), channel_id=1, source_target_pairs={{0,1},{1,0},{2,3},{3,2},{4,8},{5,9},{6,10},{7,11},{8,4},{9,5},{10,... | collective-permute-start | bytes 393224 | tf_op jit(solution)/shard_map/ppermute | solution.py:263
  21.0 7.5 %collective-permute-start.8 = (bf16[1072,128]{1,0:T(8,128)(2,1)S(1)}, bf16[1072,128]{1,0:T(8,128)(2,1)S(1)}, u32[]{:S(2)}, u32[]{:S(2)}) collective-permute-start(bf16[1072,128]{1,0:T(8,128)(2,1)S(1)} %far_values_a.1), channel_id=1, source_target_pairs={{0,16},{1,2},{2,1},{3,19},{4,20},{5,6},{6,5},{7,23},{8,24},{9,10},... | collective-permute-start | bytes 823304 | tf_op jit(solution)/shard_map/ppermute | solution.py:328
  23.1 5.4 %collective-permute-start.9 = (bf16[544,128]{1,0:T(8,128)(2,1)S(1)}, bf16[544,128]{1,0:T(8,128)(2,1)S(1)}, u32[]{:S(2)}, u32[]{:S(2)}) collective-permute-start(bf16[544,128]{1,0:T(8,128)(2,1)S(1)} %far_values_b.1), channel_id=1, source_target_pairs={{0,16},{1,2},{2,1},{3,19},{4,20},{5,6},{6,5},{7,23},{8,24},{9,10},... | collective-permute-start | bytes 417800 | tf_op jit(solution)/shard_map/ppermute | solution.py:343
  23.8 4.7 %collective-permute-start.10 = (bf16[1104,128]{1,0:T(8,128)(2,1)S(1)}, bf16[1104,128]{1,0:T(8,128)(2,1)S(1)}, u32[]{:S(2)}, u32[]{:S(2)}) collective-permute-start(bf16[1104,128]{1,0:T(8,128)(2,1)S(1)} %get-tuple-element.69), channel_id=1, source_target_pairs={{0,1},{1,0},{2,3},{3,2},{4,5},{5,4},{6,7},{7,6},{8,9},{9,8},{10,11... | collective-permute-start | bytes 847880 | tf_op jit(solution)/shard_map/ppermute | solution.py:337
  24.2 1.6 %collective-permute-start.11 = (bf16[512,128]{1,0:T(8,128)(2,1)S(1)}, bf16[512,128]{1,0:T(8,128)(2,1)S(1)}, u32[]{:S(2)}, u32[]{:S(2)}) collective-permute-start(bf16[512,128]{1,0:T(8,128)(2,1)S(1)} %get-tuple-element.70), channel_id=1, source_target_pairs={{0,1},{1,0},{2,3},{3,2},{4,5},{5,4},{6,7},{7,6},{8,9},{9,8},{10,11... | collective-permute-start | bytes 393224 | tf_op jit(solution)/shard_map/ppermute | solution.py:347

commit v3 on v2

v3 whole, which is shorter than its diff:
```python
import functools
import math

import jax
import jax.numpy as jnp
from jax import lax
from jax.experimental import pallas as pl
from jax.experimental.pallas import tpu as pltpu
from jax.sharding import PartitionSpec as P

HD = 128
TILE = 64
TH = 4
TW = 2
STAT = 16
FLAG_ROWS = 16
FILL = -1e30
LOG2E = 1.4426950408889634


def plane_pairs(n_blk, n_uly, parity):
    blks = TH // n_uly
    route = []
    for blk in range(n_blk):
        t = blk // blks
        other = t + 1 if t % 2 == parity else t - 1
        for u in range(n_uly):
            there = blk, n_uly - 1 - u
            if 0 <= other < n_blk // blks:
                there = other * blks + blk % blks, u
            route.append((blk * n_uly + u, there[0] * n_uly + there[1]))
    return route


def row_pairs(n_groups, n_blk, n_uly):
    route = []
    size = n_blk * n_uly
    for g in range(n_groups):
        for i in range(size):
            h = i % TH
            if h == 1:
                there = g * size + i + 1
            elif h == 2:
                there = g * size + i - 1
            else:
                there = (g + 1) % n_groups * size + i
            route.append((g * size + i, there))
    return route


def place():
    n_uly = lax.axis_size("uly")
    rows = TH // n_uly
    blk = lax.axis_index("blk")
    row = lax.rem(blk, rows) * n_uly + lax.axis_index("uly")
    return lax.rem(lax.div(blk, rows), 2), row, (row > 0) & (row < TH - 1)


def flag_rows(keep, parity, key_row, query_row):
    first = lax.broadcasted_iota(jnp.int32, (1, HD), 1) < TILE
    tiles = keep.shape[0]
    line = lax.rem(query_row * TW, tiles)
    base = (keep.shape[1] - tiles) // 2
    step = 1 - 2 * parity
    rows = []
    for dt in (0, step, -step):
        column = base + TH * TW * dt + TW * (key_row - query_row) + line
        for w in range(TW):
            col = jnp.clip(column + w, 0, keep.shape[1] - 1)
            low = (keep[line, col] > 0).astype(jnp.float32)
            high = (keep[line + 1, col] > 0).astype(jnp.float32)
            rows.append(jnp.where(first, low, high))
    return rows


def prepare_kernel(keep_hbm, q_hbm, bias, q_out, keep, sems):
    tokens = q_hbm.shape[0]
    flags = pltpu.make_async_copy(keep_hbm, keep, sems.at[0])
    flags.start()
    copy = pltpu.make_async_copy(q_hbm, q_out.at[:tokens], sems.at[1])
    copy.start()
    flags.wait()
    parity, row, _ = place()
    sibling = row + 1 - 2 * lax.rem(row, 2)
    across = jnp.where(row < TH // 2, row + 1, row - 1)
    rows = flag_rows(keep, parity, row, row) + flag_rows(keep, parity, row, sibling)
    rows += [jnp.ones((1, HD), jnp.float32)] * (bias.shape[0] - len(rows))
    bias[...] = (jnp.concatenate(rows, axis=0) - 1.0) * -FILL
    rows = flag_rows(keep, parity, across, row)
    rows += [jnp.zeros((1, HD), jnp.float32)] * (FLAG_ROWS - len(rows))
    q_out[tokens:, :HD] = jnp.concatenate(rows, axis=0).astype(q_out.dtype)
    copy.wait()


def unit(h, q, keys, flags, p_ref, st_ref, src):
    scale = LOG2E / math.sqrt(HD)
    s = lax.dot_general(keys, q, (((1,), (1,)), ((), ())), preferred_element_type=jnp.float32)
    t = jnp.concatenate([s[n * TILE : (n + 1) * TILE] * scale + flag for n, flag in enumerate(flags)], axis=0)
    m = jnp.max(t, axis=0, keepdims=True)
    e = jnp.exp2(t - m)
    p_ref[h, :, src * HD : (src + 1) * HD] = e.astype(jnp.bfloat16)
    st_ref[src, h : h + 1, :] = m
    st_ref[src, STAT + h : STAT + h + 1, :] = jnp.sum(e, axis=0, keepdims=True)


def all_heads(qs, ks, flags, p_ref, st_ref):
    rows = ks[0].shape[0]
    st_ref[...] = jnp.ones_like(st_ref)
    for h in range(p_ref.shape[0]):
        cols = pl.ds(h * HD, HD)
        keys = jnp.concatenate([k[:, cols] for k in ks], axis=0)
        for src, q in enumerate(qs):
            unit(h, q[:rows, cols], keys, flags[src], p_ref, st_ref, src)


def bias_rows(bias, src, planes):
    return [bias[(src * 3 + n) * TW + w : (src * 3 + n) * TW + w + 1, :] for n in planes for w in range(TW)]


def own_scores_kernel(bias, k_hbm, v_hbm, q_own, q_d, p, st, k_own, v_a, v_b, sems):
    copies = [
        pltpu.make_async_copy(k_hbm, k_own, sems.at[0]),
        pltpu.make_async_copy(v_hbm.at[:, : v_a.shape[1]], v_a, sems.at[1]),
        pltpu.make_async_copy(v_hbm.at[:, v_a.shape[1] :], v_b, sems.at[2]),
    ]
    for copy in copies:
        copy.start()
    for copy in copies:
        copy.wait()
    all_heads((q_own, q_d), (k_own,), [bias_rows(bias, src, (0,)) for src in range(2)], p, st)


def near_scores_kernel(bias, k_e, k_o, q_own, q_d, p, st):
    all_heads((q_own, q_d), (k_e, k_o), [bias_rows(bias, src, (1, 2)) for src in range(2)], p, st)


def far_scores_kernel(k_own, k_e, k_o, q_x, p, st):
    _, _, inner = place()

    @pl.when(inner)
    def _():
        tokens = k_own.shape[0]
        flags = (q_x[tokens:, :HD].astype(jnp.float32) - 1.0) * -FILL
        all_heads((q_x,), (k_own, k_e, k_o), [[flags[n : n + 1] for n in range(3 * TW)]], p, st)


def split(values, pieces):
    out = []
    for _ in range(pieces):
        piece = values.astype(jnp.bfloat16).astype(jnp.float32)
        out.append(piece)
        values = values - piece
    return out


def stat_rows(heads):
    return -(-5 * heads // 16) * 16


def put_stats(o_ref, peak, total):
    at = o_ref.shape[0] - stat_rows(peak.shape[0])
    rows = split(peak, 3) + split(total, 2)
    spare = o_ref.shape[0] - at - 5 * peak.shape[0]
    if spare:
        rows.append(jnp.zeros((spare, HD), jnp.float32))
    o_ref[at:, :] = jnp.concatenate(rows, axis=0).astype(jnp.bfloat16)


def get_stats(o_ref, heads):
    rows = o_ref[o_ref.shape[0] - stat_rows(heads) :, :].astype(jnp.float32)
    part = [rows[n * heads : (n + 1) * heads] for n in range(5)]
    return part[0] + part[1] + part[2], part[3] + part[4]


def weigh(values, p):
    return lax.dot_general(values, p, (((0,), (0,)), ((), ())), preferred_element_type=jnp.float32)


def far_values_kernel(heads, p, st, v_own, v_e, v_o, o_x):
    _, _, inner = place()
    lo, hi = heads[0], heads[-1] + 1

    @pl.when(inner)
    def _():
        total = st[0, STAT + lo : STAT + hi]
        put_stats(o_x, st[0, lo:hi], total)
        factor = 1.0 / total
        for n, h in enumerate(heads):
            cols = pl.ds(n * HD, HD)
            values = jnp.concatenate([v_own[:, cols], v_e[:, cols], v_o[:, cols]], axis=0)
            o_x[cols, :] = (weigh(values, p[h]) * factor[n : n + 1]).astype(o_x.dtype)


def merge(st_0, st_1, src):
    m0, l0, m1, l1 = st_0[src, :STAT], st_0[src, STAT:], st_1[src, :STAT], st_1[src, STAT:]
    peak = jnp.maximum(m0, m1)
    f0, f1 = jnp.exp2(m0 - peak), jnp.exp2(m1 - peak)
    total = f0 * l0 + f1 * l1
    return peak, total, (f0 / total, f1 / total)


def near_values_kernel(heads, every, p_0, p_1, st_0, st_1, v_own, v_e, v_o, o_own, o_d, *st_own):
    own = merge(st_0, st_1, 0)
    sib = merge(st_0, st_1, 1)
    if st_own:
        st_own[0][:STAT] = own[0]
        st_own[0][STAT:] = own[1]
        put_stats(o_d, sib[0][:every], sib[1][:every])
    for n, h in enumerate(heads):
        cols = pl.ds(n * HD, HD)
        beside = jnp.concatenate([v_e[:, cols], v_o[:, cols]], axis=0)
        part_0, part_1 = weigh(v_own[:, cols], p_0[h]), weigh(beside, p_1[h])
        for src, (out, factors) in enumerate(((o_own, own[2]), (o_d, sib[2]))):
            lanes = slice(src * HD, (src + 1) * HD)
            o = part_0[:, lanes] * factors[0][h : h + 1] + part_1[:, lanes] * factors[1][h : h + 1]
            out[cols, :] = o.astype(out.dtype)


def combine_kernel(heads, every, o_own, o_x, o_d, sib, st_own, *refs):
    out, buf, sem = refs[-3:]
    _, _, inner = place()
    lo, hi = heads[0], heads[-1] + 1
    m0, l0 = st_own[lo:hi], st_own[STAT + lo : STAT + hi]
    m1, l1 = [v[lo:hi] for v in get_stats(sib, every)]
    m2, l2 = get_stats(o_x, len(heads))
    m2, l2 = jnp.where(inner, m2, FILL), jnp.where(inner, l2, 0.0)
    peak = jnp.maximum(jnp.maximum(m0, m1), m2)
    f0, f1, f2 = l0 * jnp.exp2(m0 - peak), l1 * jnp.exp2(m1 - peak), l2 * jnp.exp2(m2 - peak)
    total = f0 + f1 + f2
    w0, w1, w2 = f0 / total, f1 / total, f2 / total
    for n in range(len(heads)):
        cols = pl.ds(n * HD, HD)
        x = jnp.where(inner, o_x[cols, :].astype(jnp.float32), 0.0)
        o = o_own[cols, :] * w0[n : n + 1] + o_d[cols, :].astype(jnp.float32) * w1[n : n + 1] + x * w2[n : n + 1]
        buf[:, cols] = o.T.astype(buf.dtype)
    copy = pltpu.make_async_copy(buf, out.at[:, lo * HD : hi * HD], sem)
    copy.start()
    copy.wait()


def body(n_groups, query, key, value, keep):
    n_blk, n_uly = lax.axis_size("blk"), lax.axis_size("uly")
    rows, width = query.shape
    heads = width // HD
    first = heads * 7 // 12
    heads_a, heads_b = range(first), range(first, heads)
    wide_a, wide_b = len(heads_a) * HD, len(heads_b) * HD
    everyone = ("groups", "blk", "uly")
    cross = row_pairs(n_groups, n_blk, n_uly)
    cores = [(0, 1), (1, 0)]
    vmem, hbm = pl.BlockSpec(memory_space=pltpu.VMEM), pl.BlockSpec(memory_space=pltpu.HBM)
    bf16, f32 = jnp.bfloat16, jnp.float32

    def exchange(x, parity):
        return lax.ppermute(x, ("blk", "uly"), plane_pairs(n_blk, n_uly, parity))

    def call(kernel, name, us, in_specs, out_shape, scratch=(), out_specs=None, aliases=None):
        return pl.pallas_call(
            kernel,
            in_specs=in_specs,
            out_specs=out_specs or jax.tree.map(lambda _: vmem, out_shape),
            out_shape=out_shape,
            scratch_shapes=scratch,
            input_output_aliases=aliases or {},
            compiler_params=pltpu.CompilerParams(vmem_limit_bytes=16 * 1024 * 1024),
            cost_estimate=pl.CostEstimate(flops=int(us * 1e9), bytes_accessed=0, transcendentals=0),
            name=name,
        )

    def array(dtype, *shape):
        return jax.ShapeDtypeStruct(shape, dtype)

    k_e = exchange(key, 0)
    k_o = exchange(key, 1)
    q_d = lax.ppermute(query, "uly", cores)
    q_late, _ = lax.optimization_barrier((query, q_d))
    bias, q_own = call(
        prepare_kernel,
        "prepare",
        0.7,
        [hbm, hbm],
        [array(f32, 16, HD), array(bf16, rows + FLAG_ROWS, width)],
        [pltpu.SMEM(keep.shape, keep.dtype), pltpu.SemaphoreType.DMA((2,))],
    )(keep, q_late)
    q_x = lax.ppermute(q_own, everyone, cross)

    st_near = array(f32, 2, 2 * STAT, rows)
    p_0, st_0, k_own, v_a, v_b = call(
        own_scores_kernel,
        "own_scores",
        1.5,
        [vmem, hbm, hbm, vmem, vmem],
        [array(bf16, heads, rows, 2 * rows), st_near]
        + [array(bf16, rows, width), array(bf16, rows, wide_a), array(bf16, rows, wide_b)],
        [pltpu.SemaphoreType.DMA((3,))],
    )(bias, key, value, q_own, q_d)

    va_e = exchange(v_a, 0)
    va_o = exchange(v_a, 1)
    v_even, k_e, _ = lax.optimization_barrier((v_b, k_e, st_0))
    vb_e = exchange(v_even, 0)

    p_1, st_1 = call(near_scores_kernel, "near_scores", 2, [vmem] * 5, [array(bf16, heads, 2 * rows, 2 * rows), st_near])(
        bias, k_e, k_o, q_own, q_d
    )
    v_odd, q_x, _ = lax.optimization_barrier((v_b, q_x, st_1))
    vb_o = exchange(v_odd, 1)
    p_x, st_x = call(
        far_scores_kernel, "far_scores", 0, [vmem] * 4, [array(bf16, heads, 3 * rows, rows), array(f32, 1, 2 * STAT, rows)]
    )(k_own, k_e, k_o, q_x)

    va_e, va_o, _ = lax.optimization_barrier((va_e, va_o, st_x))
    xa = call(
        functools.partial(far_values_kernel, heads_a),
        "far_values_a",
        0,
        [vmem] * 5,
        array(bf16, wide_a + stat_rows(len(heads_a)), rows),
    )(p_x, st_x, v_a, va_e, va_o)
    back_xa = lax.ppermute(xa, everyone, cross)
    va_e, va_o, _ = lax.optimization_barrier((va_e, va_o, xa))
    own_a, da, st_own = call(
        functools.partial(near_values_kernel, heads_a, heads),
        "near_values_a",
        0,
        [vmem] * 7,
        [array(f32, wide_a, rows), array(bf16, wide_a + stat_rows(heads), rows), array(f32, 2 * STAT, rows)],
    )(p_0, p_1, st_0, st_1, v_a, va_e, va_o)
    back_da = lax.ppermute(da, "uly", cores)

    vb_e, vb_o, _, _ = lax.optimization_barrier((vb_e, vb_o, st_own, xa))
    xb = call(
        functools.partial(far_values_kernel, heads_b),
        "far_values_b",
        5,
        [vmem] * 5,
        array(bf16, wide_b + stat_rows(len(heads_b)), rows),
    )(p_x, st_x, v_b, vb_e, vb_o)
    back_xb = lax.ppermute(xb, everyone, cross)
    own_b, db = call(
        functools.partial(near_values_kernel, heads_b, heads),
        "near_values_b",
        5,
        [vmem] * 7,
        [array(f32, wide_b, rows), array(bf16, wide_b, rows)],
    )(p_0, p_1, st_0, st_1, v_b, vb_e, vb_o)
    back_db = lax.ppermute(db, "uly", cores)

    out = array(query.dtype, rows, width)
    half = call(
        functools.partial(combine_kernel, heads_a, heads),
        "combine_a",
        0,
        [vmem] * 5,
        out,
        [pltpu.VMEM((rows, wide_a), query.dtype), pltpu.SemaphoreType.DMA],
        hbm,
    )(own_a, back_xa, back_da, back_da, st_own)
    return call(
        functools.partial(combine_kernel, heads_b, heads),
        "combine_b",
        0,
        [vmem] * 5 + [hbm],
        out,
        [pltpu.VMEM((rows, wide_b), query.dtype), pltpu.SemaphoreType.DMA],
        hbm,
        {5: 0},
    )(own_b, back_xb, back_db, back_da, st_own, half)


def solution(mesh):
    tokens = P(("groups", "blk", "uly"), None)
    return jax.shard_map(
        functools.partial(body, mesh.shape["groups"]),
        mesh=mesh,
        in_specs=(tokens, tokens, tokens, P(("groups", "blk"), None)),
        out_specs=tokens,
        check_vma=False,
    )
```

time: 29.7 us -> 28.1 us (0.946)
  the two profiles are of different devices: /device:TPU:1 before, /device:TPU:0 now
where the time goes in v3:
time: 28.1 us; the launch traced here: 27.7 us
  starting transfers between devices  14.6 us (52%)
  waiting for transfers between devices  5.85 us (21%)
  Pallas kernels  5.52 us (20%)
  local copies, waits for them, and re-layouts  1.68 us (6%)
    ppermute x6, starting transfers between devices, exchange(): return lax.ppermute(x, ('blk', 'uly'), plane_pairs(n_blk, n_uly, parity))  7.69 us
    ppermute x6, waiting for transfers between devices, exchange(): return lax.ppermute(x, ('blk', 'uly'), plane_pairs(n_blk, n_uly, parity))  4.02 us
    ppermute x1, starting transfers between devices, body(): back_xa = lax.ppermute(xa, everyone, cross)  1.89 us
    ppermute x1, starting transfers between devices, body(): q_x = lax.ppermute(q_own, everyone, cross)  1.71 us
    ppermute x1, starting transfers between devices, body(): back_xb = lax.ppermute(xb, everyone, cross)  1.69 us
    unnamed x8, local copies, waits for them, and re-layouts  1.68 us
    ppermute x1, waiting for transfers between devices, body(): back_xb = lax.ppermute(xb, everyone, cross)  1.64 us
    pallas_call x1, Pallas kernels, body(): call(near_scores_kernel, 'near_scores', 2, [vmem] * 5, [array(bf16, heads...  1.16 us
  transfers between devices with their start and end apart: 12, of which 5 were waited for; matrix products, arithmetic and copies ran while one was open for 0% of the time, Pallas kernels for 17%

profile of v3, /device:TPU:0, one launch (start us, length us, event | category | flops | bytes accessed | tf_op | source)
XLA Modules:
  0.0 27.7 jit_solution(4852596893994429155)
XLA Ops:
  0.0 0.5 %collective-permute-start = (bf16[128,1536]{1,0:T(8,128)(2,1)}, bf16[128,1536]{1,0:T(8,128)(2,1)S(1)}, u32[]{:S(2)}, u32[]{:S(2)}) collective-permute-start(bf16[128,1536]{1,0:T(8,128)(2,1)} %q_hbm), channel_id=1, source_target_pairs={{0,1},{1,0},{2,3},{3,2},{4,5},{5,4},{6,7},{7,6},{8,9},{9,8},{10,11... | collective-permute-start | bytes 1179656 | tf_op jit(solution)/shard_map/ppermute | solution.py:275
  0.5 2.6 %collective-permute-start.1 = (bf16[128,1536]{1,0:T(8,128)(2,1)}, bf16[128,1536]{1,0:T(8,128)(2,1)S(1)}, u32[]{:S(2)}, u32[]{:S(2)}) collective-permute-start(bf16[128,1536]{1,0:T(8,128)(2,1)} %k_hbm.1), channel_id=1, source_target_pairs={{0,4},{1,5},{2,6},{3,7},{4,0},{5,1},{6,2},{7,3},{8,12},{9,13},{10,... | collective-permute-start | bytes 1179656 | tf_op jit(solution)/shard_map/ppermute | solution.py:255
  3.0 0.2 collective-permute-start.2
  3.3 0.0 collective-permute-done.q_d
  3.3 0.0 copy-start
  3.3 1.0 %copy-done = bf16[128,1536]{1,0:T(8,128)(2,1)S(1)} copy-done((bf16[128,1536]{1,0:T(8,128)(2,1)S(1)}, bf16[128,1536]{1,0:T(8,128)(2,1)}, u32[]{:S(2)}) %copy-start) | copy-done | bytes 393240
  4.3 0.0 copy-start.3
  4.3 0.7 %copy-done.3 = s32[4,28]{1,0:T(4,128)S(1)} copy-done((s32[4,28]{1,0:T(4,128)S(1)}, s32[4,28]{1,0:T(4,128)}, u32[]{:S(2)}) %copy-start.3) | copy-done | bytes 472
  4.9 0.0 copy-start.1
  4.9 0.0 copy-start.2
  4.9 0.7 %prepare.1 = (f32[16,128]{1,0:T(8,128)S(1)}, bf16[144,1536]{1,0:T(8,128)(2,1)S(1)}) custom-call(s32[4,28]{1,0:T(4,128)S(1)} %copy-done.3, bf16[128,1536]{1,0:T(8,128)(2,1)S(1)} %copy-done), custom_call_target="tpu_custom_call" | custom-call | flops 700000000 | tf_op jit(solution)/shard_map/prepare/pallas_call | solution.py:277
  5.7 1.7 %collective-permute-start.4 = (bf16[144,1536]{1,0:T(8,128)(2,1)S(1)}, bf16[144,1536]{1,0:T(8,128)(2,1)S(1)}, u32[]{:S(2)}, u32[]{:S(2)}) collective-permute-start(bf16[144,1536]{1,0:T(8,128)(2,1)S(1)} %get-tuple-element.34.q_own), channel_id=1, source_target_pairs={{0,16},{1,2},{2,1},{3,19},{4,20},{5,6},{6,5},{7,23},{8,24},{9,10},... | collective-permute-start | bytes 1327112 | tf_op jit(solution)/shard_map/ppermute | solution.py:285
  7.4 0.0 copy-done.1
  7.4 0.0 copy-done.2
  7.4 1.0 %own_scores.1 = (bf16[12,128,256]{2,1,0:T(8,128)(2,1)S(1)}, f32[2,32,128]{2,1,0:T(8,128)S(1)}, bf16[128,1536]{1,0:T(8,128)(2,1)S(1)}, bf16[128,896]{1,0:T(8,128)(2,1)S(1)}, bf16[128,640]{1,0:T(8,128)(2,1)S(1)}) custom-call(f32[16,128]{1,0:T(8,128)S(1)} %get-tuple-element.33.bias, bf16[128,1536]{1,0:T(8,128)(2,1)S(1)} %copy-done.2, ...), custom_call_target="tpu_custom_call" | custom-call | flops 1500000000 | tf_op jit(solution)/shard_map/own_scores/pallas_call | solution.py:288
  8.4 2.9 %collective-permute-start.6 = (bf16[128,896]{1,0:T(8,128)(2,1)S(1)}, bf16[128,896]{1,0:T(8,128)(2,1)S(1)}, u32[]{:S(2)}, u32[]{:S(2)}) collective-permute-start(bf16[128,896]{1,0:T(8,128)(2,1)S(1)} %get-tuple-element.43.v_own), channel_id=1, source_target_pairs={{0,4},{1,5},{2,6},{3,7},{4,0},{5,1},{6,2},{7,3},{8,12},{9,13},{10,... | collective-permute-start | bytes 688136 | tf_op jit(solution)/shard_map/ppermute | solution.py:255
  11.3 0.0 collective-permute-start.7
  11.3 1.9 %collective-permute-done.1.k_e = bf16[128,1536]{1,0:T(8,128)(2,1)S(1)} collective-permute-done((bf16[128,1536]{1,0:T(8,128)(2,1)}, bf16[128,1536]{1,0:T(8,128)(2,1)S(1)}, u32[]{:S(2)}, u32[]{:S(2)}) %collective-permute-start.1) | collective-permute-done | bytes 393248 | tf_op jit(solution)/shard_map/ppermute | solution.py:255
  13.2 1.9 %collective-permute-start.3 = (bf16[128,640]{1,0:T(8,128)(2,1)S(1)}, bf16[128,640]{1,0:T(8,128)(2,1)S(1)}, u32[]{:S(2)}, u32[]{:S(2)}) collective-permute-start(bf16[128,640]{1,0:T(8,128)(2,1)S(1)} %get-tuple-element.42.v_own), channel_id=1, source_target_pairs={{0,4},{1,5},{2,6},{3,7},{4,0},{5,1},{6,2},{7,3},{8,12},{9,13},{10,... | collective-permute-start | bytes 491528 | tf_op jit(solution)/shard_map/ppermute | solution.py:255
  15.2 0.0 collective-permute-done.2.k_o
  15.2 1.2 %near_scores.1 = (bf16[12,256,256]{2,1,0:T(8,128)(2,1)S(1)}, f32[2,32,128]{2,1,0:T(8,128)S(1)}) custom-call(f32[16,128]{1,0:T(8,128)S(1)} %get-tuple-element.33.bias, bf16[128,1536]{1,0:T(8,128)(2,1)S(1)} %collective-permute-done.1.k_e, bf16[128,1536]{1,0:T(8,128)(2,1)S(1)} %collective-permute-done.2.k_o, bf16[144,1536]{1,0:T(8,128)(2,1)S(1)} %get-tuple-element.34.q_own, ...), custom_call_target="tpu_custom_call" | custom-call | flops 2000000000 | tf_op jit(solution)/shard_map/near_scores/pallas_call | solution.py:303
  16.3 0.0 collective-permute-done.4.q_x
  16.3 0.1 collective-permute-start.5
  16.4 1.7 %collective-permute-done.6.v_e = bf16[128,896]{1,0:T(8,128)(2,1)S(1)} collective-permute-done((bf16[128,896]{1,0:T(8,128)(2,1)S(1)}, bf16[128,896]{1,0:T(8,128)(2,1)S(1)}, u32[]{:S(2)}, u32[]{:S(2)}) %collective-permute-start.6) | collective-permute-done | bytes 229408 | tf_op jit(solution)/shard_map/ppermute | solution.py:255
  18.1 0.0 collective-permute-done.7.v_o
  18.1 1.9 %collective-permute-start.11 = (bf16[944,128]{1,0:T(8,128)(2,1)S(1)}, bf16[944,128]{1,0:T(8,128)(2,1)S(1)}, u32[]{:S(2)}, u32[]{:S(2)}) collective-permute-start(bf16[944,128]{1,0:T(8,128)(2,1)S(1)} %far_values_a.1), channel_id=1, source_target_pairs={{0,16},{1,2},{2,1},{3,19},{4,20},{5,6},{6,5},{7,23},{8,24},{9,10},... | collective-permute-start | bytes 725000 | tf_op jit(solution)/shard_map/ppermute | solution.py:320
  20.0 0.4 %near_values_a.1 = (f32[896,128]{1,0:T(8,128)S(1)}, bf16[960,128]{1,0:T(8,128)(2,1)S(1)}, f32[32,128]{1,0:T(8,128)S(1)}) custom-call(bf16[12,128,256]{2,1,0:T(8,128)(2,1)S(1)} %get-tuple-element.35.p_0, bf16[12,256,256]{2,1,0:T(8,128)(2,1)S(1)} %get-tuple-element.39.p_1, f32[2,32,128]{2,1,0:T(8,128)S(1)} %get-tuple-element.37.st_0, ...), custom_call_target="tpu_custom_call" | custom-call | tf_op jit(solution)/shard_map/near_values_a/pallas_call | solution.py:322
  20.5 0.6 %collective-permute-start.10 = (bf16[960,128]{1,0:T(8,128)(2,1)S(1)}, bf16[960,128]{1,0:T(8,128)(2,1)S(1)}, u32[]{:S(2)}, u32[]{:S(2)}) collective-permute-start(bf16[960,128]{1,0:T(8,128)(2,1)S(1)} %get-tuple-element.57), channel_id=1, source_target_pairs={{0,1},{1,0},{2,3},{3,2},{4,5},{5,4},{6,7},{7,6},{8,9},{9,8},{10,11... | collective-permute-start | bytes 737288 | tf_op jit(solution)/shard_map/ppermute | solution.py:329
  21.1 0.4 %collective-permute-done.3.v_e = bf16[128,640]{1,0:T(8,128)(2,1)S(1)} collective-permute-done((bf16[128,640]{1,0:T(8,128)(2,1)S(1)}, bf16[128,640]{1,0:T(8,128)(2,1)S(1)}, u32[]{:S(2)}, u32[]{:S(2)}) %collective-permute-start.3) | collective-permute-done | bytes 163872 | tf_op jit(solution)/shard_map/ppermute | solution.py:255
  21.4 0.0 collective-permute-done.5.v_o
  21.5 1.7 %collective-permute-start.8 = (bf16[672,128]{1,0:T(8,128)(2,1)S(1)}, bf16[672,128]{1,0:T(8,128)(2,1)S(1)}, u32[]{:S(2)}, u32[]{:S(2)}) collective-permute-start(bf16[672,128]{1,0:T(8,128)(2,1)S(1)} %far_values_b.1), channel_id=1, source_target_pairs={{0,16},{1,2},{2,1},{3,19},{4,20},{5,6},{6,5},{7,23},{8,24},{9,10},... | collective-permute-start | bytes 516104 | tf_op jit(solution)/shard_map/ppermute | solution.py:339
  23.1 0.4 %near_values_b.1 = (f32[640,128]{1,0:T(8,128)S(1)}, bf16[640,128]{1,0:T(8,128)(2,1)S(1)}) custom-call(bf16[12,128,256]{2,1,0:T(8,128)(2,1)S(1)} %get-tuple-element.35.p_0, bf16[12,256,256]{2,1,0:T(8,128)(2,1)S(1)} %get-tuple-element.39.p_1, f32[2,32,128]{2,1,0:T(8,128)S(1)} %get-tuple-element.37.st_0, f32[2,32,128]{2,1,0:T(8,128)S(1)} %get-tuple-element.40.st_1, ...), custom_call_target="tpu_custom_call" | custom-call | flops 5000000000 | tf_op jit(solution)/shard_map/near_values_b/pallas_call | solution.py:340
  23.5 0.6 %collective-permute-start.9 = (bf16[640,128]{1,0:T(8,128)(2,1)S(1)}, bf16[640,128]{1,0:T(8,128)(2,1)S(1)}, u32[]{:S(2)}, u32[]{:S(2)}) collective-permute-start(bf16[640,128]{1,0:T(8,128)(2,1)S(1)} %get-tuple-element.56), channel_id=1, source_target_pairs={{0,1},{1,0},{2,3},{3,2},{4,5},{5,4},{6,7},{7,6},{8,9},{9,8},{10,11... | collective-permute-start | bytes 491528 | tf_op jit(solution)/shard_map/ppermute | solution.py:347
  24.1 0.2 collective-permute-done.11.o_x
  24.3 0.0 collective-permute-done.10.o_d.sib
  24.3 0.9 %combine_a.1.refs_0_ = bf16[128,1536]{1,0:T(8,128)(2,1)} custom-call(f32[896,128]{1,0:T(8,128)S(1)} %get-tuple-element.58.o_own, bf16[944,128]{1,0:T(8,128)(2,1)S(1)} %collective-permute-done.11.o_x, bf16[960,128]{1,0:T(8,128)(2,1)S(1)} %collective-permute-done.10.o_d.sib, bf16[960,128]{1,0:T(8,128)(2,1)S(1)} %collective-permute-done.10.o_d.sib, ...), custom_call_target="tpu_custom_call" | custom-call | tf_op jit(solution)/shard_map/combine_a/pallas_call | solution.py:350
  25.2 0.0 collective-permute-done.9.o_d
  25.2 1.6 %collective-permute-done.8.o_x = bf16[672,128]{1,0:T(8,128)(2,1)S(1)} collective-permute-done((bf16[672,128]{1,0:T(8,128)(2,1)S(1)}, bf16[672,128]{1,0:T(8,128)(2,1)S(1)}, u32[]{:S(2)}, u32[]{:S(2)}) %collective-permute-start.8) | collective-permute-done | bytes 172064 | tf_op jit(solution)/shard_map/ppermute | solution.py:339
  26.9 0.9 %combine_b.1 = bf16[128,1536]{1,0:T(8,128)(2,1)} custom-call(f32[640,128]{1,0:T(8,128)S(1)} %get-tuple-element.55.o_own, bf16[672,128]{1,0:T(8,128)(2,1)S(1)} %collective-permute-done.8.o_x, bf16[640,128]{1,0:T(8,128)(2,1)S(1)} %collective-permute-done.9.o_d, bf16[960,128]{1,0:T(8,128)(2,1)S(1)} %collective-permute-done.10.o_d.sib, ...), custom_call_target="tpu_custom_call", output_to_operand_aliasing={{}: (5, {})} | custom-call | tf_op jit(solution)/shard_map/combine_b/pallas_call | solution.py:359
  (3 shorter events, 0.0 us)
Async XLA Ops:
  0.0 3.3 %collective-permute-start = (bf16[128,1536]{1,0:T(8,128)(2,1)}, bf16[128,1536]{1,0:T(8,128)(2,1)S(1)}, u32[]{:S(2)}, u32[]{:S(2)}) collective-permute-start(bf16[128,1536]{1,0:T(8,128)(2,1)} %q_hbm), channel_id=1, source_target_pairs={{0,1},{1,0},{2,3},{3,2},{4,5},{5,4},{6,7},{7,6},{8,9},{9,8},{10,11... | collective-permute-start | bytes 1179656 | tf_op jit(solution)/shard_map/ppermute | solution.py:275
  0.5 12.7 %collective-permute-start.1 = (bf16[128,1536]{1,0:T(8,128)(2,1)}, bf16[128,1536]{1,0:T(8,128)(2,1)S(1)}, u32[]{:S(2)}, u32[]{:S(2)}) collective-permute-start(bf16[128,1536]{1,0:T(8,128)(2,1)} %k_hbm.1), channel_id=1, source_target_pairs={{0,4},{1,5},{2,6},{3,7},{4,0},{5,1},{6,2},{7,3},{8,12},{9,13},{10,... | collective-permute-start | bytes 1179656 | tf_op jit(solution)/shard_map/ppermute | solution.py:255
  3.0 12.1 %collective-permute-start.2 = (bf16[128,1536]{1,0:T(8,128)(2,1)}, bf16[128,1536]{1,0:T(8,128)(2,1)S(1)}, u32[]{:S(2)}, u32[]{:S(2)}) collective-permute-start(bf16[128,1536]{1,0:T(8,128)(2,1)} %k_hbm.1), channel_id=1, source_target_pairs={{0,1},{1,0},{2,3},{3,2},{4,8},{5,9},{6,10},{7,11},{8,4},{9,5},{10,... | collective-permute-start | bytes 1179656 | tf_op jit(solution)/shard_map/ppermute | solution.py:255
  3.3 1.0 %copy-start = (bf16[128,1536]{1,0:T(8,128)(2,1)S(1)}, bf16[128,1536]{1,0:T(8,128)(2,1)}, u32[]{:S(2)}) copy-start(bf16[128,1536]{1,0:T(8,128)(2,1)} %q_hbm) | copy-start | bytes 1179652
  4.3 0.7 %copy-start.3 = (s32[4,28]{1,0:T(4,128)S(1)}, s32[4,28]{1,0:T(4,128)}, u32[]{:S(2)}) copy-start(s32[4,28]{1,0:T(4,128)} %keep_hbm.1) | copy-start | bytes 1348
  4.9 2.4 %copy-start.1 = (bf16[128,1536]{1,0:T(8,128)(2,1)S(1)}, bf16[128,1536]{1,0:T(8,128)(2,1)}, u32[]{:S(2)}) copy-start(bf16[128,1536]{1,0:T(8,128)(2,1)} %v_hbm.1) | copy-start | bytes 1179652
  4.9 2.5 %copy-start.2 = (bf16[128,1536]{1,0:T(8,128)(2,1)S(1)}, bf16[128,1536]{1,0:T(8,128)(2,1)}, u32[]{:S(2)}) copy-start(bf16[128,1536]{1,0:T(8,128)(2,1)} %k_hbm.1) | copy-start | bytes 1179652
  5.7 10.6 %collective-permute-start.4 = (bf16[144,1536]{1,0:T(8,128)(2,1)S(1)}, bf16[144,1536]{1,0:T(8,128)(2,1)S(1)}, u32[]{:S(2)}, u32[]{:S(2)}) collective-permute-start(bf16[144,1536]{1,0:T(8,128)(2,1)S(1)} %get-tuple-element.34.q_own), channel_id=1, source_target_pairs={{0,16},{1,2},{2,1},{3,19},{4,20},{5,6},{6,5},{7,23},{8,24},{9,10},... | collective-permute-start | bytes 1327112 | tf_op jit(solution)/shard_map/ppermute | solution.py:285
  8.4 9.7 %collective-permute-start.6 = (bf16[128,896]{1,0:T(8,128)(2,1)S(1)}, bf16[128,896]{1,0:T(8,128)(2,1)S(1)}, u32[]{:S(2)}, u32[]{:S(2)}) collective-permute-start(bf16[128,896]{1,0:T(8,128)(2,1)S(1)} %get-tuple-element.43.v_own), channel_id=1, source_target_pairs={{0,4},{1,5},{2,6},{3,7},{4,0},{5,1},{6,2},{7,3},{8,12},{9,13},{10,... | collective-permute-start | bytes 688136 | tf_op jit(solution)/shard_map/ppermute | solution.py:255
  11.3 6.9 %collective-permute-start.7 = (bf16[128,896]{1,0:T(8,128)(2,1)S(1)}, bf16[128,896]{1,0:T(8,128)(2,1)S(1)}, u32[]{:S(2)}, u32[]{:S(2)}) collective-permute-start(bf16[128,896]{1,0:T(8,128)(2,1)S(1)} %get-tuple-element.43.v_own), channel_id=1, source_target_pairs={{0,1},{1,0},{2,3},{3,2},{4,8},{5,9},{6,10},{7,11},{8,4},{9,5},{10,... | collective-permute-start | bytes 688136 | tf_op jit(solution)/shard_map/ppermute | solution.py:255
  13.2 8.2 %collective-permute-start.3 = (bf16[128,640]{1,0:T(8,128)(2,1)S(1)}, bf16[128,640]{1,0:T(8,128)(2,1)S(1)}, u32[]{:S(2)}, u32[]{:S(2)}) collective-permute-start(bf16[128,640]{1,0:T(8,128)(2,1)S(1)} %get-tuple-element.42.v_own), channel_id=1, source_target_pairs={{0,4},{1,5},{2,6},{3,7},{4,0},{5,1},{6,2},{7,3},{8,12},{9,13},{10,... | collective-permute-start | bytes 491528 | tf_op jit(solution)/shard_map/ppermute | solution.py:255
  16.3 5.1 %collective-permute-start.5 = (bf16[128,640]{1,0:T(8,128)(2,1)S(1)}, bf16[128,640]{1,0:T(8,128)(2,1)S(1)}, u32[]{:S(2)}, u32[]{:S(2)}) collective-permute-start(bf16[128,640]{1,0:T(8,128)(2,1)S(1)} %get-tuple-element.42.v_own), channel_id=1, source_target_pairs={{0,1},{1,0},{2,3},{3,2},{4,8},{5,9},{6,10},{7,11},{8,4},{9,5},{10,... | collective-permute-start | bytes 491528 | tf_op jit(solution)/shard_map/ppermute | solution.py:255
  18.1 6.2 %collective-permute-start.11 = (bf16[944,128]{1,0:T(8,128)(2,1)S(1)}, bf16[944,128]{1,0:T(8,128)(2,1)S(1)}, u32[]{:S(2)}, u32[]{:S(2)}) collective-permute-start(bf16[944,128]{1,0:T(8,128)(2,1)S(1)} %far_values_a.1), channel_id=1, source_target_pairs={{0,16},{1,2},{2,1},{3,19},{4,20},{5,6},{6,5},{7,23},{8,24},{9,10},... | collective-permute-start | bytes 725000 | tf_op jit(solution)/shard_map/ppermute | solution.py:320
  20.5 3.8 %collective-permute-start.10 = (bf16[960,128]{1,0:T(8,128)(2,1)S(1)}, bf16[960,128]{1,0:T(8,128)(2,1)S(1)}, u32[]{:S(2)}, u32[]{:S(2)}) collective-permute-start(bf16[960,128]{1,0:T(8,128)(2,1)S(1)} %get-tuple-element.57), channel_id=1, source_target_pairs={{0,1},{1,0},{2,3},{3,2},{4,5},{5,4},{6,7},{7,6},{8,9},{9,8},{10,11... | collective-permute-start | bytes 737288 | tf_op jit(solution)/shard_map/ppermute | solution.py:329
  21.5 5.4 %collective-permute-start.8 = (bf16[672,128]{1,0:T(8,128)(2,1)S(1)}, bf16[672,128]{1,0:T(8,128)(2,1)S(1)}, u32[]{:S(2)}, u32[]{:S(2)}) collective-permute-start(bf16[672,128]{1,0:T(8,128)(2,1)S(1)} %far_values_b.1), channel_id=1, source_target_pairs={{0,16},{1,2},{2,1},{3,19},{4,20},{5,6},{6,5},{7,23},{8,24},{9,10},... | collective-permute-start | bytes 516104 | tf_op jit(solution)/shard_map/ppermute | solution.py:339
  23.5 1.7 %collective-permute-start.9 = (bf16[640,128]{1,0:T(8,128)(2,1)S(1)}, bf16[640,128]{1,0:T(8,128)(2,1)S(1)}, u32[]{:S(2)}, u32[]{:S(2)}) collective-permute-start(bf16[640,128]{1,0:T(8,128)(2,1)S(1)} %get-tuple-element.56), channel_id=1, source_target_pairs={{0,1},{1,0},{2,3},{3,2},{4,5},{5,4},{6,7},{7,6},{8,9},{9,8},{10,11... | collective-permute-start | bytes 491528 | tf_op jit(solution)/shard_map/ppermute | solution.py:347

commit v4 on v0

v4 whole, which is shorter than its diff:
```python
import functools
import math

import jax
import jax.numpy as jnp
from jax import lax
from jax.experimental import pallas as pl
from jax.experimental.pallas import tpu as pltpu
from jax.sharding import PartitionSpec as P

HD = 128
TILE = 64
TH = 4
TW = 2
STAT = 16
FLAG_ROWS = 16
FILL = -1e30
LOG2E = 1.4426950408889634


def plane_pairs(n_blk, n_uly, parity):
    blks = TH // n_uly
    route = []
    for blk in range(n_blk):
        t = blk // blks
        other = t + 1 if t % 2 == parity else t - 1
        for u in range(n_uly):
            there = blk, n_uly - 1 - u
            if 0 <= other < n_blk // blks:
                there = other * blks + blk % blks, u
            route.append((blk * n_uly + u, there[0] * n_uly + there[1]))
    return route


def chip_pairs(n_blk, n_uly):
    blks = TH // n_uly
    return [(blk, blk - blk % blks + blks - 1 - blk % blks) for blk in range(n_blk)]


def place():
    n_uly = lax.axis_size("uly")
    rows = TH // n_uly
    blk = lax.axis_index("blk")
    row = lax.rem(blk, rows) * n_uly + lax.axis_index("uly")
    return lax.rem(lax.div(blk, rows), 2), row, (row > 0) & (row < TH - 1)


def flag_rows(keep, parity, key_row, query_row):
    first = lax.broadcasted_iota(jnp.int32, (1, HD), 1) < TILE
    tiles = keep.shape[0]
    line = lax.rem(query_row * TW, tiles)
    base = (keep.shape[1] - tiles) // 2
    step = 1 - 2 * parity
    rows = []
    for dt in (0, step, -step):
        column = base + TH * TW * dt + TW * (key_row - query_row) + line
        for w in range(TW):
            col = jnp.clip(column + w, 0, keep.shape[1] - 1)
            low = (keep[line, col] > 0).astype(jnp.float32)
            high = (keep[line + 1, col] > 0).astype(jnp.float32)
            rows.append(jnp.where(first, low, high))
    return rows


def by_role(middle, outer):
    _, _, inner = place()
    pl.when(inner)(middle)
    pl.when(jnp.logical_not(inner))(outer)


def my_columns(width, mine=True):
    u = lax.axis_index("uly")
    return pl.ds(pl.multiple_of((u if mine else 1 - u) * width, HD), width)


def cut_kernel(k_hbm, v_hbm, k_own, v_own, sems):
    columns = my_columns(k_own.shape[1])
    copies = [
        pltpu.make_async_copy(x.at[:, columns], out, sems.at[n]) for n, (x, out) in enumerate(((k_hbm, k_own), (v_hbm, v_own)))
    ]
    for copy in copies:
        copy.start()
    for copy in copies:
        copy.wait()


def pack_kernel(k_own, v_own, k_d, v_d, first, k_o, v_o):
    rows, width = k_own.shape

    columns = my_columns(width)

    def middle():
        first[:rows, :] = k_own[...]
        first[rows:, :] = v_own[...]
        k_o[...] = k_d[:, columns]
        v_o[...] = v_d[:, columns]

    def outer():
        first[:rows, :] = k_d[:, columns]
        first[rows:, :] = v_d[:, columns]
        k_o[...] = k_own[...]
        v_o[...] = v_own[...]

    by_role(middle, outer)


def arrange_kernel(keep_hbm, q_hbm, q_d, q_i, q_o, bias, mine, keep, sems):
    tokens, width = q_o.shape
    flags = pltpu.make_async_copy(keep_hbm, keep, sems.at[0])
    flags.start()
    copy = pltpu.make_async_copy(q_hbm.at[:, my_columns(width)], mine, sems.at[1])
    copy.start()
    flags.wait()
    parity, row, inner = place()
    sibling = row + 1 - 2 * lax.rem(row, 2)
    middle_row, outer_row = jnp.where(inner, row, sibling), jnp.where(inner, sibling, row)
    rows = []
    for keys in (middle_row, outer_row):
        for queries in (middle_row, outer_row):
            rows += flag_rows(keep, parity, keys, queries)
    bias[...] = (jnp.concatenate(rows, axis=0) - 1.0) * -FILL
    rows = flag_rows(keep, parity, TH - 1 - middle_row, middle_row)
    rows += [jnp.zeros((1, HD), jnp.float32)] * (FLAG_ROWS - len(rows))
    q_i[tokens:, :HD] = jnp.concatenate(rows, axis=0).astype(q_i.dtype)
    copy.wait()

    def middle():
        q_i[:tokens, :] = mine[...]
        q_o[...] = q_d[:, my_columns(width)]

    def outer():
        q_i[:tokens, :] = q_d[:, my_columns(width)]
        q_o[...] = mine[...]

    by_role(middle, outer)


def softmax_part(q, keys, flags):
    scale = LOG2E / math.sqrt(HD)
    s = lax.dot_general(keys, q, (((1,), (1,)), ((), ())), preferred_element_type=jnp.float32)
    t = jnp.concatenate([s[n * TILE : (n + 1) * TILE] * scale + flag for n, flag in enumerate(flags)], axis=0)
    m = jnp.max(t, axis=0, keepdims=True)
    e = jnp.exp2(t - m)
    return e.astype(jnp.bfloat16), m, jnp.sum(e, axis=0, keepdims=True)


def bias_rows(bias, keys):
    count = 3 * TW
    return [[bias[n : n + 1, :] for n in range(at, at + count)] for at in (2 * keys * count, (2 * keys + 1) * count)]


def far_kernel(first, r_e, r_o, q_x, o_x):
    rows = first.shape[0] // 2
    heads = first.shape[1] // HD
    flags = (q_x[rows:, :HD].astype(jnp.float32) - 1.0) * -FILL
    flags = [flags[n : n + 1] for n in range(3 * TW)]
    peaks, totals = [], []
    for h in range(heads):
        cols = pl.ds(h * HD, HD)
        p, m, total = softmax_part(
            q_x[:rows, cols], jnp.concatenate([x[:rows, cols] for x in (first, r_e, r_o)], axis=0), flags
        )
        o = weigh(jnp.concatenate([x[rows:, cols] for x in (first, r_e, r_o)], axis=0), p)
        o_x[cols, :] = (o / total).astype(o_x.dtype)
        peaks.append(m)
        totals.append(total)
    put_stats(o_x, jnp.concatenate(peaks, axis=0), jnp.concatenate(totals, axis=0))


def middle_kernel(bias, first, r_e, r_o, q_i, q_o, acc, st):
    rows = first.shape[0] // 2
    flags = bias_rows(bias, 0)
    for h in range(first.shape[1] // HD):
        cols = pl.ds(h * HD, HD)
        keys = jnp.concatenate([x[:rows, cols] for x in (first, r_e, r_o)], axis=0)
        values = jnp.concatenate([x[rows:, cols] for x in (first, r_e, r_o)], axis=0)
        for src, q in enumerate((q_i, q_o)):
            p, m, total = softmax_part(q[:rows, cols], keys, flags[src])
            acc[cols, src * HD : (src + 1) * HD] = weigh(values, p)
            st[src, h : h + 1, :] = m
            st[src, STAT + h : STAT + h + 1, :] = total


def outer_scores_kernel(bias, k_own, k_e, k_o, q_i, q_o, p_ref, st):
    rows = k_own.shape[0]
    flags = bias_rows(bias, 1)
    for h in range(p_ref.shape[0]):
        cols = pl.ds(h * HD, HD)
        keys = jnp.concatenate([k[:, cols] for k in (k_own, k_e, k_o)], axis=0)
        for src, q in enumerate((q_i, q_o)):
            p, m, total = softmax_part(q[:rows, cols], keys, flags[src])
            p_ref[h, :, src * HD : (src + 1) * HD] = p
            st[src, h : h + 1, :] = m
            st[src, STAT + h : STAT + h + 1, :] = total


def split(values, pieces):
    out = []
    for _ in range(pieces):
        piece = values.astype(jnp.bfloat16).astype(jnp.float32)
        out.append(piece)
        values = values - piece
    return out


def stat_rows(heads):
    return -(-5 * heads // 16) * 16


def put_stats(o_ref, peak, total):
    at = peak.shape[0] * HD
    rows = split(peak, 3) + split(total, 2)
    spare = o_ref.shape[0] - at - 5 * peak.shape[0]
    if spare:
        rows.append(jnp.zeros((spare, HD), jnp.float32))
    o_ref[at:, :] = jnp.concatenate(rows, axis=0).astype(jnp.bfloat16)


def get_stats(o_ref, heads):
    rows = o_ref[heads * HD :, :].astype(jnp.float32)
    part = [rows[n * heads : (n + 1) * heads] for n in range(5)]
    return part[0] + part[1] + part[2], part[3] + part[4]


def weigh(values, p):
    return lax.dot_general(values, p, (((0,), (0,)), ((), ())), preferred_element_type=jnp.float32)


def scale_parts(parts):
    peak = functools.reduce(jnp.maximum, [m for m, _ in parts])
    scales = [jnp.exp2(m - peak) for m, _ in parts]
    total = sum(f * l for f, (_, l) in zip(scales, parts))
    return [f / total for f in scales]


def outer_values_kernel(p, v_own, v_e, acc):
    rows = v_own.shape[0]
    for h in range(p.shape[0]):
        cols = pl.ds(h * HD, HD)
        acc[cols, :] = weigh(jnp.concatenate([v_own[:, cols], v_e[:, cols]], axis=0), p[h, : 2 * rows, :])


def finish_kernel(mine, p, st_i, st_o, acc, acc_o, v_o, x, out):
    heads = p.shape[0]

    def run(src):
        parts = [(st[src, :heads], st[src, STAT : STAT + heads]) for st in (st_i, st_o)]
        if src == 0:
            parts.append(get_stats(x, heads))
        scale = scale_parts(parts)
        if src == 0:
            scale[2] = scale[2] * parts[2][1]
        lanes = slice(src * HD, (src + 1) * HD)
        for h in range(heads):
            cols = pl.ds(h * HD, HD)
            rest = acc_o[cols, lanes] + weigh(v_o[:, cols], p[h, 2 * v_o.shape[0] :, lanes])
            o = acc[cols, lanes] * scale[0][h : h + 1] + rest * scale[1][h : h + 1]
            if src == 0:
                o = o + x[cols, :].astype(jnp.float32) * scale[2][h : h + 1]
            out[:, cols] = o.T.astype(out.dtype)

    by_role(lambda: run(0 if mine else 1), lambda: run(1 if mine else 0))


def put_kernel(own, back, out, sems):
    width = own.shape[1]
    copies = [
        pltpu.make_async_copy(x, out.at[:, my_columns(width, mine)], sems.at[n])
        for n, (x, mine) in enumerate(((own, True), (back, False)))
    ]
    for copy in copies:
        copy.start()
    for copy in copies:
        copy.wait()


def body(query, key, value, keep):
    n_blk, n_uly = lax.axis_size("blk"), lax.axis_size("uly")
    rows, width = query.shape
    half = width // 2
    heads = half // HD
    cores = [(0, 1), (1, 0)]
    vmem, hbm = pl.BlockSpec(memory_space=pltpu.VMEM), pl.BlockSpec(memory_space=pltpu.HBM)
    bf16, f32 = jnp.bfloat16, jnp.float32

    def exchange(x, parity):
        return lax.ppermute(x, ("blk", "uly"), plane_pairs(n_blk, n_uly, parity))

    def across(x):
        return lax.ppermute(x, "blk", chip_pairs(n_blk, n_uly))

    def swap(x):
        return lax.ppermute(x, "uly", cores)

    def call(kernel, name, us, in_specs, out_shape, scratch=(), out_specs=None):
        return pl.pallas_call(
            kernel,
            in_specs=in_specs,
            out_specs=out_specs or jax.tree.map(lambda _: vmem, out_shape),
            out_shape=out_shape,
            scratch_shapes=scratch,
            compiler_params=pltpu.CompilerParams(vmem_limit_bytes=16 * 1024 * 1024),
            cost_estimate=pl.CostEstimate(flops=int(us * 1e9), bytes_accessed=0, transcendentals=0),
            name=name,
        )

    def array(dtype, *shape):
        return jax.ShapeDtypeStruct(shape, dtype)

    def in_hbm(x):
        return pltpu.with_memory_space_constraint(x, pltpu.HBM)

    part = array(bf16, rows, half)
    dma = pltpu.SemaphoreType.DMA
    stats = array(f32, 2, 2 * STAT, rows)

    k_d, v_d, q_d = swap(key), swap(value), swap(query)
    k_own, v_own = call(cut_kernel, "cut", 1, [hbm] * 2, [part] * 2, [dma((2,))])(in_hbm(key), in_hbm(value))
    first, k_o, v_o = call(pack_kernel, "pack", 0, [vmem] * 4, [array(bf16, 2 * rows, half), part, part])(
        k_own, v_own, k_d, v_d
    )

    r_o, r_e = exchange(first, 1), exchange(first, 0)
    q_d, _ = lax.optimization_barrier((q_d, k_o))
    q_i, q_o, bias = call(
        arrange_kernel,
        "arrange",
        0,
        [hbm, hbm, vmem],
        [array(bf16, rows + FLAG_ROWS, half), part, array(f32, 12 * TW, HD)],
        [pltpu.VMEM((rows, half), bf16), pltpu.SMEM(keep.shape, keep.dtype), dma((2,))],
    )(in_hbm(keep), in_hbm(query), q_d)
    q_x = across(q_i)

    k_late, _ = lax.optimization_barrier((k_o, bias))
    ko_o, ko_e = exchange(k_late, 1), exchange(k_late, 0)

    v_even, r_e = lax.optimization_barrier((v_o, r_e))
    vo_e = exchange(v_even, 0)
    x = call(far_kernel, "far", 0, [vmem] * 4, array(bf16, half + stat_rows(heads), rows))(first, r_e, r_o, q_x)
    v_odd, r_o, r_e, _ = lax.optimization_barrier((v_o, r_o, r_e, x))
    x = across(x)
    vo_o = exchange(v_odd, 1)
    acc, st_i = call(middle_kernel, "middle", 1, [vmem] * 6, [array(f32, half, 2 * rows), stats])(
        bias, first, r_e, r_o, q_i, q_o
    )
    ko_o, ko_e, _ = lax.optimization_barrier((ko_o, ko_e, st_i))
    p_o, st_o = call(outer_scores_kernel, "outer_scores", 1, [vmem] * 6, [array(bf16, heads, 3 * rows, 2 * rows), stats])(
        bias, k_o, ko_e, ko_o, q_i, q_o
    )
    vo_e, _ = lax.optimization_barrier((vo_e, st_o))
    acc_o = call(outer_values_kernel, "outer_values", 1, [vmem] * 3, array(f32, half, 2 * rows))(p_o, v_o, vo_e)
    vo_o, _ = lax.optimization_barrier((vo_o, acc_o))
    parts = p_o, st_i, st_o, acc, acc_o, vo_o, x
    out_sib = call(functools.partial(finish_kernel, False), "finish_sibling", 0, [vmem] * 7, part)(*parts)
    back = swap(out_sib)
    acc, _ = lax.optimization_barrier((acc, out_sib))
    parts = p_o, st_i, st_o, acc, acc_o, vo_o, x
    out_own = call(functools.partial(finish_kernel, True), "finish_own", 0, [vmem] * 7, part)(*parts)
    return call(put_kernel, "put", 0, [vmem] * 2, array(query.dtype, rows, width), [dma((2,))], hbm)(out_own, back)


def solution(mesh):
    tokens = P(("groups", "blk", "uly"), None)
    return jax.shard_map(
        body,
        mesh=mesh,
        in_specs=(tokens, tokens, tokens, P(("groups", "blk"), None)),
        out_specs=tokens,
        check_vma=False,
    )
```

time: 111 us -> 27.2 us (0.25)
  the two profiles are of different devices: /device:TPU:9 before, /device:TPU:0 now
where the time goes in v4:
time: 27.2 us; the launch traced here: 26.8 us
  starting transfers between devices  12.4 us (46%)
  waiting for transfers between devices  7.79 us (29%)
  Pallas kernels  6.49 us (24%)
    ppermute x6, starting transfers between devices, exchange(): return lax.ppermute(x, ('blk', 'uly'), plane_pairs(n_blk, n_uly, parity))  8.23 us
    ppermute x6, waiting for transfers between devices, exchange(): return lax.ppermute(x, ('blk', 'uly'), plane_pairs(n_blk, n_uly, parity))  5.83 us
    ppermute x2, starting transfers between devices, across(): return lax.ppermute(x, 'blk', chip_pairs(n_blk, n_uly))  3.12 us
    ppermute x4, waiting for transfers between devices, swap(): return lax.ppermute(x, 'uly', cores)  1.63 us
    pallas_call x1, Pallas kernels, body(): call(middle_kernel, 'middle', 1, [vmem] * 6, [array(f32, half, 2 * rows),...  1.07 us
    pallas_call x1, Pallas kernels, body(): call(cut_kernel, 'cut', 1, [hbm] * 2, [part] * 2, [dma((2,))])  1.04 us
    ppermute x4, starting transfers between devices, swap(): return lax.ppermute(x, 'uly', cores)  1.03 us
    pallas_call x1, Pallas kernels, body(): call(arrange_kernel, 'arrange', 0, [hbm, hbm, vmem], [array(bf16, rows +...  0.97 us
  transfers between devices with their start and end apart: 12, of which 5 were waited for; matrix products, arithmetic and copies ran while one was open for 0% of the time, Pallas kernels for 20%

profile of v4, /device:TPU:0, one launch (start us, length us, event | category | flops | bytes accessed | tf_op | source)
XLA Modules:
  0.0 26.8 jit_solution(3179199592640199654)
XLA Ops:
  0.0 0.5 %collective-permute-start.1 = (bf16[128,1536]{1,0:T(8,128)(2,1)}, bf16[128,1536]{1,0:T(8,128)(2,1)S(1)}, u32[]{:S(2)}, u32[]{:S(2)}) collective-permute-start(bf16[128,1536]{1,0:T(8,128)(2,1)} %k_hbm.1), channel_id=1, source_target_pairs={{0,1},{1,0},{2,3},{3,2},{4,5},{5,4},{6,7},{7,6},{8,9},{9,8},{10,11... | collective-permute-start | bytes 1179656 | tf_op jit(solution)/shard_map/ppermute | solution.py:293
  0.5 0.1 collective-permute-start.2
  0.5 0.5 %collective-permute-start = (bf16[128,1536]{1,0:T(8,128)(2,1)}, bf16[128,1536]{1,0:T(8,128)(2,1)S(1)}, u32[]{:S(2)}, u32[]{:S(2)}) collective-permute-start(bf16[128,1536]{1,0:T(8,128)(2,1)} %q_hbm.1), channel_id=1, source_target_pairs={{0,1},{1,0},{2,3},{3,2},{4,5},{5,4},{6,7},{7,6},{8,9},{9,8},{10,11... | collective-permute-start | bytes 1179656 | tf_op jit(solution)/shard_map/ppermute | solution.py:293
  1.0 1.0 %cut.1 = (bf16[128,768]{1,0:T(8,128)(2,1)S(1)}, bf16[128,768]{1,0:T(8,128)(2,1)S(1)}) custom-call(bf16[128,1536]{1,0:T(8,128)(2,1)} %k_hbm.1, bf16[128,1536]{1,0:T(8,128)(2,1)} %v_hbm.1), custom_call_target="tpu_custom_call" | custom-call | flops 1000000000 | tf_op jit(solution)/shard_map/cut/pallas_call | solution.py:318
  2.0 0.0 collective-permute-done.1.k_d
  2.0 0.6 %collective-permute-done.2.v_d = bf16[128,1536]{1,0:T(8,128)(2,1)S(1)} collective-permute-done((bf16[128,1536]{1,0:T(8,128)(2,1)}, bf16[128,1536]{1,0:T(8,128)(2,1)S(1)}, u32[]{:S(2)}, u32[]{:S(2)}) %collective-permute-start.2) | collective-permute-done | bytes 393248 | tf_op jit(solution)/shard_map/ppermute | solution.py:293
  2.6 0.1 pack.1
  2.6 3.0 %collective-permute-start.6 = (bf16[256,768]{1,0:T(8,128)(2,1)S(1)}, bf16[256,768]{1,0:T(8,128)(2,1)S(1)}, u32[]{:S(2)}, u32[]{:S(2)}) collective-permute-start(bf16[256,768]{1,0:T(8,128)(2,1)S(1)} %get-tuple-element.35.first), channel_id=1, source_target_pairs={{0,4},{1,5},{2,6},{3,7},{4,0},{5,1},{6,2},{7,3},{8,12},{9,13},{10,... | collective-permute-start | bytes 1179656 | tf_op jit(solution)/shard_map/ppermute | solution.py:287
  5.6 0.0 collective-permute-start.5
  5.6 0.0 collective-permute-done.q_d
  5.6 1.0 %arrange.1 = (bf16[144,768]{1,0:T(8,128)(2,1)S(1)}, bf16[128,768]{1,0:T(8,128)(2,1)S(1)}, f32[24,128]{1,0:T(8,128)S(1)}) custom-call(s32[4,28]{1,0:T(4,128)} %keep_hbm.1, bf16[128,1536]{1,0:T(8,128)(2,1)} %q_hbm.1, bf16[128,1536]{1,0:T(8,128)(2,1)S(1)} %collective-permute-done.q_d), custom_call_target="tpu_custom_call" | custom-call | tf_op jit(solution)/shard_map/arrange/pallas_call | solution.py:325
  6.6 1.6 %collective-permute-start.7 = (bf16[144,768]{1,0:T(8,128)(2,1)S(1)}, bf16[144,768]{1,0:T(8,128)(2,1)S(1)}, u32[]{:S(2)}, u32[]{:S(2)}) collective-permute-start(bf16[144,768]{1,0:T(8,128)(2,1)S(1)} %get-tuple-element.38.q_i), channel_id=1, source_target_pairs={{0,2},{2,0},{4,6},{6,4},{8,10},{10,8},{12,14},{14,12},{1,3},{3,1},... | collective-permute-start | bytes 663560 | tf_op jit(solution)/shard_map/ppermute | solution.py:290
  8.2 0.2 collective-permute-start.3
  8.4 2.9 %collective-permute-start.4 = (bf16[128,768]{1,0:T(8,128)(2,1)S(1)}, bf16[128,768]{1,0:T(8,128)(2,1)S(1)}, u32[]{:S(2)}, u32[]{:S(2)}) collective-permute-start(bf16[128,768]{1,0:T(8,128)(2,1)S(1)} %get-tuple-element.34.k_own), channel_id=1, source_target_pairs={{0,4},{1,5},{2,6},{3,7},{4,0},{5,1},{6,2},{7,3},{8,12},{9,13},{10,... | collective-permute-start | bytes 589832 | tf_op jit(solution)/shard_map/ppermute | solution.py:287
  11.3 4.2 %collective-permute-done.6.r_e = bf16[256,768]{1,0:T(8,128)(2,1)S(1)} collective-permute-done((bf16[256,768]{1,0:T(8,128)(2,1)S(1)}, bf16[256,768]{1,0:T(8,128)(2,1)S(1)}, u32[]{:S(2)}, u32[]{:S(2)}) %collective-permute-start.6) | collective-permute-done | bytes 393248 | tf_op jit(solution)/shard_map/ppermute | solution.py:287
  15.5 2.1 %collective-permute-start.8 = (bf16[128,768]{1,0:T(8,128)(2,1)S(1)}, bf16[128,768]{1,0:T(8,128)(2,1)S(1)}, u32[]{:S(2)}, u32[]{:S(2)}) collective-permute-start(bf16[128,768]{1,0:T(8,128)(2,1)S(1)} %get-tuple-element.50.v_own), channel_id=1, source_target_pairs={{0,4},{1,5},{2,6},{3,7},{4,0},{5,1},{6,2},{7,3},{8,12},{9,13},{10,... | collective-permute-start | bytes 589832 | tf_op jit(solution)/shard_map/ppermute | solution.py:287
  17.6 0.0 collective-permute-done.7.q_x
  17.6 0.0 collective-permute-done.5.r_o
  17.6 0.7 %far.1 = bf16[800,128]{1,0:T(8,128)(2,1)S(1)} custom-call(bf16[256,768]{1,0:T(8,128)(2,1)S(1)} %get-tuple-element.35.first, bf16[256,768]{1,0:T(8,128)(2,1)S(1)} %collective-permute-done.6.r_e, bf16[256,768]{1,0:T(8,128)(2,1)S(1)} %collective-permute-done.5.r_o, bf16[144,768]{1,0:T(8,128)(2,1)S(1)} %collective-permute-done.7.q_x), custom_call_target="tpu_custom_call" | custom-call | tf_op jit(solution)/shard_map/far/pallas_call | solution.py:340
  18.3 1.6 %collective-permute-start.10 = (bf16[800,128]{1,0:T(8,128)(2,1)S(1)}, bf16[800,128]{1,0:T(8,128)(2,1)S(1)}, u32[]{:S(2)}, u32[]{:S(2)}) collective-permute-start(bf16[800,128]{1,0:T(8,128)(2,1)S(1)} %far.1), channel_id=1, source_target_pairs={{0,2},{2,0},{4,6},{6,4},{8,10},{10,8},{12,14},{14,12},{1,3},{3,1},... | collective-permute-start | bytes 614408 | tf_op jit(solution)/shard_map/ppermute | solution.py:290
  19.9 0.0 collective-permute-start.9
  19.9 1.1 %middle.1 = (f32[768,256]{1,0:T(8,128)S(1)}, f32[2,32,128]{2,1,0:T(8,128)S(1)}) custom-call(f32[24,128]{1,0:T(8,128)S(1)} %get-tuple-element.33.bias, bf16[256,768]{1,0:T(8,128)(2,1)S(1)} %get-tuple-element.35.first, bf16[256,768]{1,0:T(8,128)(2,1)S(1)} %collective-permute-done.6.r_e, bf16[256,768]{1,0:T(8,128)(2,1)S(1)} %collective-permute-done.5.r_o, ...), custom_call_target="tpu_custom_call" | custom-call | flops 1000000000 | tf_op jit(solution)/shard_map/middle/pallas_call | solution.py:344
  21.0 0.0 collective-permute-done.3.k_o
  21.0 0.0 collective-permute-done.4.k_e
  21.0 0.9 %outer_scores.1 = (bf16[6,384,256]{2,1,0:T(8,128)(2,1)S(1)}, f32[2,32,128]{2,1,0:T(8,128)S(1)}) custom-call(f32[24,128]{1,0:T(8,128)S(1)} %get-tuple-element.33.bias, bf16[128,768]{1,0:T(8,128)(2,1)S(1)} %get-tuple-element.34.k_own, bf16[128,768]{1,0:T(8,128)(2,1)S(1)} %collective-permute-done.4.k_e, bf16[128,768]{1,0:T(8,128)(2,1)S(1)} %collective-permute-done.3.k_o, ...), custom_call_target="tpu_custom_call" | custom-call | flops 1000000000 | tf_op jit(solution)/shard_map/outer_scores/pallas_call | solution.py:348
  21.9 1.6 %collective-permute-done.8.v_e = bf16[128,768]{1,0:T(8,128)(2,1)S(1)} collective-permute-done((bf16[128,768]{1,0:T(8,128)(2,1)S(1)}, bf16[128,768]{1,0:T(8,128)(2,1)S(1)}, u32[]{:S(2)}, u32[]{:S(2)}) %collective-permute-start.8) | collective-permute-done | bytes 196640 | tf_op jit(solution)/shard_map/ppermute | solution.py:287
  23.5 0.3 %outer_values.1.acc_o = f32[768,256]{1,0:T(8,128)S(1)} custom-call(bf16[6,384,256]{2,1,0:T(8,128)(2,1)S(1)} %get-tuple-element.45.p, bf16[128,768]{1,0:T(8,128)(2,1)S(1)} %get-tuple-element.50.v_own, bf16[128,768]{1,0:T(8,128)(2,1)S(1)} %collective-permute-done.8.v_e), custom_call_target="tpu_custom_call" | custom-call | flops 1000000000 | tf_op jit(solution)/shard_map/outer_values/pallas_call | solution.py:352
  23.8 0.0 collective-permute-done.9.v_o
  23.8 0.3 %collective-permute-done.10.x = bf16[800,128]{1,0:T(8,128)(2,1)S(1)} collective-permute-done((bf16[800,128]{1,0:T(8,128)(2,1)S(1)}, bf16[800,128]{1,0:T(8,128)(2,1)S(1)}, u32[]{:S(2)}, u32[]{:S(2)}) %collective-permute-start.10) | collective-permute-done | bytes 204832 | tf_op jit(solution)/shard_map/ppermute | solution.py:290
  24.2 0.3 %finish_sibling.1 = bf16[128,768]{1,0:T(8,128)(2,1)S(1)} custom-call(bf16[6,384,256]{2,1,0:T(8,128)(2,1)S(1)} %get-tuple-element.45.p, f32[2,32,128]{2,1,0:T(8,128)S(1)} %get-tuple-element.42.st_i, f32[2,32,128]{2,1,0:T(8,128)S(1)} %get-tuple-element.46.st_o, f32[768,256]{1,0:T(8,128)S(1)} %get-tuple-element.52.acc, f32[768,256]{1,0:T(8,128)S(1)} %outer_values.1.acc_o, ...), custom_call_target="tpu_custom_call" | custom-call | tf_op jit(solution)/shard_map/finish_sibling/pallas_call | solution.py:355
  24.5 0.1 collective-permute-start.11
  24.6 0.4 %finish_own.1.own = bf16[128,768]{1,0:T(8,128)(2,1)S(1)} custom-call(bf16[6,384,256]{2,1,0:T(8,128)(2,1)S(1)} %get-tuple-element.45.p, f32[2,32,128]{2,1,0:T(8,128)S(1)} %get-tuple-element.42.st_i, f32[2,32,128]{2,1,0:T(8,128)S(1)} %get-tuple-element.46.st_o, f32[768,256]{1,0:T(8,128)S(1)} %get-tuple-element.52.acc, f32[768,256]{1,0:T(8,128)S(1)} %outer_values.1.acc_o, ...), custom_call_target="tpu_custom_call" | custom-call | tf_op jit(solution)/shard_map/finish_own/pallas_call | solution.py:359
  24.9 1.1 %collective-permute-done.11.back = bf16[128,768]{1,0:T(8,128)(2,1)S(1)} collective-permute-done((bf16[128,768]{1,0:T(8,128)(2,1)S(1)}, bf16[128,768]{1,0:T(8,128)(2,1)S(1)}, u32[]{:S(2)}, u32[]{:S(2)}) %collective-permute-start.11) | collective-permute-done | bytes 196640 | tf_op jit(solution)/shard_map/ppermute | solution.py:293
  26.0 0.8 %put.1 = bf16[128,1536]{1,0:T(8,128)(2,1)} custom-call(bf16[128,768]{1,0:T(8,128)(2,1)S(1)} %finish_own.1.own, bf16[128,768]{1,0:T(8,128)(2,1)S(1)} %collective-permute-done.11.back), custom_call_target="tpu_custom_call" | custom-call | tf_op jit(solution)/shard_map/put/pallas_call | solution.py:360
Async XLA Ops:
  0.0 2.0 %collective-permute-start.1 = (bf16[128,1536]{1,0:T(8,128)(2,1)}, bf16[128,1536]{1,0:T(8,128)(2,1)S(1)}, u32[]{:S(2)}, u32[]{:S(2)}) collective-permute-start(bf16[128,1536]{1,0:T(8,128)(2,1)} %k_hbm.1), channel_id=1, source_target_pairs={{0,1},{1,0},{2,3},{3,2},{4,5},{5,4},{6,7},{7,6},{8,9},{9,8},{10,11... | collective-permute-start | bytes 1179656 | tf_op jit(solution)/shard_map/ppermute | solution.py:293
  0.5 2.1 %collective-permute-start.2 = (bf16[128,1536]{1,0:T(8,128)(2,1)}, bf16[128,1536]{1,0:T(8,128)(2,1)S(1)}, u32[]{:S(2)}, u32[]{:S(2)}) collective-permute-start(bf16[128,1536]{1,0:T(8,128)(2,1)} %v_hbm.1), channel_id=1, source_target_pairs={{0,1},{1,0},{2,3},{3,2},{4,5},{5,4},{6,7},{7,6},{8,9},{9,8},{10,11... | collective-permute-start | bytes 1179656 | tf_op jit(solution)/shard_map/ppermute | solution.py:293
  0.5 5.1 %collective-permute-start = (bf16[128,1536]{1,0:T(8,128)(2,1)}, bf16[128,1536]{1,0:T(8,128)(2,1)S(1)}, u32[]{:S(2)}, u32[]{:S(2)}) collective-permute-start(bf16[128,1536]{1,0:T(8,128)(2,1)} %q_hbm.1), channel_id=1, source_target_pairs={{0,1},{1,0},{2,3},{3,2},{4,5},{5,4},{6,7},{7,6},{8,9},{9,8},{10,11... | collective-permute-start | bytes 1179656 | tf_op jit(solution)/shard_map/ppermute | solution.py:293
  2.6 12.9 %collective-permute-start.6 = (bf16[256,768]{1,0:T(8,128)(2,1)S(1)}, bf16[256,768]{1,0:T(8,128)(2,1)S(1)}, u32[]{:S(2)}, u32[]{:S(2)}) collective-permute-start(bf16[256,768]{1,0:T(8,128)(2,1)S(1)} %get-tuple-element.35.first), channel_id=1, source_target_pairs={{0,4},{1,5},{2,6},{3,7},{4,0},{5,1},{6,2},{7,3},{8,12},{9,13},{10,... | collective-permute-start | bytes 1179656 | tf_op jit(solution)/shard_map/ppermute | solution.py:287
  5.6 12.0 %collective-permute-start.5 = (bf16[256,768]{1,0:T(8,128)(2,1)S(1)}, bf16[256,768]{1,0:T(8,128)(2,1)S(1)}, u32[]{:S(2)}, u32[]{:S(2)}) collective-permute-start(bf16[256,768]{1,0:T(8,128)(2,1)S(1)} %get-tuple-element.35.first), channel_id=1, source_target_pairs={{0,1},{1,0},{2,3},{3,2},{4,8},{5,9},{6,10},{7,11},{8,4},{9,5},{10,... | collective-permute-start | bytes 1179656 | tf_op jit(solution)/shard_map/ppermute | solution.py:287
  6.6 11.0 %collective-permute-start.7 = (bf16[144,768]{1,0:T(8,128)(2,1)S(1)}, bf16[144,768]{1,0:T(8,128)(2,1)S(1)}, u32[]{:S(2)}, u32[]{:S(2)}) collective-permute-start(bf16[144,768]{1,0:T(8,128)(2,1)S(1)} %get-tuple-element.38.q_i), channel_id=1, source_target_pairs={{0,2},{2,0},{4,6},{6,4},{8,10},{10,8},{12,14},{14,12},{1,3},{3,1},... | collective-permute-start | bytes 663560 | tf_op jit(solution)/shard_map/ppermute | solution.py:290
  8.2 12.8 %collective-permute-start.3 = (bf16[128,768]{1,0:T(8,128)(2,1)S(1)}, bf16[128,768]{1,0:T(8,128)(2,1)S(1)}, u32[]{:S(2)}, u32[]{:S(2)}) collective-permute-start(bf16[128,768]{1,0:T(8,128)(2,1)S(1)} %get-tuple-element.34.k_own), channel_id=1, source_target_pairs={{0,1},{1,0},{2,3},{3,2},{4,8},{5,9},{6,10},{7,11},{8,4},{9,5},{10,... | collective-permute-start | bytes 589832 | tf_op jit(solution)/shard_map/ppermute | solution.py:287
  8.4 12.6 %collective-permute-start.4 = (bf16[128,768]{1,0:T(8,128)(2,1)S(1)}, bf16[128,768]{1,0:T(8,128)(2,1)S(1)}, u32[]{:S(2)}, u32[]{:S(2)}) collective-permute-start(bf16[128,768]{1,0:T(8,128)(2,1)S(1)} %get-tuple-element.34.k_own), channel_id=1, source_target_pairs={{0,4},{1,5},{2,6},{3,7},{4,0},{5,1},{6,2},{7,3},{8,12},{9,13},{10,... | collective-permute-start | bytes 589832 | tf_op jit(solution)/shard_map/ppermute | solution.py:287
  15.5 7.9 %collective-permute-start.8 = (bf16[128,768]{1,0:T(8,128)(2,1)S(1)}, bf16[128,768]{1,0:T(8,128)(2,1)S(1)}, u32[]{:S(2)}, u32[]{:S(2)}) collective-permute-start(bf16[128,768]{1,0:T(8,128)(2,1)S(1)} %get-tuple-element.50.v_own), channel_id=1, source_target_pairs={{0,4},{1,5},{2,6},{3,7},{4,0},{5,1},{6,2},{7,3},{8,12},{9,13},{10,... | collective-permute-start | bytes 589832 | tf_op jit(solution)/shard_map/ppermute | solution.py:287
  18.3 5.8 %collective-permute-start.10 = (bf16[800,128]{1,0:T(8,128)(2,1)S(1)}, bf16[800,128]{1,0:T(8,128)(2,1)S(1)}, u32[]{:S(2)}, u32[]{:S(2)}) collective-permute-start(bf16[800,128]{1,0:T(8,128)(2,1)S(1)} %far.1), channel_id=1, source_target_pairs={{0,2},{2,0},{4,6},{6,4},{8,10},{10,8},{12,14},{14,12},{1,3},{3,1},... | collective-permute-start | bytes 614408 | tf_op jit(solution)/shard_map/ppermute | solution.py:290
  19.9 3.9 %collective-permute-start.9 = (bf16[128,768]{1,0:T(8,128)(2,1)S(1)}, bf16[128,768]{1,0:T(8,128)(2,1)S(1)}, u32[]{:S(2)}, u32[]{:S(2)}) collective-permute-start(bf16[128,768]{1,0:T(8,128)(2,1)S(1)} %get-tuple-element.50.v_own), channel_id=1, source_target_pairs={{0,1},{1,0},{2,3},{3,2},{4,8},{5,9},{6,10},{7,11},{8,4},{9,5},{10,... | collective-permute-start | bytes 589832 | tf_op jit(solution)/shard_map/ppermute | solution.py:287
  24.5 1.5 %collective-permute-start.11 = (bf16[128,768]{1,0:T(8,128)(2,1)S(1)}, bf16[128,768]{1,0:T(8,128)(2,1)S(1)}, u32[]{:S(2)}, u32[]{:S(2)}) collective-permute-start(bf16[128,768]{1,0:T(8,128)(2,1)S(1)} %finish_sibling.1), channel_id=1, source_target_pairs={{0,1},{1,0},{2,3},{3,2},{4,5},{5,4},{6,7},{7,6},{8,9},{9,8},{10,11... | collective-permute-start | bytes 589832 | tf_op jit(solution)/shard_map/ppermute | solution.py:293

commit v5 on v4

--- a/solution.py
+++ b/solution.py
@@ -73,44 +73,17 @@
     return pl.ds(pl.multiple_of((u if mine else 1 - u) * width, HD), width)
 
 
-def cut_kernel(k_hbm, v_hbm, k_own, v_own, sems):
+def cut_kernel(keep_hbm, k_hbm, v_hbm, q_hbm, k_own, v_own, q_own, flags, bias, keep, sems):
+    table = pltpu.make_async_copy(keep_hbm, keep, sems.at[3])
+    table.start()
     columns = my_columns(k_own.shape[1])
     copies = [
-        pltpu.make_async_copy(x.at[:, columns], out, sems.at[n]) for n, (x, out) in enumerate(((k_hbm, k_own), (v_hbm, v_own)))
+        pltpu.make_async_copy(x.at[:, columns], out, sems.at[n])
+        for n, (x, out) in enumerate(((k_hbm, k_own), (v_hbm, v_own), (q_hbm, q_own)))
     ]
     for copy in copies:
         copy.start()
-    for copy in copies:
-        copy.wait()
-
-
-def pack_kernel(k_own, v_own, k_d, v_d, first, k_o, v_o):
-    rows, width = k_own.shape
-
-    columns = my_columns(width)
-
-    def middle():
-        first[:rows, :] = k_own[...]
-        first[rows:, :] = v_own[...]
-        k_o[...] = k_d[:, columns]
-        v_o[...] = v_d[:, columns]
-
-    def outer():
-        first[:rows, :] = k_d[:, columns]
-        first[rows:, :] = v_d[:, columns]
-        k_o[...] = k_own[...]
-        v_o[...] = v_own[...]
-
-    by_role(middle, outer)
-
-
-def arrange_kernel(keep_hbm, q_hbm, q_d, q_i, q_o, bias, mine, keep, sems):
-    tokens, width = q_o.shape
-    flags = pltpu.make_async_copy(keep_hbm, keep, sems.at[0])
-    flags.start()
-    copy = pltpu.make_async_copy(q_hbm.at[:, my_columns(width)], mine, sems.at[1])
-    copy.start()
-    flags.wait()
+    table.wait()
     parity, row, inner = place()
     sibling = row + 1 - 2 * lax.rem(row, 2)
     middle_row, outer_row = jnp.where(inner, row, sibling), jnp.where(inner, sibling, row)
@@ -121,16 +94,43 @@
     bias[...] = (jnp.concatenate(rows, axis=0) - 1.0) * -FILL
     rows = flag_rows(keep, parity, TH - 1 - middle_row, middle_row)
     rows += [jnp.zeros((1, HD), jnp.float32)] * (FLAG_ROWS - len(rows))
-    q_i[tokens:, :HD] = jnp.concatenate(rows, axis=0).astype(q_i.dtype)
-    copy.wait()
+    flags[...] = jnp.concatenate(rows, axis=0).astype(flags.dtype)
+    for copy in copies:
+        copy.wait()
+
+
+def pack_kernel(k_own, v_own, k_d, v_d, first, k_o, v_o):
+    rows, width = k_own.shape
+
+    columns = my_columns(width)
 
     def middle():
-        q_i[:tokens, :] = mine[...]
-        q_o[...] = q_d[:, my_columns(width)]
+        first[:rows, :] = k_own[...]
+        first[rows:, :] = v_own[...]
+        k_o[...] = k_d[:, columns]
+        v_o[...] = v_d[:, columns]
 
     def outer():
-        q_i[:tokens, :] = q_d[:, my_columns(width)]
-        q_o[...] = mine[...]
+        first[:rows, :] = k_d[:, columns]
+        first[rows:, :] = v_d[:, columns]
+        k_o[...] = k_own[...]
+        v_o[...] = v_own[...]
+
+    by_role(middle, outer)
+
+
+def arrange_kernel(flags, q_own, q_d, q_i, q_o):
+    tokens, width = q_o.shape
+    columns = my_columns(width)
+    q_i[tokens:, :HD] = flags[...]
+
+    def middle():
+        q_i[:tokens, :] = q_own[...]
+        q_o[...] = q_d[:, columns]
+
+    def outer():
+        q_i[:tokens, :] = q_d[:, columns]
+        q_o[...] = q_own[...]
 
     by_role(middle, outer)
 
@@ -149,34 +149,38 @@
     return [[bias[n : n + 1, :] for n in range(at, at + count)] for at in (2 * keys * count, (2 * keys + 1) * count)]
 
 
-def far_kernel(first, r_e, r_o, q_x, o_x):
+def join_kernel(first, r_e, keys, values):
     rows = first.shape[0] // 2
-    heads = first.shape[1] // HD
+    for out, at in ((keys, 0), (values, rows)):
+        for n, part in enumerate((first, r_e)):
+            out[n * rows : (n + 1) * rows, :] = part[at : at + rows, :]
+
+
+def far_kernel(keys, values, r_o, q_x, o_x):
+    rows = r_o.shape[0] // 2
     flags = (q_x[rows:, :HD].astype(jnp.float32) - 1.0) * -FILL
     flags = [flags[n : n + 1] for n in range(3 * TW)]
     peaks, totals = [], []
-    for h in range(heads):
-        cols = pl.ds(h * HD, HD)
-        p, m, total = softmax_part(
-            q_x[:rows, cols], jnp.concatenate([x[:rows, cols] for x in (first, r_e, r_o)], axis=0), flags
-        )
-        o = weigh(jnp.concatenate([x[rows:, cols] for x in (first, r_e, r_o)], axis=0), p)
+    for h in range(keys.shape[1] // HD):
+        cols = pl.ds(h * HD, HD)
+        p, m, total = softmax_part(q_x[:rows, cols], jnp.concatenate([keys[:, cols], r_o[:rows, cols]], axis=0), flags)
+        o = weigh(jnp.concatenate([values[:, cols], r_o[rows:, cols]], axis=0), p)
         o_x[cols, :] = (o / total).astype(o_x.dtype)
         peaks.append(m)
         totals.append(total)
     put_stats(o_x, jnp.concatenate(peaks, axis=0), jnp.concatenate(totals, axis=0))
 
 
-def middle_kernel(bias, first, r_e, r_o, q_i, q_o, acc, st):
-    rows = first.shape[0] // 2
+def middle_kernel(bias, keys, values, r_o, q_i, q_o, acc, st):
+    rows = r_o.shape[0] // 2
     flags = bias_rows(bias, 0)
-    for h in range(first.shape[1] // HD):
-        cols = pl.ds(h * HD, HD)
-        keys = jnp.concatenate([x[:rows, cols] for x in (first, r_e, r_o)], axis=0)
-        values = jnp.concatenate([x[rows:, cols] for x in (first, r_e, r_o)], axis=0)
+    for h in range(keys.shape[1] // HD):
+        cols = pl.ds(h * HD, HD)
+        every_key = jnp.concatenate([keys[:, cols], r_o[:rows, cols]], axis=0)
+        every_value = jnp.concatenate([values[:, cols], r_o[rows:, cols]], axis=0)
         for src, q in enumerate((q_i, q_o)):
-            p, m, total = softmax_part(q[:rows, cols], keys, flags[src])
-            acc[cols, src * HD : (src + 1) * HD] = weigh(values, p)
+            p, m, total = softmax_part(q[:rows, cols], every_key, flags[src])
+            acc[cols, src * HD : (src + 1) * HD] = weigh(every_value, p)
             st[src, h : h + 1, :] = m
             st[src, STAT + h : STAT + h + 1, :] = total
 
@@ -240,7 +244,13 @@
         acc[cols, :] = weigh(jnp.concatenate([v_own[:, cols], v_e[:, cols]], axis=0), p[h, : 2 * rows, :])
 
 
-def finish_kernel(mine, p, st_i, st_o, acc, acc_o, v_o, x, out):
+def turn_kernel(v, out):
+    for h in range(v.shape[1] // HD):
+        cols = pl.ds(h * HD, HD)
+        out[cols, :] = v[:, cols].T
+
+
+def finish_kernel(mine, p, st_i, st_o, acc, acc_o, v_t, x, out):
     heads = p.shape[0]
 
     def run(src):
@@ -253,7 +263,8 @@
         lanes = slice(src * HD, (src + 1) * HD)
         for h in range(heads):
             cols = pl.ds(h * HD, HD)
-            rest = acc_o[cols, lanes] + weigh(v_o[:, cols], p[h, 2 * v_o.shape[0] :, lanes])
+            rest = jnp.dot(v_t[cols, :], p[h, 2 * v_t.shape[1] :, lanes], preferred_element_type=jnp.float32)
+            rest = acc_o[cols, lanes] + rest
             o = acc[cols, lanes] * scale[0][h : h + 1] + rest * scale[1][h : h + 1]
             if src == 0:
                 o = o + x[cols, :].astype(jnp.float32) * scale[2][h : h + 1]
@@ -315,34 +326,38 @@
     stats = array(f32, 2, 2 * STAT, rows)
 
     k_d, v_d, q_d = swap(key), swap(value), swap(query)
-    k_own, v_own = call(cut_kernel, "cut", 1, [hbm] * 2, [part] * 2, [dma((2,))])(in_hbm(key), in_hbm(value))
+    k_own, v_own, q_own, flags, bias = call(
+        cut_kernel,
+        "cut",
+        1,
+        [hbm] * 4,
+        [part, part, part, array(bf16, FLAG_ROWS, HD), array(f32, 12 * TW, HD)],
+        [pltpu.SMEM(keep.shape, keep.dtype), dma((4,))],
+    )(in_hbm(keep), in_hbm(key), in_hbm(value), in_hbm(query))
     first, k_o, v_o = call(pack_kernel, "pack", 0, [vmem] * 4, [array(bf16, 2 * rows, half), part, part])(
         k_own, v_own, k_d, v_d
     )
 
     r_o, r_e = exchange(first, 1), exchange(first, 0)
     q_d, _ = lax.optimization_barrier((q_d, k_o))
-    q_i, q_o, bias = call(
-        arrange_kernel,
-        "arrange",
-        0,
-        [hbm, hbm, vmem],
-        [array(bf16, rows + FLAG_ROWS, half), part, array(f32, 12 * TW, HD)],
-        [pltpu.VMEM((rows, half), bf16), pltpu.SMEM(keep.shape, keep.dtype), dma((2,))],
-    )(in_hbm(keep), in_hbm(query), q_d)
+    q_i, q_o = call(arrange_kernel, "arrange", 0, [vmem] * 3, [array(bf16, rows + FLAG_ROWS, half), part])(
+        flags, q_own, q_d
+    )
     q_x = across(q_i)
 
-    k_late, _ = lax.optimization_barrier((k_o, bias))
+    k_late, _ = lax.optimization_barrier((k_o, q_o))
     ko_o, ko_e = exchange(k_late, 1), exchange(k_late, 0)
 
-    v_even, r_e = lax.optimization_barrier((v_o, r_e))
+    v_even, q_x = lax.optimization_barrier((v_o, q_x))
     vo_e = exchange(v_even, 0)
-    x = call(far_kernel, "far", 0, [vmem] * 4, array(bf16, half + stat_rows(heads), rows))(first, r_e, r_o, q_x)
-    v_odd, r_o, r_e, _ = lax.optimization_barrier((v_o, r_o, r_e, x))
+    v_odd, r_e = lax.optimization_barrier((v_o, r_e))
+    vo_o = exchange(v_odd, 1)
+    keys, values = call(join_kernel, "join", 0.1, [vmem] * 2, [array(bf16, 2 * rows, half)] * 2)(first, r_e)
+    r_o, _ = lax.optimization_barrier((r_o, values))
+    x = call(far_kernel, "far", 0, [vmem] * 4, array(bf16, half + stat_rows(heads), rows))(keys, values, r_o, q_x)
     x = across(x)
-    vo_o = exchange(v_odd, 1)
-    acc, st_i = call(middle_kernel, "middle", 1, [vmem] * 6, [array(f32, half, 2 * rows), stats])(
-        bias, first, r_e, r_o, q_i, q_o
+    acc, st_i = call(middle_kernel, "middle", 0, [vmem] * 6, [array(f32, half, 2 * rows), stats])(
+        bias, keys, values, r_o, q_i, q_o
     )
     ko_o, ko_e, _ = lax.optimization_barrier((ko_o, ko_e, st_i))
     p_o, st_o = call(outer_scores_kernel, "outer_scores", 1, [vmem] * 6, [array(bf16, heads, 3 * rows, 2 * rows), stats])(
@@ -351,11 +366,12 @@
     vo_e, _ = lax.optimization_barrier((vo_e, st_o))
     acc_o = call(outer_values_kernel, "outer_values", 1, [vmem] * 3, array(f32, half, 2 * rows))(p_o, v_o, vo_e)
     vo_o, _ = lax.optimization_barrier((vo_o, acc_o))
-    parts = p_o, st_i, st_o, acc, acc_o, vo_o, x
+    v_t = call(turn_kernel, "turn", 2, [vmem], array(bf16, half, rows))(vo_o)
+    parts = p_o, st_i, st_o, acc, acc_o, v_t, x
     out_sib = call(functools.partial(finish_kernel, False), "finish_sibling", 0, [vmem] * 7, part)(*parts)
     back = swap(out_sib)
     acc, _ = lax.optimization_barrier((acc, out_sib))
-    parts = p_o, st_i, st_o, acc, acc_o, vo_o, x
+    parts = p_o, st_i, st_o, acc, acc_o, v_t, x
     out_own = call(functools.partial(finish_kernel, True), "finish_own", 0, [vmem] * 7, part)(*parts)
     return call(put_kernel, "put", 0, [vmem] * 2, array(query.dtype, rows, width), [dma((2,))], hbm)(out_own, back)
 

time: 27.2 us -> 26.9 us (0.989); the launches traced: 26.8 us -> 26.7 us
  Pallas kernels: 6.49 us -> 5.74 us
  starting transfers between devices: 12.4 us -> 12.8 us
  waiting for transfers between devices: 7.79 us -> 8.13 us
    ppermute x2, waiting for transfers between devices: 0.34 us -> 3.43 us  [across(): return lax.ppermute(x, 'blk', chip_pairs(n_blk, n_uly))]
    ppermute x6, waiting for transfers between devices: 5.83 us -> 3.14 us  [exchange(): return lax.ppermute(x, ('blk', 'uly'), plane_pairs(n_blk, n_uly, parity))]
    pallas_call x3 -> x5, Pallas kernels: 3.08 us -> 2.4 us  [the longest x1 1.15 us: body(): call(cut_kernel, 'cut', 1, [hbm] * 4, [part, part, part, array(bf16, FLAG...]
  transfers between devices with their start and end apart: 12 -> 12, of which waited for: 5 -> 6; matrix products, arithmetic and copies ran while one was open for 0% -> 0% of each run, Pallas kernels for 20% -> 18%
where the time goes in v5:
time: 26.9 us; the launch traced here: 26.7 us
  starting transfers between devices  12.8 us (48%)
  waiting for transfers between devices  8.13 us (30%)
  Pallas kernels  5.74 us (21%)
    ppermute x6, starting transfers between devices, exchange(): return lax.ppermute(x, ('blk', 'uly'), plane_pairs(n_blk, n_uly, parity))  8.39 us
    ppermute x2, waiting for transfers between devices, across(): return lax.ppermute(x, 'blk', chip_pairs(n_blk, n_uly))  3.43 us
    ppermute x2, starting transfers between devices, across(): return lax.ppermute(x, 'blk', chip_pairs(n_blk, n_uly))  3.33 us
    ppermute x6, waiting for transfers between devices, exchange(): return lax.ppermute(x, ('blk', 'uly'), plane_pairs(n_blk, n_uly, parity))  3.14 us
    ppermute x4, waiting for transfers between devices, swap(): return lax.ppermute(x, 'uly', cores)  1.55 us
    pallas_call x1, Pallas kernels, body(): call(cut_kernel, 'cut', 1, [hbm] * 4, [part, part, part, array(bf16, FLAG...  1.15 us
    pallas_call x1, Pallas kernels, body(): call(middle_kernel, 'middle', 0, [vmem] * 6, [array(f32, half, 2 * rows),...  1.07 us
    ppermute x4, starting transfers between devices, swap(): return lax.ppermute(x, 'uly', cores)  1.03 us
  transfers between devices with their start and end apart: 12, of which 6 were waited for; matrix products, arithmetic and copies ran while one was open for 0% of the time, Pallas kernels for 18%

profile of v5, /device:TPU:0, one launch (start us, length us, event | category | flops | bytes accessed | tf_op | source)
XLA Modules:
  0.0 26.7 jit_solution(11826565786086849042)
XLA Ops:
  0.0 0.5 %collective-permute-start = (bf16[128,1536]{1,0:T(8,128)(2,1)}, bf16[128,1536]{1,0:T(8,128)(2,1)S(1)}, u32[]{:S(2)}, u32[]{:S(2)}) collective-permute-start(bf16[128,1536]{1,0:T(8,128)(2,1)} %k_hbm.1), channel_id=1, source_target_pairs={{0,1},{1,0},{2,3},{3,2},{4,5},{5,4},{6,7},{7,6},{8,9},{9,8},{10,11... | collective-permute-start | bytes 1179656 | tf_op jit(solution)/shard_map/ppermute | solution.py:304
  0.5 0.1 collective-permute-start.1
  0.5 0.5 %collective-permute-start.2 = (bf16[128,1536]{1,0:T(8,128)(2,1)}, bf16[128,1536]{1,0:T(8,128)(2,1)S(1)}, u32[]{:S(2)}, u32[]{:S(2)}) collective-permute-start(bf16[128,1536]{1,0:T(8,128)(2,1)} %q_hbm.1), channel_id=1, source_target_pairs={{0,1},{1,0},{2,3},{3,2},{4,5},{5,4},{6,7},{7,6},{8,9},{9,8},{10,11... | collective-permute-start | bytes 1179656 | tf_op jit(solution)/shard_map/ppermute | solution.py:304
  1.0 1.1 %cut.1 = (bf16[128,768]{1,0:T(8,128)(2,1)S(1)}, bf16[128,768]{1,0:T(8,128)(2,1)S(1)}, bf16[128,768]{1,0:T(8,128)(2,1)S(1)}, bf16[16,128]{1,0:T(8,128)(2,1)S(1)}, f32[24,128]{1,0:T(8,128)S(1)}) custom-call(s32[4,28]{1,0:T(4,128)} %keep_hbm.1, bf16[128,1536]{1,0:T(8,128)(2,1)} %k_hbm.1, bf16[128,1536]{1,0:T(8,128)(2,1)} %v_hbm.1, bf16[128,1536]{1,0:T(8,128)(2,1)} %q_hbm.1), custom_call_target="tpu_custom_call" | custom-call | flops 1000000000 | tf_op jit(solution)/shard_map/cut/pallas_call | solution.py:329
  2.1 0.0 collective-permute-done.k_d
  2.1 0.4 %collective-permute-done.1.v_d = bf16[128,1536]{1,0:T(8,128)(2,1)S(1)} collective-permute-done((bf16[128,1536]{1,0:T(8,128)(2,1)}, bf16[128,1536]{1,0:T(8,128)(2,1)S(1)}, u32[]{:S(2)}, u32[]{:S(2)}) %collective-permute-start.1) | collective-permute-done | bytes 393248 | tf_op jit(solution)/shard_map/ppermute | solution.py:304
  2.6 0.1 pack.1
  2.6 3.0 %collective-permute-start.5 = (bf16[256,768]{1,0:T(8,128)(2,1)S(1)}, bf16[256,768]{1,0:T(8,128)(2,1)S(1)}, u32[]{:S(2)}, u32[]{:S(2)}) collective-permute-start(bf16[256,768]{1,0:T(8,128)(2,1)S(1)} %get-tuple-element.42.first), channel_id=1, source_target_pairs={{0,4},{1,5},{2,6},{3,7},{4,0},{5,1},{6,2},{7,3},{8,12},{9,13},{10,... | collective-permute-start | bytes 1179656 | tf_op jit(solution)/shard_map/ppermute | solution.py:298
  5.6 0.0 collective-permute-start.6
  5.6 0.0 collective-permute-done.2.q_d
  5.7 1.6 %collective-permute-start.7 = (bf16[144,768]{1,0:T(8,128)(2,1)S(1)}, bf16[144,768]{1,0:T(8,128)(2,1)S(1)}, u32[]{:S(2)}, u32[]{:S(2)}) collective-permute-start(bf16[144,768]{1,0:T(8,128)(2,1)S(1)} %get-tuple-element.48.q_i), channel_id=1, source_target_pairs={{0,2},{2,0},{4,6},{6,4},{8,10},{10,8},{12,14},{14,12},{1,3},{3,1},... | collective-permute-start | bytes 663560 | tf_op jit(solution)/shard_map/ppermute | solution.py:301
  7.2 0.2 collective-permute-start.3
  7.5 2.9 %collective-permute-start.4 = (bf16[128,768]{1,0:T(8,128)(2,1)S(1)}, bf16[128,768]{1,0:T(8,128)(2,1)S(1)}, u32[]{:S(2)}, u32[]{:S(2)}) collective-permute-start(bf16[128,768]{1,0:T(8,128)(2,1)S(1)} %get-tuple-element.41.k_own), channel_id=1, source_target_pairs={{0,4},{1,5},{2,6},{3,7},{4,0},{5,1},{6,2},{7,3},{8,12},{9,13},{10,... | collective-permute-start | bytes 589832 | tf_op jit(solution)/shard_map/ppermute | solution.py:298
  10.4 3.2 %collective-permute-done.7.q_x = bf16[144,768]{1,0:T(8,128)(2,1)S(1)} collective-permute-done((bf16[144,768]{1,0:T(8,128)(2,1)S(1)}, bf16[144,768]{1,0:T(8,128)(2,1)S(1)}, u32[]{:S(2)}, u32[]{:S(2)}) %collective-permute-start.7) | collective-permute-done | bytes 221216 | tf_op jit(solution)/shard_map/ppermute | solution.py:301
  13.6 2.2 %collective-permute-start.8 = (bf16[128,768]{1,0:T(8,128)(2,1)S(1)}, bf16[128,768]{1,0:T(8,128)(2,1)S(1)}, u32[]{:S(2)}, u32[]{:S(2)}) collective-permute-start(bf16[128,768]{1,0:T(8,128)(2,1)S(1)} %get-tuple-element.57.v_own), channel_id=1, source_target_pairs={{0,4},{1,5},{2,6},{3,7},{4,0},{5,1},{6,2},{7,3},{8,12},{9,13},{10,... | collective-permute-start | bytes 589832 | tf_op jit(solution)/shard_map/ppermute | solution.py:298
  15.8 0.0 collective-permute-done.5.r_e
  15.8 0.0 collective-permute-start.9
  15.8 0.1 join.1
  15.9 0.0 collective-permute-done.6.r_o
  15.9 0.7 %far.1 = bf16[800,128]{1,0:T(8,128)(2,1)S(1)} custom-call(bf16[256,768]{1,0:T(8,128)(2,1)S(1)} %get-tuple-element.45.keys, bf16[256,768]{1,0:T(8,128)(2,1)S(1)} %get-tuple-element.46.values, bf16[256,768]{1,0:T(8,128)(2,1)S(1)} %collective-permute-done.6.r_o, bf16[144,768]{1,0:T(8,128)(2,1)S(1)} %collective-permute-done.7.q_x), custom_call_target="tpu_custom_call" | custom-call | tf_op jit(solution)/shard_map/far/pallas_call | solution.py:357
  16.6 1.8 %collective-permute-start.10 = (bf16[800,128]{1,0:T(8,128)(2,1)S(1)}, bf16[800,128]{1,0:T(8,128)(2,1)S(1)}, u32[]{:S(2)}, u32[]{:S(2)}) collective-permute-start(bf16[800,128]{1,0:T(8,128)(2,1)S(1)} %far.1), channel_id=1, source_target_pairs={{0,2},{2,0},{4,6},{6,4},{8,10},{10,8},{12,14},{14,12},{1,3},{3,1},... | collective-permute-start | bytes 614408 | tf_op jit(solution)/shard_map/ppermute | solution.py:301
  18.4 1.1 %middle.1 = (f32[768,256]{1,0:T(8,128)S(1)}, f32[2,32,128]{2,1,0:T(8,128)S(1)}) custom-call(f32[24,128]{1,0:T(8,128)S(1)} %get-tuple-element.33.bias, bf16[256,768]{1,0:T(8,128)(2,1)S(1)} %get-tuple-element.45.keys, bf16[256,768]{1,0:T(8,128)(2,1)S(1)} %get-tuple-element.46.values, bf16[256,768]{1,0:T(8,128)(2,1)S(1)} %collective-permute-done.6.r_o, ...), custom_call_target="tpu_custom_call" | custom-call | tf_op jit(solution)/shard_map/middle/pallas_call | solution.py:359
  19.5 0.0 collective-permute-done.3.k_o
  19.5 0.3 %collective-permute-done.4.k_e = bf16[128,768]{1,0:T(8,128)(2,1)S(1)} collective-permute-done((bf16[128,768]{1,0:T(8,128)(2,1)S(1)}, bf16[128,768]{1,0:T(8,128)(2,1)S(1)}, u32[]{:S(2)}, u32[]{:S(2)}) %collective-permute-start.4) | collective-permute-done | bytes 196640 | tf_op jit(solution)/shard_map/ppermute | solution.py:298
  19.8 0.9 %outer_scores.1 = (bf16[6,384,256]{2,1,0:T(8,128)(2,1)S(1)}, f32[2,32,128]{2,1,0:T(8,128)S(1)}) custom-call(f32[24,128]{1,0:T(8,128)S(1)} %get-tuple-element.33.bias, bf16[128,768]{1,0:T(8,128)(2,1)S(1)} %get-tuple-element.41.k_own, bf16[128,768]{1,0:T(8,128)(2,1)S(1)} %collective-permute-done.4.k_e, bf16[128,768]{1,0:T(8,128)(2,1)S(1)} %collective-permute-done.3.k_o, ...), custom_call_target="tpu_custom_call" | custom-call | flops 1000000000 | tf_op jit(solution)/shard_map/outer_scores/pallas_call | solution.py:363
  20.7 2.8 %collective-permute-done.8.v_e = bf16[128,768]{1,0:T(8,128)(2,1)S(1)} collective-permute-done((bf16[128,768]{1,0:T(8,128)(2,1)S(1)}, bf16[128,768]{1,0:T(8,128)(2,1)S(1)}, u32[]{:S(2)}, u32[]{:S(2)}) %collective-permute-start.8) | collective-permute-done | bytes 196640 | tf_op jit(solution)/shard_map/ppermute | solution.py:298
  23.5 0.3 %outer_values.1.acc_o = f32[768,256]{1,0:T(8,128)S(1)} custom-call(bf16[6,384,256]{2,1,0:T(8,128)(2,1)S(1)} %get-tuple-element.52.p, bf16[128,768]{1,0:T(8,128)(2,1)S(1)} %get-tuple-element.57.v_own, bf16[128,768]{1,0:T(8,128)(2,1)S(1)} %collective-permute-done.8.v_e), custom_call_target="tpu_custom_call" | custom-call | flops 1000000000 | tf_op jit(solution)/shard_map/outer_values/pallas_call | solution.py:367
  23.8 0.0 collective-permute-done.9.v
  23.8 0.1 turn.1.v_t
  23.9 0.2 collective-permute-done.10.x
  24.2 0.3 %finish_sibling.1 = bf16[128,768]{1,0:T(8,128)(2,1)S(1)} custom-call(bf16[6,384,256]{2,1,0:T(8,128)(2,1)S(1)} %get-tuple-element.52.p, f32[2,32,128]{2,1,0:T(8,128)S(1)} %get-tuple-element.49.st_i, f32[2,32,128]{2,1,0:T(8,128)S(1)} %get-tuple-element.53.st_o, f32[768,256]{1,0:T(8,128)S(1)} %get-tuple-element.60.acc, f32[768,256]{1,0:T(8,128)S(1)} %outer_values.1.acc_o, ...), custom_call_target="tpu_custom_call" | custom-call | tf_op jit(solution)/shard_map/finish_sibling/pallas_call | solution.py:371
  24.5 0.1 collective-permute-start.11
  24.5 0.3 %finish_own.1.own = bf16[128,768]{1,0:T(8,128)(2,1)S(1)} custom-call(bf16[6,384,256]{2,1,0:T(8,128)(2,1)S(1)} %get-tuple-element.52.p, f32[2,32,128]{2,1,0:T(8,128)S(1)} %get-tuple-element.49.st_i, f32[2,32,128]{2,1,0:T(8,128)S(1)} %get-tuple-element.53.st_o, f32[768,256]{1,0:T(8,128)S(1)} %get-tuple-element.60.acc, f32[768,256]{1,0:T(8,128)S(1)} %outer_values.1.acc_o, ...), custom_call_target="tpu_custom_call" | custom-call | tf_op jit(solution)/shard_map/finish_own/pallas_call | solution.py:375
  24.9 1.1 %collective-permute-done.11.back = bf16[128,768]{1,0:T(8,128)(2,1)S(1)} collective-permute-done((bf16[128,768]{1,0:T(8,128)(2,1)S(1)}, bf16[128,768]{1,0:T(8,128)(2,1)S(1)}, u32[]{:S(2)}, u32[]{:S(2)}) %collective-permute-start.11) | collective-permute-done | bytes 196640 | tf_op jit(solution)/shard_map/ppermute | solution.py:304
  26.0 0.8 %put.1 = bf16[128,1536]{1,0:T(8,128)(2,1)} custom-call(bf16[128,768]{1,0:T(8,128)(2,1)S(1)} %finish_own.1.own, bf16[128,768]{1,0:T(8,128)(2,1)S(1)} %collective-permute-done.11.back), custom_call_target="tpu_custom_call" | custom-call | tf_op jit(solution)/shard_map/put/pallas_call | solution.py:376
  (1 shorter events, 0.0 us)
Async XLA Ops:
  0.0 2.1 %collective-permute-start = (bf16[128,1536]{1,0:T(8,128)(2,1)}, bf16[128,1536]{1,0:T(8,128)(2,1)S(1)}, u32[]{:S(2)}, u32[]{:S(2)}) collective-permute-start(bf16[128,1536]{1,0:T(8,128)(2,1)} %k_hbm.1), channel_id=1, source_target_pairs={{0,1},{1,0},{2,3},{3,2},{4,5},{5,4},{6,7},{7,6},{8,9},{9,8},{10,11... | collective-permute-start | bytes 1179656 | tf_op jit(solution)/shard_map/ppermute | solution.py:304
  0.5 2.1 %collective-permute-start.1 = (bf16[128,1536]{1,0:T(8,128)(2,1)}, bf16[128,1536]{1,0:T(8,128)(2,1)S(1)}, u32[]{:S(2)}, u32[]{:S(2)}) collective-permute-start(bf16[128,1536]{1,0:T(8,128)(2,1)} %v_hbm.1), channel_id=1, source_target_pairs={{0,1},{1,0},{2,3},{3,2},{4,5},{5,4},{6,7},{7,6},{8,9},{9,8},{10,11... | collective-permute-start | bytes 1179656 | tf_op jit(solution)/shard_map/ppermute | solution.py:304
  0.5 5.1 %collective-permute-start.2 = (bf16[128,1536]{1,0:T(8,128)(2,1)}, bf16[128,1536]{1,0:T(8,128)(2,1)S(1)}, u32[]{:S(2)}, u32[]{:S(2)}) collective-permute-start(bf16[128,1536]{1,0:T(8,128)(2,1)} %q_hbm.1), channel_id=1, source_target_pairs={{0,1},{1,0},{2,3},{3,2},{4,5},{5,4},{6,7},{7,6},{8,9},{9,8},{10,11... | collective-permute-start | bytes 1179656 | tf_op jit(solution)/shard_map/ppermute | solution.py:304
  2.6 13.2 %collective-permute-start.5 = (bf16[256,768]{1,0:T(8,128)(2,1)S(1)}, bf16[256,768]{1,0:T(8,128)(2,1)S(1)}, u32[]{:S(2)}, u32[]{:S(2)}) collective-permute-start(bf16[256,768]{1,0:T(8,128)(2,1)S(1)} %get-tuple-element.42.first), channel_id=1, source_target_pairs={{0,4},{1,5},{2,6},{3,7},{4,0},{5,1},{6,2},{7,3},{8,12},{9,13},{10,... | collective-permute-start | bytes 1179656 | tf_op jit(solution)/shard_map/ppermute | solution.py:298
  5.6 10.2 %collective-permute-start.6 = (bf16[256,768]{1,0:T(8,128)(2,1)S(1)}, bf16[256,768]{1,0:T(8,128)(2,1)S(1)}, u32[]{:S(2)}, u32[]{:S(2)}) collective-permute-start(bf16[256,768]{1,0:T(8,128)(2,1)S(1)} %get-tuple-element.42.first), channel_id=1, source_target_pairs={{0,1},{1,0},{2,3},{3,2},{4,8},{5,9},{6,10},{7,11},{8,4},{9,5},{10,... | collective-permute-start | bytes 1179656 | tf_op jit(solution)/shard_map/ppermute | solution.py:298
  5.7 7.9 %collective-permute-start.7 = (bf16[144,768]{1,0:T(8,128)(2,1)S(1)}, bf16[144,768]{1,0:T(8,128)(2,1)S(1)}, u32[]{:S(2)}, u32[]{:S(2)}) collective-permute-start(bf16[144,768]{1,0:T(8,128)(2,1)S(1)} %get-tuple-element.48.q_i), channel_id=1, source_target_pairs={{0,2},{2,0},{4,6},{6,4},{8,10},{10,8},{12,14},{14,12},{1,3},{3,1},... | collective-permute-start | bytes 663560 | tf_op jit(solution)/shard_map/ppermute | solution.py:301
  7.2 12.2 %collective-permute-start.3 = (bf16[128,768]{1,0:T(8,128)(2,1)S(1)}, bf16[128,768]{1,0:T(8,128)(2,1)S(1)}, u32[]{:S(2)}, u32[]{:S(2)}) collective-permute-start(bf16[128,768]{1,0:T(8,128)(2,1)S(1)} %get-tuple-element.41.k_own), channel_id=1, source_target_pairs={{0,1},{1,0},{2,3},{3,2},{4,8},{5,9},{6,10},{7,11},{8,4},{9,5},{10,... | collective-permute-start | bytes 589832 | tf_op jit(solution)/shard_map/ppermute | solution.py:298
  7.5 12.3 %collective-permute-start.4 = (bf16[128,768]{1,0:T(8,128)(2,1)S(1)}, bf16[128,768]{1,0:T(8,128)(2,1)S(1)}, u32[]{:S(2)}, u32[]{:S(2)}) collective-permute-start(bf16[128,768]{1,0:T(8,128)(2,1)S(1)} %get-tuple-element.41.k_own), channel_id=1, source_target_pairs={{0,4},{1,5},{2,6},{3,7},{4,0},{5,1},{6,2},{7,3},{8,12},{9,13},{10,... | collective-permute-start | bytes 589832 | tf_op jit(solution)/shard_map/ppermute | solution.py:298
  13.6 9.9 %collective-permute-start.8 = (bf16[128,768]{1,0:T(8,128)(2,1)S(1)}, bf16[128,768]{1,0:T(8,128)(2,1)S(1)}, u32[]{:S(2)}, u32[]{:S(2)}) collective-permute-start(bf16[128,768]{1,0:T(8,128)(2,1)S(1)} %get-tuple-element.57.v_own), channel_id=1, source_target_pairs={{0,4},{1,5},{2,6},{3,7},{4,0},{5,1},{6,2},{7,3},{8,12},{9,13},{10,... | collective-permute-start | bytes 589832 | tf_op jit(solution)/shard_map/ppermute | solution.py:298
  15.8 8.0 %collective-permute-start.9 = (bf16[128,768]{1,0:T(8,128)(2,1)S(1)}, bf16[128,768]{1,0:T(8,128)(2,1)S(1)}, u32[]{:S(2)}, u32[]{:S(2)}) collective-permute-start(bf16[128,768]{1,0:T(8,128)(2,1)S(1)} %get-tuple-element.57.v_own), channel_id=1, source_target_pairs={{0,1},{1,0},{2,3},{3,2},{4,8},{5,9},{6,10},{7,11},{8,4},{9,5},{10,... | collective-permute-start | bytes 589832 | tf_op jit(solution)/shard_map/ppermute | solution.py:298
  16.6 7.5 %collective-permute-start.10 = (bf16[800,128]{1,0:T(8,128)(2,1)S(1)}, bf16[800,128]{1,0:T(8,128)(2,1)S(1)}, u32[]{:S(2)}, u32[]{:S(2)}) collective-permute-start(bf16[800,128]{1,0:T(8,128)(2,1)S(1)} %far.1), channel_id=1, source_target_pairs={{0,2},{2,0},{4,6},{6,4},{8,10},{10,8},{12,14},{14,12},{1,3},{3,1},... | collective-permute-start | bytes 614408 | tf_op jit(solution)/shard_map/ppermute | solution.py:301
  24.5 1.5 %collective-permute-start.11 = (bf16[128,768]{1,0:T(8,128)(2,1)S(1)}, bf16[128,768]{1,0:T(8,128)(2,1)S(1)}, u32[]{:S(2)}, u32[]{:S(2)}) collective-permute-start(bf16[128,768]{1,0:T(8,128)(2,1)S(1)} %finish_sibling.1), channel_id=1, source_target_pairs={{0,1},{1,0},{2,3},{3,2},{4,5},{5,4},{6,7},{7,6},{8,9},{9,8},{10,11... | collective-permute-start | bytes 589832 | tf_op jit(solution)/shard_map/ppermute | solution.py:304

commit v6 on v5

--- a/solution.py
+++ b/solution.py
@@ -165,7 +165,7 @@
         cols = pl.ds(h * HD, HD)
         p, m, total = softmax_part(q_x[:rows, cols], jnp.concatenate([keys[:, cols], r_o[:rows, cols]], axis=0), flags)
         o = weigh(jnp.concatenate([values[:, cols], r_o[rows:, cols]], axis=0), p)
-        o_x[cols, :] = (o / total).astype(o_x.dtype)
+        o_x[cols, :] = (o * (1.0 / total)).astype(o_x.dtype)
         peaks.append(m)
         totals.append(total)
     put_stats(o_x, jnp.concatenate(peaks, axis=0), jnp.concatenate(totals, axis=0))
@@ -273,16 +273,11 @@
     by_role(lambda: run(0 if mine else 1), lambda: run(1 if mine else 0))
 
 
-def put_kernel(own, back, out, sems):
-    width = own.shape[1]
-    copies = [
-        pltpu.make_async_copy(x, out.at[:, my_columns(width, mine)], sems.at[n])
-        for n, (x, mine) in enumerate(((own, True), (back, False)))
-    ]
-    for copy in copies:
-        copy.start()
-    for copy in copies:
-        copy.wait()
+def put_kernel(mine, x, *refs):
+    out, sem = refs[-2:]
+    copy = pltpu.make_async_copy(x, out.at[:, my_columns(x.shape[1], mine)], sem)
+    copy.start()
+    copy.wait()
 
 
 def body(query, key, value, keep):
@@ -303,13 +298,14 @@
     def swap(x):
         return lax.ppermute(x, "uly", cores)
 
-    def call(kernel, name, us, in_specs, out_shape, scratch=(), out_specs=None):
+    def call(kernel, name, us, in_specs, out_shape, scratch=(), out_specs=None, aliases=None):
         return pl.pallas_call(
             kernel,
             in_specs=in_specs,
             out_specs=out_specs or jax.tree.map(lambda _: vmem, out_shape),
             out_shape=out_shape,
             scratch_shapes=scratch,
+            input_output_aliases=aliases or {},
             compiler_params=pltpu.CompilerParams(vmem_limit_bytes=16 * 1024 * 1024),
             cost_estimate=pl.CostEstimate(flops=int(us * 1e9), bytes_accessed=0, transcendentals=0),
             name=name,
@@ -373,7 +369,9 @@
     acc, _ = lax.optimization_barrier((acc, out_sib))
     parts = p_o, st_i, st_o, acc, acc_o, v_t, x
     out_own = call(functools.partial(finish_kernel, True), "finish_own", 0, [vmem] * 7, part)(*parts)
-    return call(put_kernel, "put", 0, [vmem] * 2, array(query.dtype, rows, width), [dma((2,))], hbm)(out_own, back)
+    out = array(query.dtype, rows, width)
+    mine = call(functools.partial(put_kernel, True), "put_own", 0, [vmem], out, [dma], hbm)(out_own)
+    return call(functools.partial(put_kernel, False), "put_back", 0, [vmem, hbm], out, [dma], hbm, {1: 0})(back, mine)
 
 
 def solution(mesh):

time: 26.9 us -> 26.8 us (level)
  waiting for transfers between devices: 8.13 us -> 7.42 us
  Pallas kernels: 5.74 us -> 6.36 us
    ppermute x4, waiting for transfers between devices: 1.55 us -> 0.85 us  [swap(): return lax.ppermute(x, 'uly', cores)]
    pallas_call x1 -> x2, Pallas kernels: 0.76 us -> 1.38 us  [the longest x1 0.69 us: body(): call(functools.partial(put_kernel, True), 'put_own', 0, [vmem], out, [dma...]
  transfers between devices with their start and end apart: 12 -> 12, of which waited for: 6 -> 6; matrix products, arithmetic and copies ran while one was open for 0% -> 0% of each run, Pallas kernels for 18% -> 20%
where the time goes in v6:
time: 26.8 us; the launch traced here: 26.7 us
  starting transfers between devices  12.8 us (48%)
  waiting for transfers between devices  7.42 us (28%)
  Pallas kernels  6.36 us (24%)
    ppermute x6, starting transfers between devices, exchange(): return lax.ppermute(x, ('blk', 'uly'), plane_pairs(n_blk, n_uly, parity))  8.39 us
    ppermute x2, waiting for transfers between devices, across(): return lax.ppermute(x, 'blk', chip_pairs(n_blk, n_uly))  3.43 us
    ppermute x2, starting transfers between devices, across(): return lax.ppermute(x, 'blk', chip_pairs(n_blk, n_uly))  3.33 us
    ppermute x6, waiting for transfers between devices, exchange(): return lax.ppermute(x, ('blk', 'uly'), plane_pairs(n_blk, n_uly, parity))  3.14 us
    pallas_call x1, Pallas kernels, body(): call(cut_kernel, 'cut', 1, [hbm] * 4, [part, part, part, array(bf16, FLAG...  1.15 us
    pallas_call x1, Pallas kernels, body(): call(middle_kernel, 'middle', 0, [vmem] * 6, [array(f32, half, 2 * rows),...  1.07 us
    ppermute x4, starting transfers between devices, swap(): return lax.ppermute(x, 'uly', cores)  1.03 us
    pallas_call x1, Pallas kernels, body(): call(outer_scores_kernel, 'outer_scores', 1, [vmem] * 6, [array(bf16, hea...  0.89 us
  transfers between devices with their start and end apart: 12, of which 6 were waited for; matrix products, arithmetic and copies ran while one was open for 0% of the time, Pallas kernels for 20%

profile of v6, /device:TPU:0, one launch (start us, length us, event | category | flops | bytes accessed | tf_op | source)
XLA Modules:
  0.0 26.7 jit_solution(9609462975190820183)
XLA Ops:
  0.0 0.5 %collective-permute-start = (bf16[128,1536]{1,0:T(8,128)(2,1)}, bf16[128,1536]{1,0:T(8,128)(2,1)S(1)}, u32[]{:S(2)}, u32[]{:S(2)}) collective-permute-start(bf16[128,1536]{1,0:T(8,128)(2,1)} %k_hbm.1), channel_id=1, source_target_pairs={{0,1},{1,0},{2,3},{3,2},{4,5},{5,4},{6,7},{7,6},{8,9},{9,8},{10,11... | collective-permute-start | bytes 1179656 | tf_op jit(solution)/shard_map/ppermute | solution.py:299
  0.5 0.1 collective-permute-start.1
  0.5 0.5 %collective-permute-start.2 = (bf16[128,1536]{1,0:T(8,128)(2,1)}, bf16[128,1536]{1,0:T(8,128)(2,1)S(1)}, u32[]{:S(2)}, u32[]{:S(2)}) collective-permute-start(bf16[128,1536]{1,0:T(8,128)(2,1)} %q_hbm.1), channel_id=1, source_target_pairs={{0,1},{1,0},{2,3},{3,2},{4,5},{5,4},{6,7},{7,6},{8,9},{9,8},{10,11... | collective-permute-start | bytes 1179656 | tf_op jit(solution)/shard_map/ppermute | solution.py:299
  1.0 1.1 %cut.1 = (bf16[128,768]{1,0:T(8,128)(2,1)S(1)}, bf16[128,768]{1,0:T(8,128)(2,1)S(1)}, bf16[128,768]{1,0:T(8,128)(2,1)S(1)}, bf16[16,128]{1,0:T(8,128)(2,1)S(1)}, f32[24,128]{1,0:T(8,128)S(1)}) custom-call(s32[4,28]{1,0:T(4,128)} %keep_hbm.1, bf16[128,1536]{1,0:T(8,128)(2,1)} %k_hbm.1, bf16[128,1536]{1,0:T(8,128)(2,1)} %v_hbm.1, bf16[128,1536]{1,0:T(8,128)(2,1)} %q_hbm.1), custom_call_target="tpu_custom_call" | custom-call | flops 1000000000 | tf_op jit(solution)/shard_map/cut/pallas_call | solution.py:325
  2.1 0.0 collective-permute-done.k_d
  2.1 0.4 %collective-permute-done.1.v_d = bf16[128,1536]{1,0:T(8,128)(2,1)S(1)} collective-permute-done((bf16[128,1536]{1,0:T(8,128)(2,1)}, bf16[128,1536]{1,0:T(8,128)(2,1)S(1)}, u32[]{:S(2)}, u32[]{:S(2)}) %collective-permute-start.1) | collective-permute-done | bytes 393248 | tf_op jit(solution)/shard_map/ppermute | solution.py:299
  2.6 0.1 pack.1
  2.6 3.0 %collective-permute-start.5 = (bf16[256,768]{1,0:T(8,128)(2,1)S(1)}, bf16[256,768]{1,0:T(8,128)(2,1)S(1)}, u32[]{:S(2)}, u32[]{:S(2)}) collective-permute-start(bf16[256,768]{1,0:T(8,128)(2,1)S(1)} %get-tuple-element.42.first), channel_id=1, source_target_pairs={{0,4},{1,5},{2,6},{3,7},{4,0},{5,1},{6,2},{7,3},{8,12},{9,13},{10,... | collective-permute-start | bytes 1179656 | tf_op jit(solution)/shard_map/ppermute | solution.py:293
  5.6 0.0 collective-permute-start.6
  5.6 0.0 collective-permute-done.2.q_d
  5.7 1.6 %collective-permute-start.7 = (bf16[144,768]{1,0:T(8,128)(2,1)S(1)}, bf16[144,768]{1,0:T(8,128)(2,1)S(1)}, u32[]{:S(2)}, u32[]{:S(2)}) collective-permute-start(bf16[144,768]{1,0:T(8,128)(2,1)S(1)} %get-tuple-element.48.q_i), channel_id=1, source_target_pairs={{0,2},{2,0},{4,6},{6,4},{8,10},{10,8},{12,14},{14,12},{1,3},{3,1},... | collective-permute-start | bytes 663560 | tf_op jit(solution)/shard_map/ppermute | solution.py:296
  7.2 0.2 collective-permute-start.3
  7.5 2.9 %collective-permute-start.4 = (bf16[128,768]{1,0:T(8,128)(2,1)S(1)}, bf16[128,768]{1,0:T(8,128)(2,1)S(1)}, u32[]{:S(2)}, u32[]{:S(2)}) collective-permute-start(bf16[128,768]{1,0:T(8,128)(2,1)S(1)} %get-tuple-element.41.k_own), channel_id=1, source_target_pairs={{0,4},{1,5},{2,6},{3,7},{4,0},{5,1},{6,2},{7,3},{8,12},{9,13},{10,... | collective-permute-start | bytes 589832 | tf_op jit(solution)/shard_map/ppermute | solution.py:293
  10.4 3.2 %collective-permute-done.7.q_x = bf16[144,768]{1,0:T(8,128)(2,1)S(1)} collective-permute-done((bf16[144,768]{1,0:T(8,128)(2,1)S(1)}, bf16[144,768]{1,0:T(8,128)(2,1)S(1)}, u32[]{:S(2)}, u32[]{:S(2)}) %collective-permute-start.7) | collective-permute-done | bytes 221216 | tf_op jit(solution)/shard_map/ppermute | solution.py:296
  13.6 2.2 %collective-permute-start.8 = (bf16[128,768]{1,0:T(8,128)(2,1)S(1)}, bf16[128,768]{1,0:T(8,128)(2,1)S(1)}, u32[]{:S(2)}, u32[]{:S(2)}) collective-permute-start(bf16[128,768]{1,0:T(8,128)(2,1)S(1)} %get-tuple-element.57.v_own), channel_id=1, source_target_pairs={{0,4},{1,5},{2,6},{3,7},{4,0},{5,1},{6,2},{7,3},{8,12},{9,13},{10,... | collective-permute-start | bytes 589832 | tf_op jit(solution)/shard_map/ppermute | solution.py:293
  15.8 0.0 collective-permute-done.5.r_e
  15.8 0.0 collective-permute-start.9
  15.8 0.1 join.1
  15.9 0.0 collective-permute-done.6.r_o
  15.9 0.7 %far.1 = bf16[800,128]{1,0:T(8,128)(2,1)S(1)} custom-call(bf16[256,768]{1,0:T(8,128)(2,1)S(1)} %get-tuple-element.45.keys, bf16[256,768]{1,0:T(8,128)(2,1)S(1)} %get-tuple-element.46.values, bf16[256,768]{1,0:T(8,128)(2,1)S(1)} %collective-permute-done.6.r_o, bf16[144,768]{1,0:T(8,128)(2,1)S(1)} %collective-permute-done.7.q_x), custom_call_target="tpu_custom_call" | custom-call | tf_op jit(solution)/shard_map/far/pallas_call | solution.py:353
  16.6 1.8 %collective-permute-start.10 = (bf16[800,128]{1,0:T(8,128)(2,1)S(1)}, bf16[800,128]{1,0:T(8,128)(2,1)S(1)}, u32[]{:S(2)}, u32[]{:S(2)}) collective-permute-start(bf16[800,128]{1,0:T(8,128)(2,1)S(1)} %far.1), channel_id=1, source_target_pairs={{0,2},{2,0},{4,6},{6,4},{8,10},{10,8},{12,14},{14,12},{1,3},{3,1},... | collective-permute-start | bytes 614408 | tf_op jit(solution)/shard_map/ppermute | solution.py:296
  18.4 1.1 %middle.1 = (f32[768,256]{1,0:T(8,128)S(1)}, f32[2,32,128]{2,1,0:T(8,128)S(1)}) custom-call(f32[24,128]{1,0:T(8,128)S(1)} %get-tuple-element.33.bias, bf16[256,768]{1,0:T(8,128)(2,1)S(1)} %get-tuple-element.45.keys, bf16[256,768]{1,0:T(8,128)(2,1)S(1)} %get-tuple-element.46.values, bf16[256,768]{1,0:T(8,128)(2,1)S(1)} %collective-permute-done.6.r_o, ...), custom_call_target="tpu_custom_call" | custom-call | tf_op jit(solution)/shard_map/middle/pallas_call | solution.py:355
  19.5 0.0 collective-permute-done.3.k_o
  19.5 0.3 %collective-permute-done.4.k_e = bf16[128,768]{1,0:T(8,128)(2,1)S(1)} collective-permute-done((bf16[128,768]{1,0:T(8,128)(2,1)S(1)}, bf16[128,768]{1,0:T(8,128)(2,1)S(1)}, u32[]{:S(2)}, u32[]{:S(2)}) %collective-permute-start.4) | collective-permute-done | bytes 196640 | tf_op jit(solution)/shard_map/ppermute | solution.py:293
  19.8 0.9 %outer_scores.1 = (bf16[6,384,256]{2,1,0:T(8,128)(2,1)S(1)}, f32[2,32,128]{2,1,0:T(8,128)S(1)}) custom-call(f32[24,128]{1,0:T(8,128)S(1)} %get-tuple-element.33.bias, bf16[128,768]{1,0:T(8,128)(2,1)S(1)} %get-tuple-element.41.k_own, bf16[128,768]{1,0:T(8,128)(2,1)S(1)} %collective-permute-done.4.k_e, bf16[128,768]{1,0:T(8,128)(2,1)S(1)} %collective-permute-done.3.k_o, ...), custom_call_target="tpu_custom_call" | custom-call | flops 1000000000 | tf_op jit(solution)/shard_map/outer_scores/pallas_call | solution.py:359
  20.7 2.8 %collective-permute-done.8.v_e = bf16[128,768]{1,0:T(8,128)(2,1)S(1)} collective-permute-done((bf16[128,768]{1,0:T(8,128)(2,1)S(1)}, bf16[128,768]{1,0:T(8,128)(2,1)S(1)}, u32[]{:S(2)}, u32[]{:S(2)}) %collective-permute-start.8) | collective-permute-done | bytes 196640 | tf_op jit(solution)/shard_map/ppermute | solution.py:293
  23.5 0.3 %outer_values.1.acc_o = f32[768,256]{1,0:T(8,128)S(1)} custom-call(bf16[6,384,256]{2,1,0:T(8,128)(2,1)S(1)} %get-tuple-element.52.p, bf16[128,768]{1,0:T(8,128)(2,1)S(1)} %get-tuple-element.57.v_own, bf16[128,768]{1,0:T(8,128)(2,1)S(1)} %collective-permute-done.8.v_e), custom_call_target="tpu_custom_call" | custom-call | flops 1000000000 | tf_op jit(solution)/shard_map/outer_values/pallas_call | solution.py:363
  23.8 0.0 collective-permute-done.9.v
  23.8 0.1 turn.1.v_t
  23.9 0.2 collective-permute-done.10.x
  24.2 0.3 %finish_sibling.1 = bf16[128,768]{1,0:T(8,128)(2,1)S(1)} custom-call(bf16[6,384,256]{2,1,0:T(8,128)(2,1)S(1)} %get-tuple-element.52.p, f32[2,32,128]{2,1,0:T(8,128)S(1)} %get-tuple-element.49.st_i, f32[2,32,128]{2,1,0:T(8,128)S(1)} %get-tuple-element.53.st_o, f32[768,256]{1,0:T(8,128)S(1)} %get-tuple-element.60.acc, f32[768,256]{1,0:T(8,128)S(1)} %outer_values.1.acc_o, ...), custom_call_target="tpu_custom_call" | custom-call | tf_op jit(solution)/shard_map/finish_sibling/pallas_call | solution.py:367
  24.5 0.1 collective-permute-start.11
  24.5 0.3 %finish_own.1.x = bf16[128,768]{1,0:T(8,128)(2,1)S(1)} custom-call(bf16[6,384,256]{2,1,0:T(8,128)(2,1)S(1)} %get-tuple-element.52.p, f32[2,32,128]{2,1,0:T(8,128)S(1)} %get-tuple-element.49.st_i, f32[2,32,128]{2,1,0:T(8,128)S(1)} %get-tuple-element.53.st_o, f32[768,256]{1,0:T(8,128)S(1)} %get-tuple-element.60.acc, f32[768,256]{1,0:T(8,128)S(1)} %outer_values.1.acc_o, ...), custom_call_target="tpu_custom_call" | custom-call | tf_op jit(solution)/shard_map/finish_own/pallas_call | solution.py:371
  24.9 0.7 %put_own.1.refs_0_ = bf16[128,1536]{1,0:T(8,128)(2,1)} custom-call(bf16[128,768]{1,0:T(8,128)(2,1)S(1)} %finish_own.1.x), custom_call_target="tpu_custom_call" | custom-call | tf_op jit(solution)/shard_map/put_own/pallas_call | solution.py:373
  25.6 0.4 %collective-permute-done.11.x = bf16[128,768]{1,0:T(8,128)(2,1)S(1)} collective-permute-done((bf16[128,768]{1,0:T(8,128)(2,1)S(1)}, bf16[128,768]{1,0:T(8,128)(2,1)S(1)}, u32[]{:S(2)}, u32[]{:S(2)}) %collective-permute-start.11) | collective-permute-done | bytes 196640 | tf_op jit(solution)/shard_map/ppermute | solution.py:299
  26.0 0.7 %put_back.1 = bf16[128,1536]{1,0:T(8,128)(2,1)} custom-call(bf16[128,768]{1,0:T(8,128)(2,1)S(1)} %collective-permute-done.11.x, bf16[128,1536]{1,0:T(8,128)(2,1)} %put_own.1.refs_0_), custom_call_target="tpu_custom_call", output_to_operand_aliasing={{}: (1, {})} | custom-call | tf_op jit(solution)/shard_map/put_back/pallas_call | solution.py:374
  (1 shorter events, 0.0 us)
Async XLA Ops:
  0.0 2.1 %collective-permute-start = (bf16[128,1536]{1,0:T(8,128)(2,1)}, bf16[128,1536]{1,0:T(8,128)(2,1)S(1)}, u32[]{:S(2)}, u32[]{:S(2)}) collective-permute-start(bf16[128,1536]{1,0:T(8,128)(2,1)} %k_hbm.1), channel_id=1, source_target_pairs={{0,1},{1,0},{2,3},{3,2},{4,5},{5,4},{6,7},{7,6},{8,9},{9,8},{10,11... | collective-permute-start | bytes 1179656 | tf_op jit(solution)/shard_map/ppermute | solution.py:299
  0.5 2.1 %collective-permute-start.1 = (bf16[128,1536]{1,0:T(8,128)(2,1)}, bf16[128,1536]{1,0:T(8,128)(2,1)S(1)}, u32[]{:S(2)}, u32[]{:S(2)}) collective-permute-start(bf16[128,1536]{1,0:T(8,128)(2,1)} %v_hbm.1), channel_id=1, source_target_pairs={{0,1},{1,0},{2,3},{3,2},{4,5},{5,4},{6,7},{7,6},{8,9},{9,8},{10,11... | collective-permute-start | bytes 1179656 | tf_op jit(solution)/shard_map/ppermute | solution.py:299
  0.5 5.1 %collective-permute-start.2 = (bf16[128,1536]{1,0:T(8,128)(2,1)}, bf16[128,1536]{1,0:T(8,128)(2,1)S(1)}, u32[]{:S(2)}, u32[]{:S(2)}) collective-permute-start(bf16[128,1536]{1,0:T(8,128)(2,1)} %q_hbm.1), channel_id=1, source_target_pairs={{0,1},{1,0},{2,3},{3,2},{4,5},{5,4},{6,7},{7,6},{8,9},{9,8},{10,11... | collective-permute-start | bytes 1179656 | tf_op jit(solution)/shard_map/ppermute | solution.py:299
  2.6 13.2 %collective-permute-start.5 = (bf16[256,768]{1,0:T(8,128)(2,1)S(1)}, bf16[256,768]{1,0:T(8,128)(2,1)S(1)}, u32[]{:S(2)}, u32[]{:S(2)}) collective-permute-start(bf16[256,768]{1,0:T(8,128)(2,1)S(1)} %get-tuple-element.42.first), channel_id=1, source_target_pairs={{0,4},{1,5},{2,6},{3,7},{4,0},{5,1},{6,2},{7,3},{8,12},{9,13},{10,... | collective-permute-start | bytes 1179656 | tf_op jit(solution)/shard_map/ppermute | solution.py:293
  5.6 10.2 %collective-permute-start.6 = (bf16[256,768]{1,0:T(8,128)(2,1)S(1)}, bf16[256,768]{1,0:T(8,128)(2,1)S(1)}, u32[]{:S(2)}, u32[]{:S(2)}) collective-permute-start(bf16[256,768]{1,0:T(8,128)(2,1)S(1)} %get-tuple-element.42.first), channel_id=1, source_target_pairs={{0,1},{1,0},{2,3},{3,2},{4,8},{5,9},{6,10},{7,11},{8,4},{9,5},{10,... | collective-permute-start | bytes 1179656 | tf_op jit(solution)/shard_map/ppermute | solution.py:293
  5.7 7.9 %collective-permute-start.7 = (bf16[144,768]{1,0:T(8,128)(2,1)S(1)}, bf16[144,768]{1,0:T(8,128)(2,1)S(1)}, u32[]{:S(2)}, u32[]{:S(2)}) collective-permute-start(bf16[144,768]{1,0:T(8,128)(2,1)S(1)} %get-tuple-element.48.q_i), channel_id=1, source_target_pairs={{0,2},{2,0},{4,6},{6,4},{8,10},{10,8},{12,14},{14,12},{1,3},{3,1},... | collective-permute-start | bytes 663560 | tf_op jit(solution)/shard_map/ppermute | solution.py:296
  7.2 12.2 %collective-permute-start.3 = (bf16[128,768]{1,0:T(8,128)(2,1)S(1)}, bf16[128,768]{1,0:T(8,128)(2,1)S(1)}, u32[]{:S(2)}, u32[]{:S(2)}) collective-permute-start(bf16[128,768]{1,0:T(8,128)(2,1)S(1)} %get-tuple-element.41.k_own), channel_id=1, source_target_pairs={{0,1},{1,0},{2,3},{3,2},{4,8},{5,9},{6,10},{7,11},{8,4},{9,5},{10,... | collective-permute-start | bytes 589832 | tf_op jit(solution)/shard_map/ppermute | solution.py:293
  7.5 12.3 %collective-permute-start.4 = (bf16[128,768]{1,0:T(8,128)(2,1)S(1)}, bf16[128,768]{1,0:T(8,128)(2,1)S(1)}, u32[]{:S(2)}, u32[]{:S(2)}) collective-permute-start(bf16[128,768]{1,0:T(8,128)(2,1)S(1)} %get-tuple-element.41.k_own), channel_id=1, source_target_pairs={{0,4},{1,5},{2,6},{3,7},{4,0},{5,1},{6,2},{7,3},{8,12},{9,13},{10,... | collective-permute-start | bytes 589832 | tf_op jit(solution)/shard_map/ppermute | solution.py:293
  13.6 9.9 %collective-permute-start.8 = (bf16[128,768]{1,0:T(8,128)(2,1)S(1)}, bf16[128,768]{1,0:T(8,128)(2,1)S(1)}, u32[]{:S(2)}, u32[]{:S(2)}) collective-permute-start(bf16[128,768]{1,0:T(8,128)(2,1)S(1)} %get-tuple-element.57.v_own), channel_id=1, source_target_pairs={{0,4},{1,5},{2,6},{3,7},{4,0},{5,1},{6,2},{7,3},{8,12},{9,13},{10,... | collective-permute-start | bytes 589832 | tf_op jit(solution)/shard_map/ppermute | solution.py:293
  15.8 8.0 %collective-permute-start.9 = (bf16[128,768]{1,0:T(8,128)(2,1)S(1)}, bf16[128,768]{1,0:T(8,128)(2,1)S(1)}, u32[]{:S(2)}, u32[]{:S(2)}) collective-permute-start(bf16[128,768]{1,0:T(8,128)(2,1)S(1)} %get-tuple-element.57.v_own), channel_id=1, source_target_pairs={{0,1},{1,0},{2,3},{3,2},{4,8},{5,9},{6,10},{7,11},{8,4},{9,5},{10,... | collective-permute-start | bytes 589832 | tf_op jit(solution)/shard_map/ppermute | solution.py:293
  16.6 7.5 %collective-permute-start.10 = (bf16[800,128]{1,0:T(8,128)(2,1)S(1)}, bf16[800,128]{1,0:T(8,128)(2,1)S(1)}, u32[]{:S(2)}, u32[]{:S(2)}) collective-permute-start(bf16[800,128]{1,0:T(8,128)(2,1)S(1)} %far.1), channel_id=1, source_target_pairs={{0,2},{2,0},{4,6},{6,4},{8,10},{10,8},{12,14},{14,12},{1,3},{3,1},... | collective-permute-start | bytes 614408 | tf_op jit(solution)/shard_map/ppermute | solution.py:296
  24.5 1.5 %collective-permute-start.11 = (bf16[128,768]{1,0:T(8,128)(2,1)S(1)}, bf16[128,768]{1,0:T(8,128)(2,1)S(1)}, u32[]{:S(2)}, u32[]{:S(2)}) collective-permute-start(bf16[128,768]{1,0:T(8,128)(2,1)S(1)} %finish_sibling.1), channel_id=1, source_target_pairs={{0,1},{1,0},{2,3},{3,2},{4,5},{5,4},{6,7},{7,6},{8,9},{9,8},{10,11... | collective-permute-start | bytes 589832 | tf_op jit(solution)/shard_map/ppermute | solution.py:299

commit v7 on v6

--- a/solution.py
+++ b/solution.py
@@ -244,31 +244,40 @@
         acc[cols, :] = weigh(jnp.concatenate([v_own[:, cols], v_e[:, cols]], axis=0), p[h, : 2 * rows, :])
 
 
-def turn_kernel(v, out):
-    for h in range(v.shape[1] // HD):
-        cols = pl.ds(h * HD, HD)
-        out[cols, :] = v[:, cols].T
-
-
-def finish_kernel(mine, p, st_i, st_o, acc, acc_o, v_t, x, out):
+def base_kernel(p, st_i, st_o, acc, acc_o, v_o, out, st):
     heads = p.shape[0]
+    scales = []
+    for src in range(2):
+        parts = [(ref[src, :heads], ref[src, STAT : STAT + heads]) for ref in (st_i, st_o)]
+        peak = jnp.maximum(parts[0][0], parts[1][0])
+        f0, f1 = jnp.exp2(parts[0][0] - peak), jnp.exp2(parts[1][0] - peak)
+        total = f0 * parts[0][1] + f1 * parts[1][1]
+        st[src, :heads] = peak
+        st[src, STAT : STAT + heads] = total
+        scales.append((f0 / total, f1 / total))
+    for h in range(heads):
+        cols = pl.ds(h * HD, HD)
+        rest = acc_o[cols, :] + weigh(v_o[:, cols], p[h, 2 * v_o.shape[0] :, :])
+        for src, (s0, s1) in enumerate(scales):
+            lanes = slice(src * HD, (src + 1) * HD)
+            out[cols, lanes] = acc[cols, lanes] * s0[h : h + 1] + rest[:, lanes] * s1[h : h + 1]
+
+
+def finish_kernel(mine, o, st, x, out):
+    heads = out.shape[1] // HD
 
     def run(src):
-        parts = [(st[src, :heads], st[src, STAT : STAT + heads]) for st in (st_i, st_o)]
         if src == 0:
-            parts.append(get_stats(x, heads))
-        scale = scale_parts(parts)
-        if src == 0:
-            scale[2] = scale[2] * parts[2][1]
-        lanes = slice(src * HD, (src + 1) * HD)
+            m0, l0 = st[0, :heads], st[0, STAT : STAT + heads]
+            m1, l1 = get_stats(x, heads)
+            scale = scale_parts([(m0, l0), (m1, l1)])
+            w0, w1 = scale[0] * l0, scale[1] * l1
         for h in range(heads):
             cols = pl.ds(h * HD, HD)
-            rest = jnp.dot(v_t[cols, :], p[h, 2 * v_t.shape[1] :, lanes], preferred_element_type=jnp.float32)
-            rest = acc_o[cols, lanes] + rest
-            o = acc[cols, lanes] * scale[0][h : h + 1] + rest * scale[1][h : h + 1]
+            part = o[cols, src * HD : (src + 1) * HD]
             if src == 0:
-                o = o + x[cols, :].astype(jnp.float32) * scale[2][h : h + 1]
-            out[:, cols] = o.T.astype(out.dtype)
+                part = part * w0[h : h + 1] + x[cols, :].astype(jnp.float32) * w1[h : h + 1]
+            out[:, cols] = part.T.astype(out.dtype)
 
     by_role(lambda: run(0 if mine else 1), lambda: run(1 if mine else 0))
 
@@ -348,7 +357,7 @@
     vo_e = exchange(v_even, 0)
     v_odd, r_e = lax.optimization_barrier((v_o, r_e))
     vo_o = exchange(v_odd, 1)
-    keys, values = call(join_kernel, "join", 0.1, [vmem] * 2, [array(bf16, 2 * rows, half)] * 2)(first, r_e)
+    keys, values = call(join_kernel, "join", 0.05, [vmem] * 2, [array(bf16, 2 * rows, half)] * 2)(first, r_e)
     r_o, _ = lax.optimization_barrier((r_o, values))
     x = call(far_kernel, "far", 0, [vmem] * 4, array(bf16, half + stat_rows(heads), rows))(keys, values, r_o, q_x)
     x = across(x)
@@ -356,19 +365,17 @@
         bias, keys, values, r_o, q_i, q_o
     )
     ko_o, ko_e, _ = lax.optimization_barrier((ko_o, ko_e, st_i))
-    p_o, st_o = call(outer_scores_kernel, "outer_scores", 1, [vmem] * 6, [array(bf16, heads, 3 * rows, 2 * rows), stats])(
+    p_o, st_o = call(outer_scores_kernel, "outer_scores", 0.5, [vmem] * 6, [array(bf16, heads, 3 * rows, 2 * rows), stats])(
         bias, k_o, ko_e, ko_o, q_i, q_o
     )
     vo_e, _ = lax.optimization_barrier((vo_e, st_o))
-    acc_o = call(outer_values_kernel, "outer_values", 1, [vmem] * 3, array(f32, half, 2 * rows))(p_o, v_o, vo_e)
+    acc_o = call(outer_values_kernel, "outer_values", 0.3, [vmem] * 3, array(f32, half, 2 * rows))(p_o, v_o, vo_e)
     vo_o, _ = lax.optimization_barrier((vo_o, acc_o))
-    v_t = call(turn_kernel, "turn", 2, [vmem], array(bf16, half, rows))(vo_o)
-    parts = p_o, st_i, st_o, acc, acc_o, v_t, x
-    out_sib = call(functools.partial(finish_kernel, False), "finish_sibling", 0, [vmem] * 7, part)(*parts)
+    o, st = call(base_kernel, "base", 0.3, [vmem] * 6, [array(f32, half, 2 * rows), stats])(p_o, st_i, st_o, acc, acc_o, vo_o)
+    out_sib = call(functools.partial(finish_kernel, False), "finish_sibling", 0, [vmem] * 3, part)(o, st, x)
     back = swap(out_sib)
-    acc, _ = lax.optimization_barrier((acc, out_sib))
-    parts = p_o, st_i, st_o, acc, acc_o, v_t, x
-    out_own = call(functools.partial(finish_kernel, True), "finish_own", 0, [vmem] * 7, part)(*parts)
+    o, _ = lax.optimization_barrier((o, out_sib))
+    out_own = call(functools.partial(finish_kernel, True), "finish_own", 0, [vmem] * 3, part)(o, st, x)
     out = array(query.dtype, rows, width)
     mine = call(functools.partial(put_kernel, True), "put_own", 0, [vmem], out, [dma], hbm)(out_own)
     return call(functools.partial(put_kernel, False), "put_back", 0, [vmem, hbm], out, [dma], hbm, {1: 0})(back, mine)

time: 26.8 us -> 26.7 us (level)
  transfers between devices with their start and end apart: 12 -> 12, of which waited for: 6 -> 5; matrix products, arithmetic and copies ran while one was open for 0% -> 0% of each run, Pallas kernels for 20% -> 21%
where the time goes in v7:
time: 26.7 us; the launch traced here: 26.5 us
  starting transfers between devices  12.8 us (48%)
  waiting for transfers between devices  7.38 us (28%)
  Pallas kernels  6.3 us (24%)
    ppermute x6, starting transfers between devices, exchange(): return lax.ppermute(x, ('blk', 'uly'), plane_pairs(n_blk, n_uly, parity))  8.39 us
    ppermute x2, starting transfers between devices, across(): return lax.ppermute(x, 'blk', chip_pairs(n_blk, n_uly))  3.33 us
    ppermute x2, waiting for transfers between devices, across(): return lax.ppermute(x, 'blk', chip_pairs(n_blk, n_uly))  3.21 us
    ppermute x6, waiting for transfers between devices, exchange(): return lax.ppermute(x, ('blk', 'uly'), plane_pairs(n_blk, n_uly, parity))  3.15 us
    pallas_call x1, Pallas kernels, body(): call(cut_kernel, 'cut', 1, [hbm] * 4, [part, part, part, array(bf16, FLAG...  1.15 us
    pallas_call x1, Pallas kernels, body(): call(middle_kernel, 'middle', 0, [vmem] * 6, [array(f32, half, 2 * rows),...  1.08 us
    ppermute x4, starting transfers between devices, swap(): return lax.ppermute(x, 'uly', cores)  1.03 us
    ppermute x4, waiting for transfers between devices, swap(): return lax.ppermute(x, 'uly', cores)  1.02 us
  transfers between devices with their start and end apart: 12, of which 5 were waited for; matrix products, arithmetic and copies ran while one was open for 0% of the time, Pallas kernels for 21%

profile of v7, /device:TPU:0, one launch (start us, length us, event | category | flops | bytes accessed | tf_op | source)
XLA Modules:
  0.0 26.5 jit_solution(5751582102034868734)
XLA Ops:
  0.0 0.5 %collective-permute-start = (bf16[128,1536]{1,0:T(8,128)(2,1)}, bf16[128,1536]{1,0:T(8,128)(2,1)S(1)}, u32[]{:S(2)}, u32[]{:S(2)}) collective-permute-start(bf16[128,1536]{1,0:T(8,128)(2,1)} %k_hbm.1), channel_id=1, source_target_pairs={{0,1},{1,0},{2,3},{3,2},{4,5},{5,4},{6,7},{7,6},{8,9},{9,8},{10,11... | collective-permute-start | bytes 1179656 | tf_op jit(solution)/shard_map/ppermute | solution.py:308
  0.5 0.1 collective-permute-start.1
  0.5 0.5 %collective-permute-start.2 = (bf16[128,1536]{1,0:T(8,128)(2,1)}, bf16[128,1536]{1,0:T(8,128)(2,1)S(1)}, u32[]{:S(2)}, u32[]{:S(2)}) collective-permute-start(bf16[128,1536]{1,0:T(8,128)(2,1)} %q_hbm.1), channel_id=1, source_target_pairs={{0,1},{1,0},{2,3},{3,2},{4,5},{5,4},{6,7},{7,6},{8,9},{9,8},{10,11... | collective-permute-start | bytes 1179656 | tf_op jit(solution)/shard_map/ppermute | solution.py:308
  1.0 1.1 %cut.1 = (bf16[128,768]{1,0:T(8,128)(2,1)S(1)}, bf16[128,768]{1,0:T(8,128)(2,1)S(1)}, bf16[128,768]{1,0:T(8,128)(2,1)S(1)}, bf16[16,128]{1,0:T(8,128)(2,1)S(1)}, f32[24,128]{1,0:T(8,128)S(1)}) custom-call(s32[4,28]{1,0:T(4,128)} %keep_hbm.1, bf16[128,1536]{1,0:T(8,128)(2,1)} %k_hbm.1, bf16[128,1536]{1,0:T(8,128)(2,1)} %v_hbm.1, bf16[128,1536]{1,0:T(8,128)(2,1)} %q_hbm.1), custom_call_target="tpu_custom_call" | custom-call | flops 1000000000 | tf_op jit(solution)/shard_map/cut/pallas_call | solution.py:334
  2.1 0.0 collective-permute-done.k_d
  2.1 0.4 %collective-permute-done.1.v_d = bf16[128,1536]{1,0:T(8,128)(2,1)S(1)} collective-permute-done((bf16[128,1536]{1,0:T(8,128)(2,1)}, bf16[128,1536]{1,0:T(8,128)(2,1)S(1)}, u32[]{:S(2)}, u32[]{:S(2)}) %collective-permute-start.1) | collective-permute-done | bytes 393248 | tf_op jit(solution)/shard_map/ppermute | solution.py:308
  2.6 0.1 pack.1
  2.6 3.0 %collective-permute-start.5 = (bf16[256,768]{1,0:T(8,128)(2,1)S(1)}, bf16[256,768]{1,0:T(8,128)(2,1)S(1)}, u32[]{:S(2)}, u32[]{:S(2)}) collective-permute-start(bf16[256,768]{1,0:T(8,128)(2,1)S(1)} %get-tuple-element.44.first), channel_id=1, source_target_pairs={{0,4},{1,5},{2,6},{3,7},{4,0},{5,1},{6,2},{7,3},{8,12},{9,13},{10,... | collective-permute-start | bytes 1179656 | tf_op jit(solution)/shard_map/ppermute | solution.py:302
  5.6 0.0 collective-permute-start.6
  5.6 0.0 collective-permute-done.2.q_d
  5.7 1.6 %collective-permute-start.7 = (bf16[144,768]{1,0:T(8,128)(2,1)S(1)}, bf16[144,768]{1,0:T(8,128)(2,1)S(1)}, u32[]{:S(2)}, u32[]{:S(2)}) collective-permute-start(bf16[144,768]{1,0:T(8,128)(2,1)S(1)} %get-tuple-element.50.q_i), channel_id=1, source_target_pairs={{0,2},{2,0},{4,6},{6,4},{8,10},{10,8},{12,14},{14,12},{1,3},{3,1},... | collective-permute-start | bytes 663560 | tf_op jit(solution)/shard_map/ppermute | solution.py:305
  7.2 3.1 %collective-permute-start.4 = (bf16[128,768]{1,0:T(8,128)(2,1)S(1)}, bf16[128,768]{1,0:T(8,128)(2,1)S(1)}, u32[]{:S(2)}, u32[]{:S(2)}) collective-permute-start(bf16[128,768]{1,0:T(8,128)(2,1)S(1)} %get-tuple-element.43.k_own), channel_id=1, source_target_pairs={{0,4},{1,5},{2,6},{3,7},{4,0},{5,1},{6,2},{7,3},{8,12},{9,13},{10,... | collective-permute-start | bytes 589832 | tf_op jit(solution)/shard_map/ppermute | solution.py:302
  10.4 0.0 collective-permute-start.3
  10.4 3.2 %collective-permute-done.7.q_x = bf16[144,768]{1,0:T(8,128)(2,1)S(1)} collective-permute-done((bf16[144,768]{1,0:T(8,128)(2,1)S(1)}, bf16[144,768]{1,0:T(8,128)(2,1)S(1)}, u32[]{:S(2)}, u32[]{:S(2)}) %collective-permute-start.7) | collective-permute-done | bytes 221216 | tf_op jit(solution)/shard_map/ppermute | solution.py:305
  13.6 2.2 %collective-permute-start.8 = (bf16[128,768]{1,0:T(8,128)(2,1)S(1)}, bf16[128,768]{1,0:T(8,128)(2,1)S(1)}, u32[]{:S(2)}, u32[]{:S(2)}) collective-permute-start(bf16[128,768]{1,0:T(8,128)(2,1)S(1)} %get-tuple-element.59.v_own), channel_id=1, source_target_pairs={{0,4},{1,5},{2,6},{3,7},{4,0},{5,1},{6,2},{7,3},{8,12},{9,13},{10,... | collective-permute-start | bytes 589832 | tf_op jit(solution)/shard_map/ppermute | solution.py:302
  15.8 0.0 collective-permute-done.5.r_e
  15.8 0.0 collective-permute-start.9
  15.8 0.1 join.1
  15.9 0.0 collective-permute-done.6.r_o
  15.9 0.7 %far.1 = bf16[800,128]{1,0:T(8,128)(2,1)S(1)} custom-call(bf16[256,768]{1,0:T(8,128)(2,1)S(1)} %get-tuple-element.47.keys, bf16[256,768]{1,0:T(8,128)(2,1)S(1)} %get-tuple-element.48.values, bf16[256,768]{1,0:T(8,128)(2,1)S(1)} %collective-permute-done.6.r_o, bf16[144,768]{1,0:T(8,128)(2,1)S(1)} %collective-permute-done.7.q_x), custom_call_target="tpu_custom_call" | custom-call | tf_op jit(solution)/shard_map/far/pallas_call | solution.py:362
  16.6 1.8 %collective-permute-start.10 = (bf16[800,128]{1,0:T(8,128)(2,1)S(1)}, bf16[800,128]{1,0:T(8,128)(2,1)S(1)}, u32[]{:S(2)}, u32[]{:S(2)}) collective-permute-start(bf16[800,128]{1,0:T(8,128)(2,1)S(1)} %far.1), channel_id=1, source_target_pairs={{0,2},{2,0},{4,6},{6,4},{8,10},{10,8},{12,14},{14,12},{1,3},{3,1},... | collective-permute-start | bytes 614408 | tf_op jit(solution)/shard_map/ppermute | solution.py:305
  18.4 1.1 %middle.1 = (f32[768,256]{1,0:T(8,128)S(1)}, f32[2,32,128]{2,1,0:T(8,128)S(1)}) custom-call(f32[24,128]{1,0:T(8,128)S(1)} %get-tuple-element.35.bias, bf16[256,768]{1,0:T(8,128)(2,1)S(1)} %get-tuple-element.47.keys, bf16[256,768]{1,0:T(8,128)(2,1)S(1)} %get-tuple-element.48.values, bf16[256,768]{1,0:T(8,128)(2,1)S(1)} %collective-permute-done.6.r_o, ...), custom_call_target="tpu_custom_call" | custom-call | tf_op jit(solution)/shard_map/middle/pallas_call | solution.py:364
  19.5 0.3 %collective-permute-done.4.k_e = bf16[128,768]{1,0:T(8,128)(2,1)S(1)} collective-permute-done((bf16[128,768]{1,0:T(8,128)(2,1)S(1)}, bf16[128,768]{1,0:T(8,128)(2,1)S(1)}, u32[]{:S(2)}, u32[]{:S(2)}) %collective-permute-start.4) | collective-permute-done | bytes 196640 | tf_op jit(solution)/shard_map/ppermute | solution.py:302
  19.8 0.0 collective-permute-done.3.k_o
  19.8 0.9 %outer_scores.1 = (bf16[6,384,256]{2,1,0:T(8,128)(2,1)S(1)}, f32[2,32,128]{2,1,0:T(8,128)S(1)}) custom-call(f32[24,128]{1,0:T(8,128)S(1)} %get-tuple-element.35.bias, bf16[128,768]{1,0:T(8,128)(2,1)S(1)} %get-tuple-element.43.k_own, bf16[128,768]{1,0:T(8,128)(2,1)S(1)} %collective-permute-done.4.k_e, bf16[128,768]{1,0:T(8,128)(2,1)S(1)} %collective-permute-done.3.k_o, ...), custom_call_target="tpu_custom_call" | custom-call | flops 500000000 | tf_op jit(solution)/shard_map/outer_scores/pallas_call | solution.py:368
  20.7 2.8 %collective-permute-done.8.v_e = bf16[128,768]{1,0:T(8,128)(2,1)S(1)} collective-permute-done((bf16[128,768]{1,0:T(8,128)(2,1)S(1)}, bf16[128,768]{1,0:T(8,128)(2,1)S(1)}, u32[]{:S(2)}, u32[]{:S(2)}) %collective-permute-start.8) | collective-permute-done | bytes 196640 | tf_op jit(solution)/shard_map/ppermute | solution.py:302
  23.5 0.3 %outer_values.1.acc_o = f32[768,256]{1,0:T(8,128)S(1)} custom-call(bf16[6,384,256]{2,1,0:T(8,128)(2,1)S(1)} %get-tuple-element.54.p, bf16[128,768]{1,0:T(8,128)(2,1)S(1)} %get-tuple-element.59.v_own, bf16[128,768]{1,0:T(8,128)(2,1)S(1)} %collective-permute-done.8.v_e), custom_call_target="tpu_custom_call" | custom-call | flops 300000000 | tf_op jit(solution)/shard_map/outer_values/pallas_call | solution.py:372
  23.8 0.0 collective-permute-done.9.v_o
  23.8 0.3 %base.1 = (f32[768,256]{1,0:T(8,128)S(1)}, f32[2,32,128]{2,1,0:T(8,128)S(1)}) custom-call(bf16[6,384,256]{2,1,0:T(8,128)(2,1)S(1)} %get-tuple-element.54.p, f32[2,32,128]{2,1,0:T(8,128)S(1)} %get-tuple-element.51.st_i, f32[2,32,128]{2,1,0:T(8,128)S(1)} %get-tuple-element.55.st_o, f32[768,256]{1,0:T(8,128)S(1)} %get-tuple-element.56.acc, ...), custom_call_target="tpu_custom_call" | custom-call | flops 300000000 | tf_op jit(solution)/shard_map/base/pallas_call | solution.py:374
  24.1 0.0 collective-permute-done.10.x
  24.2 0.2 finish_sibling.1
  24.3 0.1 collective-permute-start.11
  24.4 0.2 finish_own.1.x
  24.6 0.7 %put_own.1.refs_0_ = bf16[128,1536]{1,0:T(8,128)(2,1)} custom-call(bf16[128,768]{1,0:T(8,128)(2,1)S(1)} %finish_own.1.x), custom_call_target="tpu_custom_call" | custom-call | tf_op jit(solution)/shard_map/put_own/pallas_call | solution.py:380
  25.3 0.6 %collective-permute-done.11.x = bf16[128,768]{1,0:T(8,128)(2,1)S(1)} collective-permute-done((bf16[128,768]{1,0:T(8,128)(2,1)S(1)}, bf16[128,768]{1,0:T(8,128)(2,1)S(1)}, u32[]{:S(2)}, u32[]{:S(2)}) %collective-permute-start.11) | collective-permute-done | bytes 196640 | tf_op jit(solution)/shard_map/ppermute | solution.py:308
  25.9 0.7 %put_back.1 = bf16[128,1536]{1,0:T(8,128)(2,1)} custom-call(bf16[128,768]{1,0:T(8,128)(2,1)S(1)} %collective-permute-done.11.x, bf16[128,1536]{1,0:T(8,128)(2,1)} %put_own.1.refs_0_), custom_call_target="tpu_custom_call", output_to_operand_aliasing={{}: (1, {})} | custom-call | tf_op jit(solution)/shard_map/put_back/pallas_call | solution.py:381
  (1 shorter events, 0.0 us)
Async XLA Ops:
  0.0 2.1 %collective-permute-start = (bf16[128,1536]{1,0:T(8,128)(2,1)}, bf16[128,1536]{1,0:T(8,128)(2,1)S(1)}, u32[]{:S(2)}, u32[]{:S(2)}) collective-permute-start(bf16[128,1536]{1,0:T(8,128)(2,1)} %k_hbm.1), channel_id=1, source_target_pairs={{0,1},{1,0},{2,3},{3,2},{4,5},{5,4},{6,7},{7,6},{8,9},{9,8},{10,11... | collective-permute-start | bytes 1179656 | tf_op jit(solution)/shard_map/ppermute | solution.py:308
  0.5 2.1 %collective-permute-start.1 = (bf16[128,1536]{1,0:T(8,128)(2,1)}, bf16[128,1536]{1,0:T(8,128)(2,1)S(1)}, u32[]{:S(2)}, u32[]{:S(2)}) collective-permute-start(bf16[128,1536]{1,0:T(8,128)(2,1)} %v_hbm.1), channel_id=1, source_target_pairs={{0,1},{1,0},{2,3},{3,2},{4,5},{5,4},{6,7},{7,6},{8,9},{9,8},{10,11... | collective-permute-start | bytes 1179656 | tf_op jit(solution)/shard_map/ppermute | solution.py:308
  0.5 5.1 %collective-permute-start.2 = (bf16[128,1536]{1,0:T(8,128)(2,1)}, bf16[128,1536]{1,0:T(8,128)(2,1)S(1)}, u32[]{:S(2)}, u32[]{:S(2)}) collective-permute-start(bf16[128,1536]{1,0:T(8,128)(2,1)} %q_hbm.1), channel_id=1, source_target_pairs={{0,1},{1,0},{2,3},{3,2},{4,5},{5,4},{6,7},{7,6},{8,9},{9,8},{10,11... | collective-permute-start | bytes 1179656 | tf_op jit(solution)/shard_map/ppermute | solution.py:308
  2.6 13.2 %collective-permute-start.5 = (bf16[256,768]{1,0:T(8,128)(2,1)S(1)}, bf16[256,768]{1,0:T(8,128)(2,1)S(1)}, u32[]{:S(2)}, u32[]{:S(2)}) collective-permute-start(bf16[256,768]{1,0:T(8,128)(2,1)S(1)} %get-tuple-element.44.first), channel_id=1, source_target_pairs={{0,4},{1,5},{2,6},{3,7},{4,0},{5,1},{6,2},{7,3},{8,12},{9,13},{10,... | collective-permute-start | bytes 1179656 | tf_op jit(solution)/shard_map/ppermute | solution.py:302
  5.6 10.2 %collective-permute-start.6 = (bf16[256,768]{1,0:T(8,128)(2,1)S(1)}, bf16[256,768]{1,0:T(8,128)(2,1)S(1)}, u32[]{:S(2)}, u32[]{:S(2)}) collective-permute-start(bf16[256,768]{1,0:T(8,128)(2,1)S(1)} %get-tuple-element.44.first), channel_id=1, source_target_pairs={{0,1},{1,0},{2,3},{3,2},{4,8},{5,9},{6,10},{7,11},{8,4},{9,5},{10,... | collective-permute-start | bytes 1179656 | tf_op jit(solution)/shard_map/ppermute | solution.py:302
  5.7 7.9 %collective-permute-start.7 = (bf16[144,768]{1,0:T(8,128)(2,1)S(1)}, bf16[144,768]{1,0:T(8,128)(2,1)S(1)}, u32[]{:S(2)}, u32[]{:S(2)}) collective-permute-start(bf16[144,768]{1,0:T(8,128)(2,1)S(1)} %get-tuple-element.50.q_i), channel_id=1, source_target_pairs={{0,2},{2,0},{4,6},{6,4},{8,10},{10,8},{12,14},{14,12},{1,3},{3,1},... | collective-permute-start | bytes 663560 | tf_op jit(solution)/shard_map/ppermute | solution.py:305
  7.2 12.5 %collective-permute-start.4 = (bf16[128,768]{1,0:T(8,128)(2,1)S(1)}, bf16[128,768]{1,0:T(8,128)(2,1)S(1)}, u32[]{:S(2)}, u32[]{:S(2)}) collective-permute-start(bf16[128,768]{1,0:T(8,128)(2,1)S(1)} %get-tuple-element.43.k_own), channel_id=1, source_target_pairs={{0,4},{1,5},{2,6},{3,7},{4,0},{5,1},{6,2},{7,3},{8,12},{9,13},{10,... | collective-permute-start | bytes 589832 | tf_op jit(solution)/shard_map/ppermute | solution.py:302
  10.4 9.4 %collective-permute-start.3 = (bf16[128,768]{1,0:T(8,128)(2,1)S(1)}, bf16[128,768]{1,0:T(8,128)(2,1)S(1)}, u32[]{:S(2)}, u32[]{:S(2)}) collective-permute-start(bf16[128,768]{1,0:T(8,128)(2,1)S(1)} %get-tuple-element.43.k_own), channel_id=1, source_target_pairs={{0,1},{1,0},{2,3},{3,2},{4,8},{5,9},{6,10},{7,11},{8,4},{9,5},{10,... | collective-permute-start | bytes 589832 | tf_op jit(solution)/shard_map/ppermute | solution.py:302
  13.6 9.9 %collective-permute-start.8 = (bf16[128,768]{1,0:T(8,128)(2,1)S(1)}, bf16[128,768]{1,0:T(8,128)(2,1)S(1)}, u32[]{:S(2)}, u32[]{:S(2)}) collective-permute-start(bf16[128,768]{1,0:T(8,128)(2,1)S(1)} %get-tuple-element.59.v_own), channel_id=1, source_target_pairs={{0,4},{1,5},{2,6},{3,7},{4,0},{5,1},{6,2},{7,3},{8,12},{9,13},{10,... | collective-permute-start | bytes 589832 | tf_op jit(solution)/shard_map/ppermute | solution.py:302
  15.8 8.0 %collective-permute-start.9 = (bf16[128,768]{1,0:T(8,128)(2,1)S(1)}, bf16[128,768]{1,0:T(8,128)(2,1)S(1)}, u32[]{:S(2)}, u32[]{:S(2)}) collective-permute-start(bf16[128,768]{1,0:T(8,128)(2,1)S(1)} %get-tuple-element.59.v_own), channel_id=1, source_target_pairs={{0,1},{1,0},{2,3},{3,2},{4,8},{5,9},{6,10},{7,11},{8,4},{9,5},{10,... | collective-permute-start | bytes 589832 | tf_op jit(solution)/shard_map/ppermute | solution.py:302
  16.6 7.6 %collective-permute-start.10 = (bf16[800,128]{1,0:T(8,128)(2,1)S(1)}, bf16[800,128]{1,0:T(8,128)(2,1)S(1)}, u32[]{:S(2)}, u32[]{:S(2)}) collective-permute-start(bf16[800,128]{1,0:T(8,128)(2,1)S(1)} %far.1), channel_id=1, source_target_pairs={{0,2},{2,0},{4,6},{6,4},{8,10},{10,8},{12,14},{14,12},{1,3},{3,1},... | collective-permute-start | bytes 614408 | tf_op jit(solution)/shard_map/ppermute | solution.py:305
  24.3 1.5 %collective-permute-start.11 = (bf16[128,768]{1,0:T(8,128)(2,1)S(1)}, bf16[128,768]{1,0:T(8,128)(2,1)S(1)}, u32[]{:S(2)}, u32[]{:S(2)}) collective-permute-start(bf16[128,768]{1,0:T(8,128)(2,1)S(1)} %finish_sibling.1), channel_id=1, source_target_pairs={{0,1},{1,0},{2,3},{3,2},{4,5},{5,4},{6,7},{7,6},{8,9},{9,8},{10,11... | collective-permute-start | bytes 589832 | tf_op jit(solution)/shard_map/ppermute | solution.py:308

commit v8 on v7

--- a/solution.py
+++ b/solution.py
@@ -282,9 +282,15 @@
     by_role(lambda: run(0 if mine else 1), lambda: run(1 if mine else 0))
 
 
-def put_kernel(mine, x, *refs):
-    out, sem = refs[-2:]
-    copy = pltpu.make_async_copy(x, out.at[:, my_columns(x.shape[1], mine)], sem)
+def finish_own_kernel(o, st, x, out, own, sem):
+    finish_kernel(True, o, st, x, own)
+    copy = pltpu.make_async_copy(own, out.at[:, my_columns(own.shape[1])], sem)
+    copy.start()
+    copy.wait()
+
+
+def put_kernel(x, _, out, sem):
+    copy = pltpu.make_async_copy(x, out.at[:, my_columns(x.shape[1], False)], sem)
     copy.start()
     copy.wait()
 
@@ -375,10 +381,10 @@
     out_sib = call(functools.partial(finish_kernel, False), "finish_sibling", 0, [vmem] * 3, part)(o, st, x)
     back = swap(out_sib)
     o, _ = lax.optimization_barrier((o, out_sib))
-    out_own = call(functools.partial(finish_kernel, True), "finish_own", 0, [vmem] * 3, part)(o, st, x)
     out = array(query.dtype, rows, width)
-    mine = call(functools.partial(put_kernel, True), "put_own", 0, [vmem], out, [dma], hbm)(out_own)
-    return call(functools.partial(put_kernel, False), "put_back", 0, [vmem, hbm], out, [dma], hbm, {1: 0})(back, mine)
+    scratch = [pltpu.VMEM((rows, half), bf16), dma]
+    mine = call(finish_own_kernel, "finish_own", 0, [vmem] * 3, out, scratch, hbm)(o, st, x)
+    return call(put_kernel, "put_back", 0, [vmem, hbm], out, [dma], hbm, {1: 0})(back, mine)
 
 
 def solution(mesh):

time: 26.7 us -> 26.7 us (level)
    pallas_call x3 -> x2, Pallas kernels: 1.53 us -> 1.53 us  [the longest x1 0.84 us: body(): call(finish_own_kernel, 'finish_own', 0, [vmem] * 3, out, scratch, hbm)]
  transfers between devices with their start and end apart: 12 -> 12, of which waited for: 5 -> 5; matrix products, arithmetic and copies ran while one was open for 0% -> 0% of each run, Pallas kernels for 21% -> 20%
where the time goes in v8:
time: 26.7 us; the launch traced here: 26.5 us
  starting transfers between devices  12.8 us (48%)
  waiting for transfers between devices  7.39 us (28%)
  Pallas kernels  6.29 us (24%)
    ppermute x6, starting transfers between devices, exchange(): return lax.ppermute(x, ('blk', 'uly'), plane_pairs(n_blk, n_uly, parity))  8.39 us
    ppermute x2, starting transfers between devices, across(): return lax.ppermute(x, 'blk', chip_pairs(n_blk, n_uly))  3.33 us
    ppermute x2, waiting for transfers between devices, across(): return lax.ppermute(x, 'blk', chip_pairs(n_blk, n_uly))  3.21 us
    ppermute x6, waiting for transfers between devices, exchange(): return lax.ppermute(x, ('blk', 'uly'), plane_pairs(n_blk, n_uly, parity))  3.15 us
    pallas_call x1, Pallas kernels, body(): call(cut_kernel, 'cut', 1, [hbm] * 4, [part, part, part, array(bf16, FLAG...  1.15 us
    pallas_call x1, Pallas kernels, body(): call(middle_kernel, 'middle', 0, [vmem] * 6, [array(f32, half, 2 * rows),...  1.08 us
    ppermute x4, starting transfers between devices, swap(): return lax.ppermute(x, 'uly', cores)  1.03 us
    ppermute x4, waiting for transfers between devices, swap(): return lax.ppermute(x, 'uly', cores)  1.03 us
  transfers between devices with their start and end apart: 12, of which 5 were waited for; matrix products, arithmetic and copies ran while one was open for 0% of the time, Pallas kernels for 20%

profile of v8, /device:TPU:0, one launch (start us, length us, event | category | flops | bytes accessed | tf_op | source)
XLA Modules:
  0.0 26.5 jit_solution(2683503339111608850)
XLA Ops:
  0.0 0.5 %collective-permute-start = (bf16[128,1536]{1,0:T(8,128)(2,1)}, bf16[128,1536]{1,0:T(8,128)(2,1)S(1)}, u32[]{:S(2)}, u32[]{:S(2)}) collective-permute-start(bf16[128,1536]{1,0:T(8,128)(2,1)} %k_hbm.1), channel_id=1, source_target_pairs={{0,1},{1,0},{2,3},{3,2},{4,5},{5,4},{6,7},{7,6},{8,9},{9,8},{10,11... | collective-permute-start | bytes 1179656 | tf_op jit(solution)/shard_map/ppermute | solution.py:314
  0.5 0.1 collective-permute-start.1
  0.5 0.5 %collective-permute-start.2 = (bf16[128,1536]{1,0:T(8,128)(2,1)}, bf16[128,1536]{1,0:T(8,128)(2,1)S(1)}, u32[]{:S(2)}, u32[]{:S(2)}) collective-permute-start(bf16[128,1536]{1,0:T(8,128)(2,1)} %q_hbm.1), channel_id=1, source_target_pairs={{0,1},{1,0},{2,3},{3,2},{4,5},{5,4},{6,7},{7,6},{8,9},{9,8},{10,11... | collective-permute-start | bytes 1179656 | tf_op jit(solution)/shard_map/ppermute | solution.py:314
  1.0 1.1 %cut.1 = (bf16[128,768]{1,0:T(8,128)(2,1)S(1)}, bf16[128,768]{1,0:T(8,128)(2,1)S(1)}, bf16[128,768]{1,0:T(8,128)(2,1)S(1)}, bf16[16,128]{1,0:T(8,128)(2,1)S(1)}, f32[24,128]{1,0:T(8,128)S(1)}) custom-call(s32[4,28]{1,0:T(4,128)} %keep_hbm.1, bf16[128,1536]{1,0:T(8,128)(2,1)} %k_hbm.1, bf16[128,1536]{1,0:T(8,128)(2,1)} %v_hbm.1, bf16[128,1536]{1,0:T(8,128)(2,1)} %q_hbm.1), custom_call_target="tpu_custom_call" | custom-call | flops 1000000000 | tf_op jit(solution)/shard_map/cut/pallas_call | solution.py:340
  2.1 0.0 collective-permute-done.k_d
  2.1 0.4 %collective-permute-done.1.v_d = bf16[128,1536]{1,0:T(8,128)(2,1)S(1)} collective-permute-done((bf16[128,1536]{1,0:T(8,128)(2,1)}, bf16[128,1536]{1,0:T(8,128)(2,1)S(1)}, u32[]{:S(2)}, u32[]{:S(2)}) %collective-permute-start.1) | collective-permute-done | bytes 393248 | tf_op jit(solution)/shard_map/ppermute | solution.py:314
  2.6 0.1 pack.1
  2.6 3.0 %collective-permute-start.5 = (bf16[256,768]{1,0:T(8,128)(2,1)S(1)}, bf16[256,768]{1,0:T(8,128)(2,1)S(1)}, u32[]{:S(2)}, u32[]{:S(2)}) collective-permute-start(bf16[256,768]{1,0:T(8,128)(2,1)S(1)} %get-tuple-element.44.first), channel_id=1, source_target_pairs={{0,4},{1,5},{2,6},{3,7},{4,0},{5,1},{6,2},{7,3},{8,12},{9,13},{10,... | collective-permute-start | bytes 1179656 | tf_op jit(solution)/shard_map/ppermute | solution.py:308
  5.6 0.0 collective-permute-start.6
  5.6 0.0 collective-permute-done.2.q_d
  5.7 1.6 %collective-permute-start.7 = (bf16[144,768]{1,0:T(8,128)(2,1)S(1)}, bf16[144,768]{1,0:T(8,128)(2,1)S(1)}, u32[]{:S(2)}, u32[]{:S(2)}) collective-permute-start(bf16[144,768]{1,0:T(8,128)(2,1)S(1)} %get-tuple-element.50.q_i), channel_id=1, source_target_pairs={{0,2},{2,0},{4,6},{6,4},{8,10},{10,8},{12,14},{14,12},{1,3},{3,1},... | collective-permute-start | bytes 663560 | tf_op jit(solution)/shard_map/ppermute | solution.py:311
  7.2 3.1 %collective-permute-start.4 = (bf16[128,768]{1,0:T(8,128)(2,1)S(1)}, bf16[128,768]{1,0:T(8,128)(2,1)S(1)}, u32[]{:S(2)}, u32[]{:S(2)}) collective-permute-start(bf16[128,768]{1,0:T(8,128)(2,1)S(1)} %get-tuple-element.43.k_own), channel_id=1, source_target_pairs={{0,4},{1,5},{2,6},{3,7},{4,0},{5,1},{6,2},{7,3},{8,12},{9,13},{10,... | collective-permute-start | bytes 589832 | tf_op jit(solution)/shard_map/ppermute | solution.py:308
  10.4 0.0 collective-permute-start.3
  10.4 3.2 %collective-permute-done.7.q_x = bf16[144,768]{1,0:T(8,128)(2,1)S(1)} collective-permute-done((bf16[144,768]{1,0:T(8,128)(2,1)S(1)}, bf16[144,768]{1,0:T(8,128)(2,1)S(1)}, u32[]{:S(2)}, u32[]{:S(2)}) %collective-permute-start.7) | collective-permute-done | bytes 221216 | tf_op jit(solution)/shard_map/ppermute | solution.py:311
  13.6 2.2 %collective-permute-start.8 = (bf16[128,768]{1,0:T(8,128)(2,1)S(1)}, bf16[128,768]{1,0:T(8,128)(2,1)S(1)}, u32[]{:S(2)}, u32[]{:S(2)}) collective-permute-start(bf16[128,768]{1,0:T(8,128)(2,1)S(1)} %get-tuple-element.59.v_own), channel_id=1, source_target_pairs={{0,4},{1,5},{2,6},{3,7},{4,0},{5,1},{6,2},{7,3},{8,12},{9,13},{10,... | collective-permute-start | bytes 589832 | tf_op jit(solution)/shard_map/ppermute | solution.py:308
  15.8 0.0 collective-permute-done.5.r_e
  15.8 0.0 collective-permute-start.9
  15.8 0.1 join.1
  15.9 0.0 collective-permute-done.6.r_o
  15.9 0.7 %far.1 = bf16[800,128]{1,0:T(8,128)(2,1)S(1)} custom-call(bf16[256,768]{1,0:T(8,128)(2,1)S(1)} %get-tuple-element.47.keys, bf16[256,768]{1,0:T(8,128)(2,1)S(1)} %get-tuple-element.48.values, bf16[256,768]{1,0:T(8,128)(2,1)S(1)} %collective-permute-done.6.r_o, bf16[144,768]{1,0:T(8,128)(2,1)S(1)} %collective-permute-done.7.q_x), custom_call_target="tpu_custom_call" | custom-call | tf_op jit(solution)/shard_map/far/pallas_call | solution.py:368
  16.6 1.8 %collective-permute-start.10 = (bf16[800,128]{1,0:T(8,128)(2,1)S(1)}, bf16[800,128]{1,0:T(8,128)(2,1)S(1)}, u32[]{:S(2)}, u32[]{:S(2)}) collective-permute-start(bf16[800,128]{1,0:T(8,128)(2,1)S(1)} %far.1), channel_id=1, source_target_pairs={{0,2},{2,0},{4,6},{6,4},{8,10},{10,8},{12,14},{14,12},{1,3},{3,1},... | collective-permute-start | bytes 614408 | tf_op jit(solution)/shard_map/ppermute | solution.py:311
  18.4 1.1 %middle.1 = (f32[768,256]{1,0:T(8,128)S(1)}, f32[2,32,128]{2,1,0:T(8,128)S(1)}) custom-call(f32[24,128]{1,0:T(8,128)S(1)} %get-tuple-element.35.bias, bf16[256,768]{1,0:T(8,128)(2,1)S(1)} %get-tuple-element.47.keys, bf16[256,768]{1,0:T(8,128)(2,1)S(1)} %get-tuple-element.48.values, bf16[256,768]{1,0:T(8,128)(2,1)S(1)} %collective-permute-done.6.r_o, ...), custom_call_target="tpu_custom_call" | custom-call | tf_op jit(solution)/shard_map/middle/pallas_call | solution.py:370
  19.5 0.3 %collective-permute-done.4.k_e = bf16[128,768]{1,0:T(8,128)(2,1)S(1)} collective-permute-done((bf16[128,768]{1,0:T(8,128)(2,1)S(1)}, bf16[128,768]{1,0:T(8,128)(2,1)S(1)}, u32[]{:S(2)}, u32[]{:S(2)}) %collective-permute-start.4) | collective-permute-done | bytes 196640 | tf_op jit(solution)/shard_map/ppermute | solution.py:308
  19.8 0.0 collective-permute-done.3.k_o
  19.8 0.9 %outer_scores.1 = (bf16[6,384,256]{2,1,0:T(8,128)(2,1)S(1)}, f32[2,32,128]{2,1,0:T(8,128)S(1)}) custom-call(f32[24,128]{1,0:T(8,128)S(1)} %get-tuple-element.35.bias, bf16[128,768]{1,0:T(8,128)(2,1)S(1)} %get-tuple-element.43.k_own, bf16[128,768]{1,0:T(8,128)(2,1)S(1)} %collective-permute-done.4.k_e, bf16[128,768]{1,0:T(8,128)(2,1)S(1)} %collective-permute-done.3.k_o, ...), custom_call_target="tpu_custom_call" | custom-call | flops 500000000 | tf_op jit(solution)/shard_map/outer_scores/pallas_call | solution.py:374
  20.7 2.8 %collective-permute-done.8.v_e = bf16[128,768]{1,0:T(8,128)(2,1)S(1)} collective-permute-done((bf16[128,768]{1,0:T(8,128)(2,1)S(1)}, bf16[128,768]{1,0:T(8,128)(2,1)S(1)}, u32[]{:S(2)}, u32[]{:S(2)}) %collective-permute-start.8) | collective-permute-done | bytes 196640 | tf_op jit(solution)/shard_map/ppermute | solution.py:308
  23.5 0.3 %outer_values.1.acc_o = f32[768,256]{1,0:T(8,128)S(1)} custom-call(bf16[6,384,256]{2,1,0:T(8,128)(2,1)S(1)} %get-tuple-element.54.p, bf16[128,768]{1,0:T(8,128)(2,1)S(1)} %get-tuple-element.59.v_own, bf16[128,768]{1,0:T(8,128)(2,1)S(1)} %collective-permute-done.8.v_e), custom_call_target="tpu_custom_call" | custom-call | flops 300000000 | tf_op jit(solution)/shard_map/outer_values/pallas_call | solution.py:378
  23.8 0.0 collective-permute-done.9.v_o
  23.8 0.3 %base.1 = (f32[768,256]{1,0:T(8,128)S(1)}, f32[2,32,128]{2,1,0:T(8,128)S(1)}) custom-call(bf16[6,384,256]{2,1,0:T(8,128)(2,1)S(1)} %get-tuple-element.54.p, f32[2,32,128]{2,1,0:T(8,128)S(1)} %get-tuple-element.51.st_i, f32[2,32,128]{2,1,0:T(8,128)S(1)} %get-tuple-element.55.st_o, f32[768,256]{1,0:T(8,128)S(1)} %get-tuple-element.56.acc, ...), custom_call_target="tpu_custom_call" | custom-call | flops 300000000 | tf_op jit(solution)/shard_map/base/pallas_call | solution.py:380
  24.1 0.0 collective-permute-done.10.x
  24.2 0.2 finish_sibling.1
  24.3 0.1 collective-permute-start.11
  24.4 0.8 %finish_own.1._ = bf16[128,1536]{1,0:T(8,128)(2,1)} custom-call(f32[768,256]{1,0:T(8,128)S(1)} %get-tuple-element.64.o, f32[2,32,128]{2,1,0:T(8,128)S(1)} %get-tuple-element.62.st, bf16[800,128]{1,0:T(8,128)(2,1)S(1)} %collective-permute-done.10.x), custom_call_target="tpu_custom_call" | custom-call | tf_op jit(solution)/shard_map/finish_own/pallas_call | solution.py:386
  25.3 0.6 %collective-permute-done.11.x = bf16[128,768]{1,0:T(8,128)(2,1)S(1)} collective-permute-done((bf16[128,768]{1,0:T(8,128)(2,1)S(1)}, bf16[128,768]{1,0:T(8,128)(2,1)S(1)}, u32[]{:S(2)}, u32[]{:S(2)}) %collective-permute-start.11) | collective-permute-done | bytes 196640 | tf_op jit(solution)/shard_map/ppermute | solution.py:314
  25.9 0.7 %put_back.1 = bf16[128,1536]{1,0:T(8,128)(2,1)} custom-call(bf16[128,768]{1,0:T(8,128)(2,1)S(1)} %collective-permute-done.11.x, bf16[128,1536]{1,0:T(8,128)(2,1)} %finish_own.1._), custom_call_target="tpu_custom_call", output_to_operand_aliasing={{}: (1, {})} | custom-call | tf_op jit(solution)/shard_map/put_back/pallas_call | solution.py:387
  (1 shorter events, 0.0 us)
Async XLA Ops:
  0.0 2.1 %collective-permute-start = (bf16[128,1536]{1,0:T(8,128)(2,1)}, bf16[128,1536]{1,0:T(8,128)(2,1)S(1)}, u32[]{:S(2)}, u32[]{:S(2)}) collective-permute-start(bf16[128,1536]{1,0:T(8,128)(2,1)} %k_hbm.1), channel_id=1, source_target_pairs={{0,1},{1,0},{2,3},{3,2},{4,5},{5,4},{6,7},{7,6},{8,9},{9,8},{10,11... | collective-permute-start | bytes 1179656 | tf_op jit(solution)/shard_map/ppermute | solution.py:314
  0.5 2.1 %collective-permute-start.1 = (bf16[128,1536]{1,0:T(8,128)(2,1)}, bf16[128,1536]{1,0:T(8,128)(2,1)S(1)}, u32[]{:S(2)}, u32[]{:S(2)}) collective-permute-start(bf16[128,1536]{1,0:T(8,128)(2,1)} %v_hbm.1), channel_id=1, source_target_pairs={{0,1},{1,0},{2,3},{3,2},{4,5},{5,4},{6,7},{7,6},{8,9},{9,8},{10,11... | collective-permute-start | bytes 1179656 | tf_op jit(solution)/shard_map/ppermute | solution.py:314
  0.5 5.1 %collective-permute-start.2 = (bf16[128,1536]{1,0:T(8,128)(2,1)}, bf16[128,1536]{1,0:T(8,128)(2,1)S(1)}, u32[]{:S(2)}, u32[]{:S(2)}) collective-permute-start(bf16[128,1536]{1,0:T(8,128)(2,1)} %q_hbm.1), channel_id=1, source_target_pairs={{0,1},{1,0},{2,3},{3,2},{4,5},{5,4},{6,7},{7,6},{8,9},{9,8},{10,11... | collective-permute-start | bytes 1179656 | tf_op jit(solution)/shard_map/ppermute | solution.py:314
  2.6 13.2 %collective-permute-start.5 = (bf16[256,768]{1,0:T(8,128)(2,1)S(1)}, bf16[256,768]{1,0:T(8,128)(2,1)S(1)}, u32[]{:S(2)}, u32[]{:S(2)}) collective-permute-start(bf16[256,768]{1,0:T(8,128)(2,1)S(1)} %get-tuple-element.44.first), channel_id=1, source_target_pairs={{0,4},{1,5},{2,6},{3,7},{4,0},{5,1},{6,2},{7,3},{8,12},{9,13},{10,... | collective-permute-start | bytes 1179656 | tf_op jit(solution)/shard_map/ppermute | solution.py:308
  5.6 10.2 %collective-permute-start.6 = (bf16[256,768]{1,0:T(8,128)(2,1)S(1)}, bf16[256,768]{1,0:T(8,128)(2,1)S(1)}, u32[]{:S(2)}, u32[]{:S(2)}) collective-permute-start(bf16[256,768]{1,0:T(8,128)(2,1)S(1)} %get-tuple-element.44.first), channel_id=1, source_target_pairs={{0,1},{1,0},{2,3},{3,2},{4,8},{5,9},{6,10},{7,11},{8,4},{9,5},{10,... | collective-permute-start | bytes 1179656 | tf_op jit(solution)/shard_map/ppermute | solution.py:308
  5.7 7.9 %collective-permute-start.7 = (bf16[144,768]{1,0:T(8,128)(2,1)S(1)}, bf16[144,768]{1,0:T(8,128)(2,1)S(1)}, u32[]{:S(2)}, u32[]{:S(2)}) collective-permute-start(bf16[144,768]{1,0:T(8,128)(2,1)S(1)} %get-tuple-element.50.q_i), channel_id=1, source_target_pairs={{0,2},{2,0},{4,6},{6,4},{8,10},{10,8},{12,14},{14,12},{1,3},{3,1},... | collective-permute-start | bytes 663560 | tf_op jit(solution)/shard_map/ppermute | solution.py:311
  7.2 12.5 %collective-permute-start.4 = (bf16[128,768]{1,0:T(8,128)(2,1)S(1)}, bf16[128,768]{1,0:T(8,128)(2,1)S(1)}, u32[]{:S(2)}, u32[]{:S(2)}) collective-permute-start(bf16[128,768]{1,0:T(8,128)(2,1)S(1)} %get-tuple-element.43.k_own), channel_id=1, source_target_pairs={{0,4},{1,5},{2,6},{3,7},{4,0},{5,1},{6,2},{7,3},{8,12},{9,13},{10,... | collective-permute-start | bytes 589832 | tf_op jit(solution)/shard_map/ppermute | solution.py:308
  10.4 9.4 %collective-permute-start.3 = (bf16[128,768]{1,0:T(8,128)(2,1)S(1)}, bf16[128,768]{1,0:T(8,128)(2,1)S(1)}, u32[]{:S(2)}, u32[]{:S(2)}) collective-permute-start(bf16[128,768]{1,0:T(8,128)(2,1)S(1)} %get-tuple-element.43.k_own), channel_id=1, source_target_pairs={{0,1},{1,0},{2,3},{3,2},{4,8},{5,9},{6,10},{7,11},{8,4},{9,5},{10,... | collective-permute-start | bytes 589832 | tf_op jit(solution)/shard_map/ppermute | solution.py:308
  13.6 9.9 %collective-permute-start.8 = (bf16[128,768]{1,0:T(8,128)(2,1)S(1)}, bf16[128,768]{1,0:T(8,128)(2,1)S(1)}, u32[]{:S(2)}, u32[]{:S(2)}) collective-permute-start(bf16[128,768]{1,0:T(8,128)(2,1)S(1)} %get-tuple-element.59.v_own), channel_id=1, source_target_pairs={{0,4},{1,5},{2,6},{3,7},{4,0},{5,1},{6,2},{7,3},{8,12},{9,13},{10,... | collective-permute-start | bytes 589832 | tf_op jit(solution)/shard_map/ppermute | solution.py:308
  15.8 8.0 %collective-permute-start.9 = (bf16[128,768]{1,0:T(8,128)(2,1)S(1)}, bf16[128,768]{1,0:T(8,128)(2,1)S(1)}, u32[]{:S(2)}, u32[]{:S(2)}) collective-permute-start(bf16[128,768]{1,0:T(8,128)(2,1)S(1)} %get-tuple-element.59.v_own), channel_id=1, source_target_pairs={{0,1},{1,0},{2,3},{3,2},{4,8},{5,9},{6,10},{7,11},{8,4},{9,5},{10,... | collective-permute-start | bytes 589832 | tf_op jit(solution)/shard_map/ppermute | solution.py:308
  16.6 7.6 %collective-permute-start.10 = (bf16[800,128]{1,0:T(8,128)(2,1)S(1)}, bf16[800,128]{1,0:T(8,128)(2,1)S(1)}, u32[]{:S(2)}, u32[]{:S(2)}) collective-permute-start(bf16[800,128]{1,0:T(8,128)(2,1)S(1)} %far.1), channel_id=1, source_target_pairs={{0,2},{2,0},{4,6},{6,4},{8,10},{10,8},{12,14},{14,12},{1,3},{3,1},... | collective-permute-start | bytes 614408 | tf_op jit(solution)/shard_map/ppermute | solution.py:311
  24.3 1.5 %collective-permute-start.11 = (bf16[128,768]{1,0:T(8,128)(2,1)S(1)}, bf16[128,768]{1,0:T(8,128)(2,1)S(1)}, u32[]{:S(2)}, u32[]{:S(2)}) collective-permute-start(bf16[128,768]{1,0:T(8,128)(2,1)S(1)} %finish_sibling.1), channel_id=1, source_target_pairs={{0,1},{1,0},{2,3},{3,2},{4,5},{5,4},{6,7},{7,6},{8,9},{9,8},{10,11... | collective-permute-start | bytes 589832 | tf_op jit(solution)/shard_map/ppermute | solution.py:314
